TPU v7x, 128 devices: a whole 4x4x4 slice. The times are simulated.
128 devices in a mesh: freq: 8 (over y, core), lat: 16 (over z, x).
Axes of the slice: x: 4, y: 4, z: 4, core: 2. Of those that a mesh axis runs over, the one named last changes fastest.
Arguments:
- spectra: float32 [2, 8, 131072], P(None, None, ('freq', 'lat')), may hold values from -6 to 6
- tile_route: int32 [131072, 1], P(('freq', 'lat')), may hold values from 0 to 255; in each aligned block of 1024 rows (0 to 1023, 1024 to 2047, ...) at most 8 rows name the same one
- bin_in_tile: int32 [131072], P(('freq', 'lat')), may hold values from 0 to 1023
- trace_offset: float32 [2, 131072], P(None, ('freq', 'lat')), may hold values from -0.5 to 0.5
- weights: float32 [131072], P(('freq', 'lat')), may hold values from 0.2 to 5
- frequency: float32 [8], P('freq'), may hold values from 0.5 to 1.5
- slowness: float32 [2, 8], replicated, may hold values from 0.6 to 1.6
- vel_index: int32 [2, 512, 512], P(None, 'lat'), may hold values from 0 to 7
Outputs:
- wavefield: float32 [2, 8, 512, 512], P(None, 'freq', 'lat')
- depth_image: float32 [2, 512, 512], P(None, 'lat', 'freq')
Inputs may be any that keep to these rules, and one draw needn't show every extreme that they name: `tile_route`: tiles of 32 x 32 bins, numbered row by row over the grid; among the rows of one device no tile is named by more than 8 traces. `bin_in_tile`: row * 32 + column of the bin within the tile.
All inputs are finite; a program needn't handle non-finite values.
Results may differ from a plain program's by a relative error of at most 0.0003.
Values sent between devices are 32-bit elements; how exact they have to be, the bound alone decides.
No kernel may reach another device: no remote copies, remote signals or barrier semaphores. Data moves between devices by JAX's collectives and lax.ppermute only.
A program may use at most 64 MiB of HBM per device.

v0:
```python
import math

import jax
import jax.numpy as jnp
from jax import lax
from jax.sharding import PartitionSpec as P

NX = 512
NY = 512
TB = 32
MODES = 8
NSTEPS = 2
NREF = 2
NVEL = 8
TILES = 256
CAP = 8


damping = 1.0
depth_step = 1.0
block_tiles = 8


def from_everyone(shard, axis):
    size = lax.axis_size(axis)
    return lax.all_to_all(
        jnp.broadcast_to(shard[None], (size, *shard.shape)), axis, 0, 0, tiled=True
    )


def over_copies(shard, axis):
    everything = from_everyone(shard, axis)
    return jnp.sum(everything, axis=0)


def in_blocks(shard, dim, size):
    before, after = (shard.shape[:dim], shard.shape[dim + 1 :])
    return jnp.moveaxis(shard.reshape(*before, size, -1, *after), dim, 0)


def summed_on_arrival(shard, axis, dim):
    size = lax.axis_size(axis)
    parts = lax.all_to_all(in_blocks(shard, dim, size), axis, 0, 0, tiled=True)
    return jnp.sum(parts, axis=0)


def items_in_groups(shard, axis, split_dim, concat_dim, work, item_dim, out_dim):
    items = jax.tree.leaves(shard)[0].shape[item_dim]
    count = 2 if items % 2 == 0 else 1
    finished = []
    for k in range(count):
        group = jax.tree.map(
            lambda a: lax.slice_in_dim(
                a, k * (items // count), (k + 1) * (items // count), axis=item_dim
            ),
            shard,
        )
        finished.append(
            work(
                lax.all_to_all(
                    group, axis, split_axis=split_dim, concat_axis=concat_dim, tiled=True
                )
            )
        )
    return jax.tree.map(lambda *parts: jnp.concatenate(parts, axis=out_dim), *finished)


def dft_real(length, direction):
    counter = jnp.arange(length)
    angles = (
        2.0 * math.pi / length * (counter[:, None] * counter[None, :] % length).astype(jnp.float32)
    )
    cosine = jnp.cos(angles)
    sine_part = direction * jnp.sin(angles)
    return jnp.stack([jnp.stack([cosine, sine_part], 1), jnp.stack([-sine_part, cosine], 1)], 0)


def twiddle(full_length, first_len, second_len, direction):
    first_at = jnp.arange(first_len)[:, None]
    second_at = jnp.arange(second_len)[None, :]
    angles = 2.0 * math.pi / full_length * (first_at * second_at % full_length).astype(jnp.float32)
    return (jnp.cos(angles), direction * jnp.sin(angles))


def complex_scale(values, cosine, sine_part, part_axis):
    real_part = jnp.take(values, 0, axis=part_axis)
    imag_part = jnp.take(values, 1, axis=part_axis)
    return jnp.stack(
        [real_part * cosine - imag_part * sine_part, real_part * sine_part + imag_part * cosine],
        part_axis,
    )


def normal_terms(trace_meta, values_in):
    slot_count = trace_meta.shape[-1]
    tile_count = slot_count // CAP
    block_width = block_tiles * CAP
    mode_ids = jnp.arange(MODES).astype(jnp.float32)[:, None, None, None, None]

    def one_block(block_at):
        meta_part = lax.dynamic_slice_in_dim(trace_meta, block_at * block_width, block_width, 4)
        data_part = lax.dynamic_slice_in_dim(values_in, block_at * block_width, block_width, 4)
        meta_part = meta_part.reshape(meta_part.shape[:4] + (block_tiles, CAP))
        data_part = data_part.reshape(data_part.shape[:4] + (block_tiles, CAP))
        weight_part = meta_part[0, :, 0]
        along_x = jnp.cos(math.pi * mode_ids * (meta_part[1, :, 0][None] + 0.5) / TB)
        along_y = jnp.cos(math.pi * mode_ids * (meta_part[2, :, 0][None] + 0.5) / TB)
        basis_vals = (along_x[:, None] * along_y[None, :]).reshape(
            (MODES * MODES,) + weight_part.shape
        )
        weighted = basis_vals * weight_part[None]
        normal = jnp.einsum(
            "iabgc,jabgc->gij", weighted, basis_vals, precision=lax.Precision.HIGHEST
        )
        right_side = jnp.einsum(
            "iabgc,paqbgc->gipq", weighted, data_part, precision=lax.Precision.HIGHEST
        )
        return (normal, right_side)

    normal, right_side = lax.map(one_block, jnp.arange(tile_count // block_tiles))
    normal = normal.reshape(tile_count, MODES * MODES, MODES * MODES)
    right_side = right_side.reshape((tile_count, MODES * MODES) + right_side.shape[3:])
    return (normal, right_side)


def fit_grid(normal, right_side, row_count):
    tile_count = normal.shape[0]
    system = normal + damping * jnp.eye(MODES * MODES, dtype=jnp.float32)
    factor = jnp.linalg.cholesky(system)
    flat_rhs = right_side.reshape(tile_count, MODES * MODES, -1)
    middle = jax.scipy.linalg.solve_triangular(factor, flat_rhs, lower=True)
    coeffs = jax.scipy.linalg.solve_triangular(factor, middle, lower=True, trans="T")
    coeffs = coeffs.reshape(row_count // TB, NY // TB, MODES, MODES, 2, -1)
    cell_pos = jnp.arange(TB).astype(jnp.float32)
    cos_table = jnp.cos(
        math.pi * jnp.arange(MODES).astype(jnp.float32)[:, None] * (cell_pos[None, :] + 0.5) / TB
    )
    viewed = jnp.einsum(
        "xyabpq,ai,bj->pqxiyj", coeffs, cos_table, cos_table, precision=lax.Precision.HIGHEST
    )
    return viewed.reshape(2, viewed.shape[1], row_count, NY)


def local(spectra, tile_route, bin_in_tile, trace_offset, weights, frequency, slowness, vel_index):
    lat_count = lax.axis_size("lat")
    row_count = vel_index.shape[1]
    tile_dev = TILES // lat_count
    slot_count = tile_dev * CAP
    total_freqs = spectra.shape[1]
    tile_id = tile_route[:, 0]
    trace_count = tile_id.shape[0]
    ranking = jnp.argsort(tile_id, stable=True)
    sorted_tiles = tile_id[ranking]
    firsts = jnp.searchsorted(sorted_tiles, sorted_tiles, side="left")
    position = sorted_tiles * CAP + jnp.arange(trace_count, dtype=jnp.int32) - firsts
    slot_of = jnp.zeros((trace_count,), jnp.int32).at[ranking].set(position)
    owner_lat = slot_of // slot_count
    within = slot_of % slot_count
    cell_x = (bin_in_tile // TB).astype(jnp.float32) + trace_offset[0]
    cell_y = (bin_in_tile % TB).astype(jnp.float32) + trace_offset[1]
    trace_meta = jnp.stack([weights, cell_x, cell_y], 0)
    meta_buf = (
        jnp.zeros((3, lat_count, slot_count), jnp.float32).at[:, owner_lat, within].set(trace_meta)
    )
    spec_buf = (
        jnp.zeros((2, total_freqs, lat_count, slot_count), jnp.float32)
        .at[:, :, owner_lat, within]
        .set(spectra)
    )
    got_spec, got_meta = (
        lax.all_to_all(spec_buf, "lat", split_axis=2, concat_axis=2, tiled=True),
        lax.all_to_all(meta_buf[:, None], "lat", split_axis=2, concat_axis=2, tiled=True),
    )
    normal, right_side = normal_terms(got_meta[:, None], got_spec[:, None])
    normal = over_copies(normal, "freq")
    right_side = summed_on_arrival(right_side, "freq", 3)
    wave_field = fit_grid(normal, right_side, row_count)
    len_x = NX // 8
    len_y = NY // 8
    w8_fwd = dft_real(8, -1.0)
    w8_inv = dft_real(8, 1.0)
    wx_fwd = dft_real(len_x, -1.0)
    wx_inv = dft_real(len_x, 1.0)
    wy_fwd = dft_real(len_y, -1.0)
    wy_inv = dft_real(len_y, 1.0)
    twx_fwd = twiddle(NX, 8, len_x, -1.0)
    twx_inv = twiddle(NX, 8, len_x, 1.0)
    twy_fwd = twiddle(NY, 8, len_y, -1.0)
    twy_inv = twiddle(NY, 8, len_y, 1.0)
    inverse_scale = 1.0 / (NX * NY)

    def forward_x(columns):
        dims_of = columns.shape
        viewed = columns.reshape(dims_of[:4] + (8, len_x))
        section_a = jnp.einsum(
            "phkqmn,pmsl->shkqln", viewed, w8_fwd, precision=lax.Precision.HIGHEST
        )
        section_b = complex_scale(section_a, twx_fwd[0], twx_fwd[1], 0)
        return jnp.einsum("shkqln,snto->thkqlo", section_b, wx_fwd, precision=lax.Precision.HIGHEST)

    def inverse_y(columns):
        section_c = jnp.einsum(
            "jthkqr,thsn->jsqrkn", columns, wy_inv, precision=lax.Precision.HIGHEST
        )
        section_b = complex_scale(section_c, twy_inv[0], twy_inv[1], 1)
        section_a = jnp.einsum(
            "jsqrkn,skpm->jpqrmn", section_b, w8_inv, precision=lax.Precision.HIGHEST
        )
        return section_a.reshape(section_a.shape[:4] + (NY,)) * inverse_scale

    lat_at = lax.axis_index("lat")
    ky_band = len_y // lat_count
    ky_index = jnp.arange(8)[None, :] + 8 * (lat_at * ky_band + jnp.arange(ky_band)[:, None])
    ky_signed = jnp.where(ky_index >= NY // 2, ky_index - NY, ky_index)
    ky_vals = 2.0 * math.pi / NY * ky_signed.astype(jnp.float32)
    kx_index = jnp.arange(8)[:, None] + 8 * jnp.arange(len_x)[None, :]
    kx_signed = jnp.where(kx_index >= NX // 2, kx_index - NX, kx_index)
    kx_vals = 2.0 * math.pi / NX * kx_signed.astype(jnp.float32)
    ky_sq = (ky_vals * ky_vals)[None, :, :, None, None, None]
    kx_sq = (kx_vals * kx_vals)[None, None, None, None, :, :]
    per_group = NVEL // NREF
    image_rows = []
    for depth_at in range(NSTEPS):
        table_row = slowness[depth_at]
        references = table_row.reshape(NREF, per_group).mean(axis=1)
        forward_dims_of = wave_field.shape
        forward_viewed = wave_field.reshape(forward_dims_of[:3] + (8, len_y))
        forward_section_a = jnp.einsum(
            "pqrmn,pmsk->sqrkn", forward_viewed, w8_fwd, precision=lax.Precision.HIGHEST
        )
        forward_section_b = complex_scale(forward_section_a, twy_fwd[0], twy_fwd[1], 0)
        spectrum_y = jnp.einsum(
            "sqrkn,snth->thkqr", forward_section_b, wy_fwd, precision=lax.Precision.HIGHEST
        )
        spectrum = forward_x(
            lax.all_to_all(spectrum_y, "lat", split_axis=1, concat_axis=4, tiled=True)
        )
        wave_num = frequency[None, :] * references[:, None]
        vertical = (wave_num * wave_num)[:, None, None, :, None, None] - kx_sq - ky_sq
        phase_angle = jnp.sqrt(jnp.maximum(vertical, 0.0)) * depth_step
        damped = jnp.exp(-jnp.sqrt(jnp.maximum(-vertical, 0.0)) * depth_step)
        shifted = complex_scale(
            spectrum[None], damped * jnp.cos(phase_angle), damped * jnp.sin(phase_angle), 1
        )
        inverse_section_c = jnp.einsum(
            "jthkqlo,tosn->jshkqln", shifted, wx_inv, precision=lax.Precision.HIGHEST
        )
        inverse_section_b = complex_scale(inverse_section_c, twx_inv[0], twx_inv[1], 1)
        inverse_section_a = jnp.einsum(
            "jshkqln,slpm->jphkqmn", inverse_section_b, w8_inv, precision=lax.Precision.HIGHEST
        )
        columns = inverse_section_a.reshape(inverse_section_a.shape[:5] + (NX,))
        returned = items_in_groups(columns, "lat", 5, 2, inverse_y, 0, 0)
        velocity = vel_index[depth_at]
        picked = velocity[None] == jnp.arange(NVEL)[:, None, None]
        local_slow = jnp.sum(jnp.where(picked, table_row[:, None, None], 0.0), 0)
        group_of = velocity // per_group
        split_phase = (
            frequency[None, :, None, None]
            * (local_slow[None, None] - references[:, None, None, None])
            * depth_step
        )
        group_mask = (group_of[None] == jnp.arange(NREF)[:, None, None]).astype(jnp.float32)
        corrected = complex_scale(returned, jnp.cos(split_phase), jnp.sin(split_phase), 1)
        wave_field = jnp.sum(corrected * group_mask[:, None, None], 0)
        summed = jnp.sum(wave_field[0], 0)
        image_rows.append(summed)
    depth_image = summed_on_arrival(jnp.stack(image_rows, 0), "freq", 2)
    return (wave_field, depth_image)


def solution(mesh):
    return jax.shard_map(
        local,
        mesh=mesh,
        in_specs=(
            P(None, None, ("freq", "lat")),
            P(("freq", "lat"), None),
            P(("freq", "lat")),
            P(None, ("freq", "lat")),
            P(("freq", "lat")),
            P("freq"),
            P(),
            P(None, "lat", None),
        ),
        out_specs=(P(None, "freq", "lat", None), P(None, "lat", "freq")),
        check_vma=False,
    )
```

profile of v0, /device:TPU:1, one launch (start us, length us, event | category | flops | bytes accessed | tf_op | source)
XLA Modules:
  0.0 513.3 jit_solution(12219274077863745258)
XLA Ops:
  0.7 5.1 sort.17
  5.8 4.5 gather_fusion.1
  10.4 50.7 %while.52 = (s32[]{:T(128)}, u32[1024]{0:T(1024)S(1)}, u32[1024]{0:T(1024)S(1)}, s32[1024]{0:T(1024)S(1)}, s32[]{:T(128)}, /*index=5*/s32[]{:T(128)}, s32[]{}) while((s32[]{:T(128)}, u32[1024]{0:T(1024)S(1)}, u32[1024]{0:T(1024)S(1)}, s32[1024]{0:T(1024)S(1)}, s32[]{:T(128)}, /*index=5*/s32[]{:T(128)}, s32[]{}) %tuple.197), condition=%wide.region_2.3_spmd.clone, body=%wide.region_1.2_spmd.clone.sunk | while | flops 19460 | bytes 67685 | solution.py:154
  10.4 4.5 gather_fusion
  15.0 4.5 gather_fusion
  19.6 4.5 gather_fusion
  24.2 4.5 gather_fusion
  28.8 4.5 gather_fusion
  33.5 4.5 gather_fusion
  38.1 4.5 gather_fusion
  42.7 4.5 gather_fusion
  47.3 4.5 gather_fusion
  51.9 4.5 gather_fusion
  70.3 8.4 %all-to-all-start = ((f32[3,1,16,128]{3,1,0,2:T(1,128)}), f32[3,1,16,128]{3,1,0,2:T(1,128)S(1)}, u32[]{:S(2)}, u32[]{:S(2)}) async-start(f32[3,1,16,128]{3,1,0,2:T(1,128)} %copy.311), calls=%async_computation | async-start | bytes 49152 | tf_op jit(solution)/shard_map/all_to_all | solution.py:172
  80.2 26.6 %scatter_fusion = f32[2,8,2048]{1,0,2:T(2,128)S(1)} fusion(f32[2,8,2048]{1,0,2:T(2,128)S(1)} %broadcast.1428, s32[1024]{0:T(1024)S(1)} %broadcast_select_fusion, f32[1024,2,8]{2,1,0:T(2,128)S(1)} %copy.313), kind=kCustom, calls=%fused_computation.4 | custom fusion | bytes 200704
  108.6 7.1 %all-to-all-start.1 = ((f32[2,8,16,128]{3,1,0,2:T(8,128)}), f32[2,8,16,128]{3,1,0,2:T(8,128)S(1)}, u32[]{:S(2)}, u32[]{:S(2)}) async-start(f32[2,8,16,128]{3,1,0,2:T(8,128)} %copy.314), calls=%async_computation.1 | async-start | bytes 262144 | tf_op jit(solution)/shard_map/all_to_all | solution.py:171
  115.8 6.8 %all-to-all-done.1 = f32[2,8,16,128]{3,1,0,2:T(8,128)S(1)} async-done(((f32[2,8,16,128]{3,1,0,2:T(8,128)}), f32[2,8,16,128]{3,1,0,2:T(8,128)S(1)}, u32[]{:S(2)}, u32[]{:S(2)}) %all-to-all-start.1) | async-done | bytes 131104 | tf_op jit(solution)/shard_map/all_to_all | solution.py:171
  122.6 30.5 %while.51 = (s32[]{:T(128)}, f32[2,8,64,64]{3,2,1,0:T(8,128)S(1)}, f32[2,8,64,2,8]{2,3,1,0,4:T(2,128)}, s32[2]{0:T(128)S(1)}, f32[3,1,1,16,128]{4,3,0,2,1:T(8,12...) while((s32[]{:T(128)}, f32[2,8,64,64]{3,2,1,0:T(8,128)S(1)}, ...), condition=%wide.region_7.8_spmd.clone.clone, body=%wide.region_6.7_spmd.clone.clone.sunk | while | flops 63080472 | bytes 7778675 | solution.py:120
  128.0 5.1 fusion.236
  133.2 4.6 fusion.235
  143.3 5.1 fusion.236
  148.5 4.6 fusion.235
  154.8 7.1 %all-to-all-start.3 = ((f32[8,1,2048]{2,1,0:T(1,128)}), f32[8,1,2048]{2,1,0:T(1,128)S(1)}, u32[]{:S(2)}, u32[]{:S(2)}) async-start(f32[8,1,2048]{2,1,0:T(1,128)} %reshape.1623), calls=%async_computation.3 | async-start | bytes 131072 | tf_op jit(solution)/shard_map/all_to_all | solution.py:43
  164.4 7.2 %reshape.1625 = f32[8,1,65536]{2,1,0:T(1,128)} reshape(f32[8,16,64,64]{3,2,1,0:T(8,128)} %broadcast_in_dim.113) | data formatting | bytes 4194304
  171.6 5.2 %all-to-all-start.2 = ((f32[8,1,65536]{2,1,0:T(1,128)}), f32[8,1,65536]{2,1,0:T(1,128)}, u32[]{:S(2)}, u32[]{:S(2)}) async-start(f32[8,1,65536]{2,1,0:T(1,128)} %reshape.1625), calls=%async_computation.2 | async-start | bytes 4194304 | tf_op jit(solution)/shard_map/all_to_all | solution.py:26
  181.4 21.7 %all-to-all-done.2 = f32[8,1,65536]{2,1,0:T(1,128)} async-done(((f32[8,1,65536]{2,1,0:T(1,128)}), f32[8,1,65536]{2,1,0:T(1,128)}, u32[]{:S(2)}, u32[]{:S(2)}) %all-to-all-start.2) | async-done | bytes 2097184 | tf_op jit(solution)/shard_map/all_to_all | solution.py:26
  203.1 7.2 %reduce.24 = f32[8,65536]{1,0:T(8,128)S(1)} reduce(f32[8,1,65536]{2,1,0:T(1,128)} %all-to-all-done.2, f32[]{:T(128)} %broadcast.1759), dimensions={1}, to_apply=%all_to_all.83.reduce_sub_computation | reduce | bytes 4194308 | tf_op jit(solution)/shard_map/all_to_all | solution.py:26
  217.0 93.8 %custom-call.11 = f32[16,64,64]{2,1,0:T(8,128)S(1)} custom-call(f32[16,64,64]{2,1,0:T(8,128)S(1)} %fusion.42), custom_call_target="Cholesky" | custom-call | tf_op jit(solution)/shard_map/jit(cholesky)/cholesky | solution.py:129
  311.1 78.8 %custom-call.12 = f32[16,1,64,64]{2,3,1,0:T(8,128)S(1)} custom-call(f32[16,1,64,64]{3,2,1,0:T(8,128)S(1)} %select_bitcast_fusion), custom_call_target="InvertDiagBlocksLowerTriangular" | custom-call | tf_op jit(solution)/shard_map/jit(_solve_triangular)/vmap()/triangular_solve | solution.py:132
  399.4 6.6 %all-to-all-done.4 = f32[16,1,2048]{2,1,0:T(1,128)S(1)} async-done(((f32[16,1,2048]{2,1,0:T(1,128)}), f32[16,1,2048]{2,1,0:T(1,128)S(1)}, u32[]{:S(2)}, u32[]{:S(2)}) %all-to-all-start.4) | async-done | bytes 131104 | tf_op jit(solution)/shard_map/all_to_all | solution.py:236
  447.0 12.0 %all_to_all.115 = f32[16,1,2048]{2,1,0:T(1,128)S(1)} all-to-all(f32[16,1,2048]{2,1,0:T(1,128)S(1)} %reshape.1633), channel_id=1, replica_groups=mesh['freq'=8,'lat'=16] {'lat'}, dimensions={0} | all-to-all | bytes 262144 | tf_op jit(solution)/shard_map/all_to_all | solution.py:236
  496.9 14.5 %all_to_all.116 = f32[8,1,4096]{2,1,0:T(1,128)S(1)} all-to-all(f32[8,1,4096]{2,1,0:T(1,128)S(1)} %reshape.1639), channel_id=1, replica_groups=mesh['freq'=8,'lat'=16] {'freq'}, dimensions={0} | all-to-all | bytes 262144 | tf_op jit(solution)/shard_map/all_to_all | solution.py:43
  (327 shorter events, 131.3 us)
Async XLA Ops:
  0.6 5.1 %copy-start = (s32[1024,1]{0,1:T(1,128)S(1)}, s32[1024,1]{0,1:T(1,128)}, u32[]{:S(2)}) copy-start(s32[1024,1]{0,1:T(1,128)} %param.37) | copy-start | bytes 12292
  10.3 55.2 %copy-start.31 = (s32[2]{0:T(128)S(1)}, s32[2]{0:T(128)}, u32[]{:S(2)}) copy-start(s32[2]{0:T(128)} %constant.471) | copy-start | bytes 28
  10.3 55.3 %copy-start.30 = (s32[2]{0:T(128)S(1)}, s32[2]{0:T(128)}, u32[]{:S(2)}) copy-start(s32[2]{0:T(128)} %constant.474) | copy-start | bytes 28
  10.3 55.4 %copy-start.24 = (f32[2,1024]{1,0:T(2,128)S(1)}, f32[2,1024]{1,0:T(2,128)}, u32[]{:S(2)}) copy-start(f32[2,1024]{1,0:T(2,128)} %param.39) | copy-start | bytes 24580
  10.3 55.4 %copy-start.25 = (s32[1024]{0:T(1024)S(1)}, s32[1024]{0:T(1024)}, u32[]{:S(2)}) copy-start(s32[1024]{0:T(1024)} %param.38) | copy-start | bytes 12292
  10.4 55.4 %copy-start.26 = (f32[1024]{0:T(1024)S(1)}, f32[1024]{0:T(1024)}, u32[]{:S(2)}) copy-start(f32[1024]{0:T(1024)} %param.40) | copy-start | bytes 12292
  61.1 17.9 %copy-start.29 = (f32[2,8]{1,0:T(2,128)S(1)}, f32[2,8]{1,0:T(2,128)}, u32[]{:S(2)}) copy-start(f32[2,8]{1,0:T(2,128)} %param.42) | copy-start | bytes 196
  61.1 17.9 %copy-start.20 = (f32[2,8,1024]{2,1,0:T(8,128)S(1)}, f32[2,8,1024]{2,1,0:T(8,128)}, u32[]{:S(2)}) copy-start(f32[2,8,1024]{2,1,0:T(8,128)} %param.36) | copy-start | bytes 196612
  70.3 38.3 %all-to-all-start = ((f32[3,1,16,128]{3,1,0,2:T(1,128)}), f32[3,1,16,128]{3,1,0,2:T(1,128)S(1)}, u32[]{:S(2)}, u32[]{:S(2)}) async-start(f32[3,1,16,128]{3,1,0,2:T(1,128)} %copy.311), calls=%async_computation | async-start | bytes 49152 | tf_op jit(solution)/shard_map/all_to_all | solution.py:172
  79.0 329.0 %copy-start.15 = (f32[8,64]{1,0:T(8,128)}, f32[8,64]{1,0:T(8,128)S(1)}, u32[]{:S(2)}) copy-start(f32[8,64]{1,0:T(8,128)S(1)} %get-tuple-element.439) | copy-start | bytes 6148
  79.0 331.4 %copy-start.2 = (f32[8,64]{1,0:T(8,128)}, f32[8,64]{1,0:T(8,128)S(1)}, u32[]{:S(2)}) copy-start(f32[8,64]{1,0:T(8,128)S(1)} %get-tuple-element.440) | copy-start | bytes 6148
  108.6 14.0 %all-to-all-start.1 = ((f32[2,8,16,128]{3,1,0,2:T(8,128)}), f32[2,8,16,128]{3,1,0,2:T(8,128)S(1)}, u32[]{:S(2)}, u32[]{:S(2)}) async-start(f32[2,8,16,128]{3,1,0,2:T(8,128)} %copy.314), calls=%async_computation.1 | async-start | bytes 262144 | tf_op jit(solution)/shard_map/all_to_all | solution.py:171
  128.0 5.1 %copy-start.13 = (f32[2,8,64,2,8]{2,3,1,0,4:T(2,128)S(1)}, f32[2,8,64,2,8]{2,3,1,0,4:T(2,128)}, u32[]{:S(2)}) copy-start(f32[2,8,64,2,8]{2,3,1,0,4:T(2,128)} %get-tuple-element.560) | copy-start | bytes 196612 | tf_op jit(solution)/shard_map/while
  128.0 5.2 %copy-start.1 = (f32[64,16,8,8]{1,3,2,0:T(8,128)S(1)}, f32[64,16,8,8]{1,3,2,0:T(8,128)}, u32[]{:S(2)}) copy-start(f32[64,16,8,8]{1,3,2,0:T(8,128)} %broadcast_multiply_fusion.10) | copy-start | bytes 786436 | tf_op jit(solution)/shard_map/while
  133.2 4.6 copy-start.14
  143.3 5.1 %copy-start.13 = (f32[2,8,64,2,8]{2,3,1,0,4:T(2,128)S(1)}, f32[2,8,64,2,8]{2,3,1,0,4:T(2,128)}, u32[]{:S(2)}) copy-start(f32[2,8,64,2,8]{2,3,1,0,4:T(2,128)} %get-tuple-element.560) | copy-start | bytes 196612 | tf_op jit(solution)/shard_map/while
  143.3 5.2 %copy-start.1 = (f32[64,16,8,8]{1,3,2,0:T(8,128)S(1)}, f32[64,16,8,8]{1,3,2,0:T(8,128)}, u32[]{:S(2)}) copy-start(f32[64,16,8,8]{1,3,2,0:T(8,128)} %broadcast_multiply_fusion.10) | copy-start | bytes 786436 | tf_op jit(solution)/shard_map/while
  148.5 4.6 copy-start.14
  154.8 16.8 %all-to-all-start.3 = ((f32[8,1,2048]{2,1,0:T(1,128)}), f32[8,1,2048]{2,1,0:T(1,128)S(1)}, u32[]{:S(2)}, u32[]{:S(2)}) async-start(f32[8,1,2048]{2,1,0:T(1,128)} %reshape.1623), calls=%async_computation.3 | async-start | bytes 131072 | tf_op jit(solution)/shard_map/all_to_all | solution.py:43
  171.6 8.2 %copy-start.12 = (s32[2,32,512]{2,1,0:T(8,128)S(1)}, s32[2,32,512]{2,1,0:T(8,128)}, u32[]{:S(2)}) copy-start(s32[2,32,512]{2,1,0:T(8,128)} %param.43) | copy-start | bytes 393220
  171.6 31.5 %all-to-all-start.2 = ((f32[8,1,65536]{2,1,0:T(1,128)}), f32[8,1,65536]{2,1,0:T(1,128)}, u32[]{:S(2)}, u32[]{:S(2)}) async-start(f32[8,1,65536]{2,1,0:T(1,128)} %reshape.1625), calls=%async_computation.2 | async-start | bytes 4194304 | tf_op jit(solution)/shard_map/all_to_all | solution.py:26
  176.8 230.7 %copy-start.8 = (f32[1,8,2,8]{1,3,0,2:T(8,128)}, f32[1,8,2,8]{1,3,0,2:T(8,128)S(1)}, u32[]{:S(2)}) copy-start(f32[1,8,2,8]{1,3,0,2:T(8,128)S(1)} %copy.308) | copy-start | bytes 1540
  176.9 230.7 %copy-start.10 = (f32[1,8,2,8]{1,3,0,2:T(8,128)}, f32[1,8,2,8]{1,3,0,2:T(8,128)S(1)}, u32[]{:S(2)}) copy-start(f32[1,8,2,8]{1,3,0,2:T(8,128)S(1)} %copy.309) | copy-start | bytes 1540
  178.5 230.0 %copy-start.22 = (f32[4,8]{1,0:T(4,128)}, f32[4,8]{1,0:T(4,128)S(1)}, u32[]{:S(2)}) copy-start(f32[4,8]{1,0:T(4,128)S(1)} %fusion.180) | copy-start | bytes 388
  395.6 10.3 %all-to-all-start.4 = ((f32[16,1,2048]{2,1,0:T(1,128)}), f32[16,1,2048]{2,1,0:T(1,128)S(1)}, u32[]{:S(2)}, u32[]{:S(2)}) async-start(f32[16,1,2048]{2,1,0:T(1,128)} %reshape.1627), calls=%async_computation.4 | async-start | bytes 262144 | tf_op jit(solution)/shard_map/all_to_all | solution.py:236
  399.2 11.2 %copy-start.17 = (f32[8,64]{1,0:T(8,128)}, f32[8,64]{1,0:T(8,128)S(1)}, u32[]{:S(2)}) copy-start(f32[8,64]{1,0:T(8,128)S(1)} %fusion.181) | copy-start | bytes 6148
  415.1 10.7 %all-to-all-start.6 = ((f32[16,1,2048]{2,1,0:T(1,128)}), f32[16,1,2048]{2,1,0:T(1,128)S(1)}, u32[]{:S(2)}, u32[]{:S(2)}) async-start(f32[16,1,2048]{2,1,0:T(1,128)} %reshape.1629), calls=%async_computation.6 | async-start | bytes 262144 | tf_op jit(solution)/shard_map/all_to_all | solution.py:60
  425.8 11.0 %all-to-all-start.5 = ((f32[16,1,2048]{2,1,0:T(1,128)}), f32[16,1,2048]{2,1,0:T(1,128)}, u32[]{:S(2)}, u32[]{:S(2)}) async-start(f32[16,1,2048]{2,1,0:T(1,128)} %reshape.1631), calls=%async_computation.5 | async-start | bytes 262144 | tf_op jit(solution)/shard_map/all_to_all | solution.py:60
  443.5 2.5 copy-start.16
  468.1 10.3 %all-to-all-start.9 = ((f32[16,1,2048]{2,1,0:T(1,128)}), f32[16,1,2048]{2,1,0:T(1,128)S(1)}, u32[]{:S(2)}, u32[]{:S(2)}) async-start(f32[16,1,2048]{2,1,0:T(1,128)} %reshape.1635), calls=%async_computation.9 | async-start | bytes 262144 | tf_op jit(solution)/shard_map/all_to_all | solution.py:60
  478.5 10.9 %all-to-all-start.8 = ((f32[16,1,2048]{2,1,0:T(1,128)}), f32[16,1,2048]{2,1,0:T(1,128)S(1)}, u32[]{:S(2)}, u32[]{:S(2)}) async-start(f32[16,1,2048]{2,1,0:T(1,128)} %reshape.1637), calls=%async_computation.8 | async-start | bytes 262144 | tf_op jit(solution)/shard_map/all_to_all | solution.py:60
  496.6 16.5 %copy-start.5 = (f32[2,32,512]{2,1,0:T(8,128)}, f32[2,32,512]{2,1,0:T(8,128)S(1)}, u32[]{:S(2)}) copy-start(f32[2,32,512]{2,1,0:T(8,128)S(1)} %fusion.66) | copy-start | bytes 393220
  (12 other events, 18.3 us)
where the time goes:
time: 519 us; the launch traced here: 513 us
  other arithmetic  212 us (41%)
  local copies, waits for them, and re-layouts  147 us (28%)
  starting transfers between devices  47 us (9%)
  waiting for transfers between devices  43.6 us (8%)
  matrix products  31.8 us (6%)
  blocking collectives  26.5 us (5%)
    another operation x4, other arithmetic, fit_grid(): factor = jnp.linalg.cholesky(system)  94 us
    another operation x3, other arithmetic, fit_grid(): jax.scipy.linalg.solve_triangular(factor, middle, lower=True, trans='T')  79 us
    unnamed x80, local copies, waits for them, and re-layouts  67.8 us
    gather x11, local copies, waits for them, and re-layouts, local(): firsts = jnp.searchsorted(sorted_tiles, sorted_tiles, side='left')  49.8 us
    all_to_all x1, waiting for transfers between devices, from_everyone(): lax.all_to_all(jnp.broadcast_to(shard[None], (size, *shard.shape)), axis,...  21.7 us
    all_to_all x4, starting transfers between devices, items_in_groups(): lax.all_to_all(group, axis, split_axis=split_dim, concat_axis=concat_dim,...  15.7 us
    all_to_all x1, blocking collectives, summed_on_arrival(): parts = lax.all_to_all(in_blocks(shard, dim, size), axis, 0, 0, tiled=True)  14.5 us
    all_to_all x1, blocking collectives, local(): lax.all_to_all(spectrum_y, 'lat', split_axis=1, concat_axis=4, tiled=True)  12 us
  transfers between devices with their start and end apart: 9, of which 7 were waited for; matrix products, arithmetic and copies ran while one was open for 12% of the time, Pallas kernels for 0%

commit v1 on v0

v1 whole, which is shorter than its diff:
```python
import math

import jax
import jax.numpy as jnp
import ml_dtypes
import numpy as np
from jax import lax
from jax.experimental import pallas as pl
from jax.experimental.pallas import tpu as pltpu
from jax.sharding import PartitionSpec as P

NX = 512
NY = 512
TB = 32
MODES = 8
HALF = 256
SCALE = 1.0 / (NX * NY)
STEP = 2.0 * math.pi / 512

f32 = jnp.float32
bf16 = jnp.bfloat16
VM = pl.BlockSpec(memory_space=pltpu.VMEM)
SM = pl.BlockSpec(memory_space=pltpu.SMEM)
ANY = pl.BlockSpec(memory_space=pl.ANY)


def pair(table):
    table = np.asarray(table, np.float32)
    high = table.astype(ml_dtypes.bfloat16)
    low = (table - high.astype(np.float32)).astype(ml_dtypes.bfloat16)
    return high, low


def column_order():
    out = []
    for q in range(2):
        first = 2 * np.arange(128) + q
        mirror = (512 - first) % 512
        if q == 0:
            mirror[0] = 256
        out.append(np.concatenate([first, mirror]))
    return np.stack(out)


def row_order():
    first = np.arange(256)
    mirror = (512 - first) % 512
    mirror[0] = 256
    return np.concatenate([first, mirror])


def angle(left, right):
    return 2.0 * np.pi / 512 * ((left[:, None] * right[None, :]) % 512)


def mode_spectrum(order):
    cell = np.arange(TB)
    modes = np.cos(np.pi * np.arange(MODES)[:, None] * (cell[None, :] + 0.5) / TB)
    place = np.arange(16)[:, None] * TB + cell[None, :]
    wave = np.exp(-2j * np.pi / 512 * ((place[:, :, None] * order[None, None, :]) % 512))
    return np.einsum("aj,yjn->yan", modes, wave).reshape(16 * MODES, -1)


def tables():
    cols, rows = column_order(), row_order()
    every = cols.reshape(-1)
    ey = mode_spectrum(every)
    ey = np.concatenate([ey.real, ey.imag], 1)
    ex = mode_spectrum(rows).T
    ex = np.concatenate(
        [np.concatenate([ex.real, -ex.imag], 1), np.concatenate([ex.imag, ex.real], 1)], 0
    )
    own = []
    for slab in range(16):
        x_at = np.concatenate([32 * slab + 2 * np.arange(16) + h for h in range(2)])
        turn = angle(x_at, rows)
        own.append(np.concatenate([np.cos(turn), np.sin(turn)], 0))
    own_high, own_low = pair(np.stack(own))
    own = np.concatenate([own_high, own_low], 1)
    half = np.arange(HALF)
    back_y, forth_y = [], []
    for q in range(2):
        turn = angle(cols[q], half)
        back_y.append(np.concatenate([np.cos(turn), np.sin(turn)], 1))
        forth_y.append(np.concatenate([np.cos(turn.T), np.sin(turn.T)], 1))
    forth_x, back_x = [], []
    for h in range(2):
        turn = angle(half, 2 * half + h)
        forth_x.append(np.concatenate([np.cos(turn), np.sin(turn)], 0))
        back_x.append(np.concatenate([np.cos(turn.T), np.sin(turn.T)], 0))
    return dict(
        ey=pair(ey),
        ex=pair(ex),
        own=own,
        back_y=pair(np.stack(back_y)),
        forth_y=pair(np.stack(forth_y)),
        forth_x=pair(np.stack(forth_x)),
        back_x=pair(np.stack(back_x)),
    )


def split(value):
    high = value.astype(bf16)
    low = (value - high.astype(f32)).astype(bf16)
    return high, low


def mm(left, right):
    return jnp.dot(left, right, preferred_element_type=f32)


def dot3(left, right):
    return mm(left[0], right[0]) + (mm(left[0], right[1]) + mm(left[1], right[0]))


def lanes(shape):
    return lax.broadcasted_iota(jnp.int32, shape, len(shape) - 1)


def turned(value, shift, axis=1):
    size = value.shape[axis]
    shift = shift % size
    return value if shift == 0 else pltpu.roll(value, shift, axis)


def cos_sin(turn):
    half = 0.5 * turn
    sq = half * half
    cosine = 1.0 / 479001600
    for c in (-1.0 / 3628800, 1.0 / 40320, -1.0 / 720, 1.0 / 24, -0.5, 1.0):
        cosine = cosine * sq + c
    sine = 1.0 / 6227020800
    for c in (-1.0 / 39916800, 1.0 / 362880, -1.0 / 5040, 1.0 / 120, -1.0 / 6, 1.0):
        sine = sine * sq + c
    sine = sine * half
    return 1.0 - 2.0 * sine * sine, 2.0 * sine * cosine


def shift_factor(wave_sq, kx, ky):
    vertical = wave_sq - kx * kx - ky * ky
    root = jnp.sqrt(jnp.abs(vertical))
    cosine, sine = cos_sin(root)
    moving = vertical > 0.0
    return jnp.where(moving, cosine, jnp.exp(-root)), jnp.where(moving, sine, 0.0)


def references_of(slow_ref, step):
    values = [slow_ref[step, i] for i in range(8)]
    refs = [
        (values[4 * g] + values[4 * g + 1] + values[4 * g + 2] + values[4 * g + 3]) * 0.25
        for g in range(2)
    ]
    return values, refs


def velocity_rows(vel_ref, vel_tmp, step):
    for c in range(4):
        vel_tmp[c] = vel_ref[step, :, 128 * c : 128 * c + 128]
    return jnp.concatenate(
        [
            jnp.concatenate([vel_tmp[c, pl.ds(h, 16, stride=2), :] for c in range(4)], 1)
            for h in range(2)
        ],
        0,
    )


def rows_to_field(step, parts, back_high, back_low, vel_ref, vel_tmp, slow_ref, freq_ref):
    halves = []
    for q in range(2):
        both = dot3(split(parts[q]), (back_high[q], back_low[q]))
        with_cos, with_sin = both[:, :HALF], both[:, HALF:]
        halves.append(
            (with_cos[:64] - with_sin[64:], with_cos[64:] + with_sin[:64])
        )
    back = [
        jnp.concatenate([halves[0][p] + halves[1][p], halves[0][p] - halves[1][p]], 1)
        for p in range(2)
    ]
    velocity = velocity_rows(vel_ref, vel_tmp, step)
    values, refs = references_of(slow_ref, step)
    picked = [jnp.where(velocity >= 4, back[p][32:], back[p][:32]) for p in range(2)]
    turn = jnp.zeros(velocity.shape, f32)
    for i in range(8):
        turn = jnp.where(velocity == i, freq_ref[0] * (values[i] - refs[i // 4]), turn)
    cosine, sine = cos_sin(turn)
    cosine, sine = cosine * SCALE, sine * SCALE
    return (
        picked[0] * cosine - picked[1] * sine,
        picked[0] * sine + picked[1] * cosine,
    )


def route_kernel(tile_ref, bin_ref, offset_ref, weight_ref, spectra_ref, out_ref):
    tile = tile_ref[...]
    tile_f = tile.astype(f32)
    below = lax.broadcasted_iota(jnp.int32, (128, 128), 0) < lanes((128, 128))
    columns = []
    ranks = []
    for j in range(8):
        here = tile_f[:, 128 * j : 128 * (j + 1)]
        here_all = jnp.broadcast_to(here, (128, 128))
        columns.append(here_all.T)
        found = jnp.where((columns[j] == here_all) & below, 1.0, 0.0)
        for i in range(j):
            found = found + jnp.where(columns[i] == here_all, 1.0, 0.0)
        ranks.append(jnp.sum(found, axis=0, keepdims=True))
    rank = jnp.concatenate(ranks, 1).astype(jnp.int32)
    row_at = (tile >> 1) * 4 + (rank & 3)
    group_at = (tile & 1) * 2 + (rank >> 2)
    place = bin_ref[...]
    cell_x = (place >> 5).astype(f32) + offset_ref[0:1, :]
    cell_y = (place & 31).astype(f32) + offset_ref[1:2, :]
    values = jnp.concatenate(
        [
            spectra_ref[...],
            jnp.concatenate([weight_ref[...], cell_x, cell_y, jnp.zeros((5, 1024), f32)], 0),
            jnp.zeros((8, 1024), f32),
        ],
        0,
    )
    spread = jnp.concatenate([jnp.where(group_at == s, values, 0.0) for s in range(4)], 0)
    high = spread.astype(bf16)
    rest = spread - high.astype(f32)
    mid = rest.astype(bf16)
    low = (rest - mid.astype(f32)).astype(bf16)
    wide = jnp.concatenate([high, mid, low], 0)
    rows = lax.broadcasted_iota(jnp.int32, (512, 1024), 0)
    chosen = jnp.where(rows == row_at, 1.0, 0.0).astype(bf16)
    moved = lax.dot_general(
        chosen, wide, (((1,), (1,)), ((), ())), preferred_element_type=f32
    )
    out_ref[...] = (moved[:, :128] + moved[:, 128:256]) + moved[:, 256:]


def solve_kernel(got_ref, out_ref):
    turned_in = got_ref[...].T
    blocks = []
    mode = lax.broadcasted_iota(jnp.int32, (8, 1024), 0).astype(f32)
    eye_rows = lax.broadcasted_iota(jnp.int32, (64, 128), 0)
    eye = jnp.where(eye_rows == lanes((64, 128)), 1.0, 0.0)
    for t in range(2):
        both = jnp.concatenate(
            [turned_in[64 * t : 64 * t + 24], turned_in[64 * t + 32 : 64 * t + 56]], 1
        )
        along_x = jnp.cos(math.pi * mode * (both[17:18] + 0.5) / TB)
        along_y = jnp.cos(math.pi * mode * (both[18:19] + 0.5) / TB)
        basis = jnp.concatenate([along_x[a : a + 1] * along_y for a in range(8)], 0)
        wide = jnp.concatenate([basis, both[0:16], jnp.zeros((48, 1024), f32)], 0)
        system = lax.dot_general(
            basis * both[16:17],
            wide,
            (((1,), (1,)), ((), ())),
            preferred_element_type=f32,
            precision=lax.Precision.HIGHEST,
        )
        system = system + eye
        blocks.append([system[8 * a : 8 * a + 8] for a in range(8)])
    sub = lax.broadcasted_iota(jnp.int32, (8, 128), 0)
    for j in range(64):
        at, inner = j // 8, j % 8
        for t in range(2):
            mine = blocks[t]
            row = mine[at][inner : inner + 1]
            row = row / row[:, j : j + 1]
            fresh = []
            for a in range(8):
                new = mine[a] - mine[a][:, j : j + 1] * row
                if a == at:
                    new = jnp.where(sub == inner, row, new)
                fresh.append(new)
            blocks[t] = fresh
    stacked = jnp.concatenate([blocks[t][a] for a in range(8) for t in range(2)], 0)
    final = stacked.T
    odd = (lax.broadcasted_iota(jnp.int32, (32, 128), 0) & 1) == 1
    for f in range(8):
        out_ref[32 * f : 32 * f + 32] = jnp.where(
            odd, final[72 + f : 73 + f], final[64 + f : 65 + f]
        )


def first_kernel(
    lat_ref,
    freq_ref,
    slow_ref,
    got_ref,
    vel_ref,
    own_hbm,
    ey_h,
    ey_l,
    ex_h,
    ex_l,
    by_h,
    by_l,
    fy_h,
    fy_l,
    out_ref,
    image_ref,
    own_ref,
    vel_tmp,
    sem,
):
    fetch = pltpu.make_async_copy(own_hbm.at[lat_ref[0]], own_ref, sem)
    fetch.start()
    rows = lax.broadcasted_iota(jnp.int32, (128, 128), 0)
    groups = lanes((128, 128)) >> 4
    stacked = []
    for p in range(2):
        value = got_ref[pl.ds(p, 128, stride=2), :]
        for k in (1, 2, 4):
            s_bit, g_bit = (rows & k) != 0, (groups & k) != 0
            down = turned(turned(value, k, 0), -16 * k, 1)
            up = turned(turned(value, -k, 0), 16 * k, 1)
            value = jnp.where(
                s_bit & ~g_bit, down, jnp.where(~s_bit & g_bit, up, value)
            )
        stacked.append(value)
    both = dot3(split(jnp.concatenate(stacked, 0)), (ey_h[...], ey_l[...]))
    along_y = jnp.concatenate(
        [both[:128, :512] - both[128:, 512:], both[:128, 512:] + both[128:, :512]], 0
    )
    along_y = split(along_y)
    fetch.wait()
    own_high, own_both = own_ref[:64], own_ref[...]
    values, refs = references_of(slow_ref, 0)
    row_at = lax.broadcasted_iota(jnp.int32, (HALF, 128), 0)
    kx = row_at.astype(f32) * STEP
    kx_edge = jnp.where(row_at[:8] == 0, 256, row_at[:8]).astype(f32) * STEP
    parts = []
    for q in range(2):
        here = tuple(a[:, 256 * q : 256 * q + 256] for a in along_y)
        spectrum = dot3((ex_h[...], ex_l[...]), here)
        at = 2 * lanes((1, 128)) + q
        at_mirror = jnp.where(at == 0, 256, at) if q == 0 else at
        per_ref = []
        for g in range(2):
            wave = freq_ref[0] * refs[g]
            wave_sq = wave * wave
            ky = at.astype(f32) * STEP
            straight = shift_factor(wave_sq, kx, ky)
            edge = shift_factor(wave_sq, kx_edge, ky)
            if q == 0:
                ky_mirror = at_mirror.astype(f32) * STEP
                straight_m = shift_factor(wave_sq, kx, ky_mirror)
                edge_m = shift_factor(wave_sq, kx_edge, ky_mirror)
            else:
                straight_m, edge_m = straight, edge
            factor = []
            for p in range(2):
                top = jnp.concatenate([straight[p], straight_m[p]], 1)
                border = jnp.concatenate([edge[p], edge_m[p]], 1)
                factor.append(jnp.concatenate([top, border, top[8:]], 0))
            re, im = spectrum[:512], spectrum[512:]
            moved = jnp.concatenate(
                [re * factor[0] - im * factor[1], re * factor[1] + im * factor[0]], 1
            )
            high, low = split(moved)
            with_high = mm(own_both, high)
            total = with_high[:64] + (with_high[64:] + mm(own_high, low))
            per_ref.append(
                (
                    total[:32, :256] - total[32:, 256:],
                    total[:32, 256:] + total[32:, :256],
                )
            )
        parts.append(
            jnp.concatenate([per_ref[g][p] for p in range(2) for g in range(2)], 0)
        )
    field = rows_to_field(0, parts, by_h, by_l, vel_ref, vel_tmp, slow_ref, freq_ref)
    image_ref[...] = field[0]
    stacked = jnp.concatenate(field, 0)
    group = lanes((16, 128)) >> 5
    for q in range(2):
        lower, upper = stacked[:, :HALF], stacked[:, HALF:]
        mixed = lower + upper if q == 0 else lower - upper
        both = dot3(split(mixed), (fy_h[q], fy_l[q]))
        with_cos, with_sin = both[:, :HALF], both[:, HALF:]
        result = (with_cos[:32] + with_sin[32:], with_cos[32:] - with_sin[:32])
        for jj in range(8):
            col, pos = jj // 4, jj % 4
            packed = None
            for p in range(2):
                for h in range(2):
                    piece = result[p][16 * h : 16 * h + 16, 128 * col : 128 * col + 128]
                    piece = turned(piece, 32 * (2 * p + h - pos))
                    packed = piece if packed is None else jnp.where(group == 2 * p + h, piece, packed)
            dest = 2 * jj + q
            out_ref[16 * dest : 16 * dest + 16] = packed


def column_kernel(lat_ref, freq_ref, slow_ref, got_ref, fx_h, fx_l, bx_h, bx_l, out_ref):
    data = got_ref[...]
    lane = lanes((HALF, 128))
    group = lane >> 5
    rolled = [turned(data, 32 * d) for d in range(4)]

    def spread(source):
        out = rolled[(0 - source) % 4]
        for t in range(1, 4):
            out = jnp.where(group == t, rolled[(t - source) % 4], out)
        return out

    found = []
    for h in range(2):
        weights = split(jnp.concatenate([spread(h), spread(2 + h)], 1))
        both = dot3((fx_h[h], fx_l[h]), weights)
        found.append(
            (
                both[:256, :128] + both[256:, 128:],
                both[:256, 128:] - both[256:, :128],
            )
        )
    upper = lane >= 64
    re, im = [
        jnp.where(upper, found[0][p] - found[1][p], found[0][p] + found[1][p]) for p in range(2)
    ]
    values, refs = references_of(slow_ref, 1)
    band = lat_ref[0]
    q, jj = band & 1, band >> 1
    row_lane = lanes((1, 128))
    at = 2 * (32 * (jj & 3) + (row_lane & 31)) + q
    at = jnp.where((at == 0) & (jj >= 4), 256, at)
    ky = at.astype(f32) * STEP
    wave = freq_ref[0] * jnp.where(((row_lane >> 5) & 1) == 1, refs[1], refs[0])
    row_at = lax.broadcasted_iota(jnp.int32, (HALF, 128), 0)
    kx = jnp.where(upper, row_at - 256, row_at).astype(f32) * STEP
    fac_re, fac_im = shift_factor(wave * wave, kx, ky)
    moved_re, moved_im = re * fac_re - im * fac_im, re * fac_im + im * fac_re
    turned_re, turned_im = turned(moved_re, 64), turned(moved_im, 64)
    for h in range(2):
        if h == 0:
            mixed = jnp.where(upper, moved_im + turned_im, moved_re + turned_re)
        else:
            mixed = jnp.where(upper, turned_im - moved_im, moved_re - turned_re)
        both = dot3((bx_h[h], bx_l[h]), split(mixed))
        crossed = turned(both[256:], 64)
        result = both[:256] + jnp.where(upper, crossed, -crossed)
        out_ref[:, h] = result.reshape(16, 16, 128)


def last_kernel(
    freq_ref, slow_ref, got_ref, vel_ref, image_ref, by_h, by_l, wave_ref, out_ref, vel_tmp, wave_tmp
):
    group = lanes((16, 128)) >> 5
    parts = []
    for q in range(2):
        rows = []
        for p in range(2):
            for g in range(2):
                for h in range(2):
                    cols = []
                    for col in range(2):
                        packed = None
                        for pos in range(4):
                            piece = got_ref[2 * (4 * col + pos) + q, h]
                            piece = turned(piece, 32 * (pos - (2 * p + g)))
                            packed = piece if packed is None else jnp.where(group == pos, piece, packed)
                        cols.append(packed)
                    rows.append(jnp.concatenate(cols, 1))
        parts.append(jnp.concatenate(rows, 0))
    field = rows_to_field(1, parts, by_h, by_l, vel_ref, vel_tmp, slow_ref, freq_ref)
    for p in range(2):
        for h in range(2):
            for c in range(4):
                wave_tmp[p, c, pl.ds(h, 16, stride=2), :] = field[p][
                    16 * h : 16 * h + 16, 128 * c : 128 * c + 128
                ]
    for p in range(2):
        wave_ref[p] = jnp.concatenate([wave_tmp[p, c] for c in range(4)], 1)
    upper = lanes((32, 128)) >= 64
    for d in range(8):
        col, pos = d // 2, d % 2
        first = turned(image_ref[:, 128 * col : 128 * col + 128], -64 * pos)
        second = turned(field[0][:, 128 * col : 128 * col + 128], 64 - 64 * pos)
        out_ref[d] = jnp.where(upper, second, first)


def sum_kernel(got_ref, out_ref, image_tmp):
    total = got_ref[0]
    for d in range(1, 8):
        total = total + got_ref[d]
    for h in range(2):
        image_tmp[pl.ds(h, 16, stride=2), :] = total[16 * h : 16 * h + 16]
    total = image_tmp[...]
    out_ref[0] = total[:, :64]
    out_ref[1] = total[:, 64:]


def call(kernel, outs, in_specs, mega, scratch=()):
    many = isinstance(outs, list)
    shapes = [jax.ShapeDtypeStruct(s, f32) for s in (outs if many else [outs])]
    return pl.pallas_call(
        kernel,
        out_shape=shapes if many else shapes[0],
        in_specs=in_specs,
        out_specs=[VM] * len(shapes) if many else VM,
        scratch_shapes=list(scratch),
        compiler_params=pltpu.CompilerParams(vmem_limit_bytes=mega * 1024 * 1024),
    )


def local(spectra, tile_route, bin_in_tile, trace_offset, weights, frequency, slowness, vel_index):
    const = tables()
    lat_at = lax.axis_index("lat").astype(jnp.int32).reshape(1)
    everyone = ("freq", "lat")
    sent = call(route_kernel, (512, 128), [VM] * 5, 24)(
        tile_route.reshape(1, 1024),
        bin_in_tile.reshape(1, 1024),
        trace_offset,
        weights.reshape(1, 1024),
        spectra.reshape(16, 1024),
    )
    got = lax.all_to_all(sent.reshape(128, 4, 128), everyone, 0, 0, tiled=True)
    sent = call(solve_kernel, (256, 128), [VM], 24)(got.reshape(512, 128))
    got = lax.all_to_all(sent.reshape(128, 2, 128), everyone, 0, 0, tiled=True)
    sent, image = call(
        first_kernel,
        [(256, 128), (32, 512)],
        [SM, SM, SM, VM, VM, ANY] + [VM] * 8,
        40,
        [
            pltpu.VMEM((128, 512), bf16),
            pltpu.VMEM((4, 32, 128), jnp.int32),
            pltpu.SemaphoreType.DMA,
        ],
    )(
        lat_at,
        frequency,
        slowness,
        got.reshape(256, 128),
        vel_index,
        const["own"],
        *const["ey"],
        *const["ex"],
        *const["back_y"],
        *const["forth_y"],
    )
    got = lax.all_to_all(sent.reshape(16, 16, 128), "lat", 0, 0, tiled=True)
    sent = call(column_kernel, (16, 2, 16, 128), [SM, SM, SM] + [VM] * 5, 24)(
        lat_at,
        frequency,
        slowness,
        got.reshape(256, 128),
        *const["forth_x"],
        *const["back_x"],
    )
    got = lax.all_to_all(sent.reshape(16, 32, 128), "lat", 0, 0, tiled=True)
    wave, sent = call(
        last_kernel, [(2, 32, 512), (8, 32, 128)],
        [SM, SM] + [VM] * 5,
        24,
        [pltpu.VMEM((4, 32, 128), jnp.int32), pltpu.VMEM((2, 4, 32, 128), f32)],
    )(
        frequency,
        slowness,
        got.reshape(16, 2, 16, 128),
        vel_index,
        image,
        *const["back_y"],
    )
    got = lax.all_to_all(sent, "freq", 0, 0, tiled=True)
    depth_image = call(sum_kernel, (2, 32, 64), [VM], 16, [pltpu.VMEM((32, 128), f32)])(got)
    return (wave.reshape(2, 1, 32, 512), depth_image)


def solution(mesh):
    return jax.shard_map(
        local,
        mesh=mesh,
        in_specs=(
            P(None, None, ("freq", "lat")),
            P(("freq", "lat"), None),
            P(("freq", "lat")),
            P(None, ("freq", "lat")),
            P(("freq", "lat")),
            P("freq"),
            P(),
            P(None, "lat", None),
        ),
        out_specs=(P(None, "freq", "lat", None), P(None, "lat", "freq")),
        check_vma=False,
    )
```

time: 519 us -> 104 us (0.20)
  other arithmetic: 212 us -> 0 us
  local copies, waits for them, and re-layouts: 147 us -> 14.9 us
  starting transfers between devices: 47 us -> 3.99 us
  waiting for transfers between devices: 43.6 us -> 9.59 us
  matrix products: 31.8 us -> 0 us
  blocking collectives: 26.5 us -> 53.8 us
  Pallas kernels: 0 us -> 19.9 us
    another operation x27 -> x0, other arithmetic: 175 us -> none  [the longest x4 94 us: fit_grid(): factor = jnp.linalg.cholesky(system)]
    gather x12 -> x0, local copies, waits for them, and re-layouts: 54.3 us -> none  [the longest x11 49.8 us: local(): firsts = jnp.searchsorted(sorted_tiles, sorted_tiles, side='left')]
    unnamed x80 -> x40, local copies, waits for them, and re-layouts: 67.8 us -> 14.9 us
    all_to_all x9 -> x1, starting transfers between devices: 47 us -> 3.99 us  [local(): got = lax.all_to_all(sent.reshape(128, 2, 128), everyone, 0, 0, tiled=True)]
    all_to_all x9 -> x1, waiting for transfers between devices: 43.6 us -> 9.59 us  [local(): got = lax.all_to_all(sent.reshape(128, 2, 128), everyone, 0, 0, tiled=True)]
    dot_general x26 -> x0, matrix products: 30.3 us -> none  [the longest x2 10.2 us: one_block(): jnp.einsum('iabgc,paqbgc->gipq', weighted, data_part, precision=lax.Preci...]
    all_to_all x2 -> x4, blocking collectives: 26.5 us -> 53.8 us  [the longest x1 22.8 us: local(): got = lax.all_to_all(sent.reshape(128, 4, 128), everyone, 0, 0, tiled=True)]
    pallas_call x0 -> x6, Pallas kernels: none -> 19.9 us  [the longest x1 7.28 us: local(): sent = call(solve_kernel, (256, 128), [VM], 24)(got.reshape(512, 128))]
  transfers between devices with their start and end apart: 9 -> 1, of which waited for: 7 -> 1; matrix products, arithmetic and copies ran while one was open for 12% -> 0% of each run, Pallas kernels for 0% -> 0%
where the time goes in v1:
time: 104 us; the launch traced here: 103 us
  blocking collectives  53.8 us (52%)
  Pallas kernels  19.9 us (19%)
  local copies, waits for them, and re-layouts  14.9 us (14%)
  waiting for transfers between devices  9.59 us (9%)
  starting transfers between devices  3.99 us (4%)
  between operations  1.36 us (1%)
    all_to_all x1, blocking collectives, local(): got = lax.all_to_all(sent.reshape(128, 4, 128), everyone, 0, 0, tiled=True)  22.8 us
    unnamed x40, local copies, waits for them, and re-layouts  14.9 us
    all_to_all x1, blocking collectives, local(): got = lax.all_to_all(sent.reshape(16, 32, 128), 'lat', 0, 0, tiled=True)  10.7 us
    all_to_all x1, blocking collectives, local(): got = lax.all_to_all(sent, 'freq', 0, 0, tiled=True)  10.7 us
    all_to_all x1, waiting for transfers between devices, local(): got = lax.all_to_all(sent.reshape(128, 2, 128), everyone, 0, 0, tiled=True)  9.59 us
    all_to_all x1, blocking collectives, local(): got = lax.all_to_all(sent.reshape(16, 16, 128), 'lat', 0, 0, tiled=True)  9.58 us
    pallas_call x1, Pallas kernels, local(): sent = call(solve_kernel, (256, 128), [VM], 24)(got.reshape(512, 128))  7.28 us
    pallas_call x1, Pallas kernels, local(): call(first_kernel, [(256, 128), (32, 512)], [SM, SM, SM, VM, VM, ANY] + [...  6.81 us
  transfers between devices with their start and end apart: 1, of which 1 were waited for; matrix products, arithmetic and copies ran while one was open for 0% of the time, Pallas kernels for 0%

profile of v1, /device:TPU:1, one launch (start us, length us, event | category | flops | bytes accessed | tf_op | source)
XLA Modules:
  0.0 103.5 jit_solution(1739496441213784774)
XLA Ops:
  0.6 0.0 copy-start.14
  0.6 0.8 copy-done.14
  1.5 0.7 copy-done.16
  2.2 0.7 copy-done.17
  2.9 0.7 copy-done.18
  3.5 0.7 copy-done.19
  4.2 1.1 %shard_map.212 = f32[512,128]{1,0:T(8,128)S(1)} custom-call(s32[1,1024]{1,0:T(1,128)S(1)} %bitcast.24, s32[1,1024]{1,0:T(1,128)S(1)} %bitcast.25, f32[2,1024]{1,0:T(2,128)S(1)} %copy-done.16, f32[1,1024]{1,0:T(1,128)S(1)} %bitcast.26, f32[16,1024]{1,0:T(8,128)S(1)} %bitcast.23), custom_call_target="tpu_custom_call" | custom-call | tf_op jit(solution)/shard_map/pallas_call | solution.py:506
  5.3 22.8 %all_to_all.25 = f32[128,4,128]{2,1,0:T(4,128)S(1)} all-to-all(f32[128,4,128]{2,1,0:T(4,128)S(1)} %bitcast.18), channel_id=1, replica_groups=mesh['freq'=8,'lat'=16] {'freq','lat'}, dimensions={0} | all-to-all | bytes 524288 | tf_op jit(solution)/shard_map/all_to_all | solution.py:513
  28.1 7.3 %shard_map.213 = f32[256,128]{1,0:T(8,128)} custom-call(f32[512,128]{1,0:T(8,128)S(1)} %bitcast.17), custom_call_target="tpu_custom_call" | custom-call | tf_op jit(solution)/shard_map/pallas_call | solution.py:514
  35.4 4.0 %all-to-all-start.1 = ((f32[128,2,128]{2,1,0:T(2,128)}), f32[128,2,128]{2,1,0:T(2,128)S(1)}, u32[]{:S(2)}, u32[]{:S(2)}) async-start(f32[128,2,128]{2,1,0:T(2,128)} %bitcast.7), calls=%async_computation.1 | async-start | bytes 262144 | tf_op jit(solution)/shard_map/all_to_all | solution.py:515
  40.0 9.6 %all-to-all-done.1 = f32[128,2,128]{2,1,0:T(2,128)S(1)} async-done(((f32[128,2,128]{2,1,0:T(2,128)}), f32[128,2,128]{2,1,0:T(2,128)S(1)}, u32[]{:S(2)}, u32[]{:S(2)}) %all-to-all-start.1) | async-done | bytes 131104 | tf_op jit(solution)/shard_map/all_to_all | solution.py:515
  49.6 1.6 %copy-done = bf16[16,128,512]{2,1,0:T(8,128)(2,1)S(1)} copy-done((bf16[16,128,512]{2,1,0:T(8,128)(2,1)S(1)}, bf16[16,128,512]{2,1,0:T(8,128)(2,1)}, u32[]{:S(2)}) %copy-start) | copy-done | bytes 2097176
  51.2 1.0 %copy-done.1 = bf16[2,256,512]{2,1,0:T(8,128)(2,1)S(1)} copy-done((bf16[2,256,512]{2,1,0:T(8,128)(2,1)S(1)}, bf16[2,256,512]{2,1,0:T(8,128)(2,1)}, u32[]{:S(2)}) %copy-start.1) | copy-done | bytes 524312
  52.2 1.0 %copy-done.2 = bf16[2,256,512]{2,1,0:T(8,128)(2,1)S(1)} copy-done((bf16[2,256,512]{2,1,0:T(8,128)(2,1)S(1)}, bf16[2,256,512]{2,1,0:T(8,128)(2,1)}, u32[]{:S(2)}) %copy-start.2) | copy-done | bytes 524312
  53.3 0.9 copy-done.3
  54.2 1.0 %copy-done.8 = bf16[2,256,512]{2,1,0:T(8,128)(2,1)S(1)} copy-done((bf16[2,256,512]{2,1,0:T(8,128)(2,1)S(1)}, bf16[2,256,512]{2,1,0:T(8,128)(2,1)}, u32[]{:S(2)}) %copy-start.8) | copy-done | bytes 524312
  55.2 1.0 %copy-done.9 = bf16[2,256,512]{2,1,0:T(8,128)(2,1)S(1)} copy-done((bf16[2,256,512]{2,1,0:T(8,128)(2,1)S(1)}, bf16[2,256,512]{2,1,0:T(8,128)(2,1)}, u32[]{:S(2)}) %copy-start.9) | copy-done | bytes 524312
  56.3 1.0 %copy-done.10 = bf16[1024,256]{1,0:T(8,128)(2,1)S(1)} copy-done((bf16[1024,256]{1,0:T(8,128)(2,1)S(1)}, bf16[1024,256]{1,0:T(8,128)(2,1)}, u32[]{:S(2)}) %copy-start.10) | copy-done | bytes 524312
  57.3 1.0 %copy-done.11 = bf16[1024,256]{1,0:T(8,128)(2,1)S(1)} copy-done((bf16[1024,256]{1,0:T(8,128)(2,1)S(1)}, bf16[1024,256]{1,0:T(8,128)(2,1)}, u32[]{:S(2)}) %copy-start.11) | copy-done | bytes 524312
  58.4 0.9 copy-done.12
  59.3 0.9 copy-done.13
  60.3 0.7 copy-done.15
  61.0 6.8 %shard_map.214 = (f32[256,128]{1,0:T(8,128)S(1)}, f32[32,512]{1,0:T(8,128)S(1)}) custom-call(s32[1]{0:T(128)} %bitcast.lat_ref, f32[1]{0:T(128)S(6)} %copy.24.freq_ref, f32[2,8]{1,0:T(2,128)S(1)} %copy-done.15, f32[256,128]{1,0:T(8,128)S(1)} %bitcast.20, s32[2,32,512]{2,1,0:T(8,128)S(1)} %copy-done.3, bf16[16,128,512]{2,1,0:T(8,128)(2,1)S(1)} %copy-done, ...), custom_call_target="tpu_custom_call" | custom-call | tf_op jit(solution)/shard_map/pallas_call | solution.py:516
  67.8 9.6 %all_to_all.26 = f32[16,16,128]{2,1,0:T(8,128)S(1)} all-to-all(f32[16,16,128]{2,1,0:T(8,128)S(1)} %bitcast.22), channel_id=1, replica_groups=mesh['freq'=8,'lat'=16] {'lat'}, dimensions={0} | all-to-all | bytes 262144 | tf_op jit(solution)/shard_map/all_to_all | solution.py:538
  77.4 0.0 copy-done.4
  77.4 0.0 copy-done.5
  77.4 0.0 copy-done.6
  77.4 2.1 %shard_map.215 = f32[16,2,16,128]{3,2,1,0:T(8,128)S(1)} custom-call(s32[1]{0:T(128)} %bitcast.lat_ref, f32[1]{0:T(128)S(6)} %copy.24.freq_ref, f32[2,8]{1,0:T(2,128)S(1)} %copy-done.15, f32[256,128]{1,0:T(8,128)S(1)} %bitcast.21, bf16[2,512,256]{2,1,0:T(8,128)(2,1)S(1)} %copy-done.7, bf16[2,512,256]{2,1,0:T(8,128)(2,1)S(1)} %copy-done.6, ...), custom_call_target="tpu_custom_call" | custom-call | tf_op jit(solution)/shard_map/pallas_call | solution.py:539
  79.5 10.7 %all_to_all.27 = f32[16,32,128]{2,1,0:T(8,128)S(1)} all-to-all(f32[16,32,128]{2,1,0:T(8,128)S(1)} %bitcast.19), channel_id=1, replica_groups=mesh['freq'=8,'lat'=16] {'lat'}, dimensions={0} | all-to-all | bytes 524288 | tf_op jit(solution)/shard_map/all_to_all | solution.py:547
  90.2 1.9 %shard_map.216 = (f32[2,32,512]{2,1,0:T(8,128)}, f32[8,32,128]{2,1,0:T(8,128)S(1)}) custom-call(f32[1]{0:T(128)S(6)} %copy.24.freq_ref, f32[2,8]{1,0:T(2,128)S(1)} %copy-done.15, f32[16,2,16,128]{3,2,1,0:T(8,128)S(1)} %bitcast.16, s32[2,32,512]{2,1,0:T(8,128)S(1)} %copy-done.3, f32[32,512]{1,0:T(8,128)S(1)} %get-tuple-element.7.image_ref, ...), custom_call_target="tpu_custom_call" | custom-call | tf_op jit(solution)/shard_map/pallas_call | solution.py:548
  92.1 10.7 %all_to_all.28.got_ref = f32[8,32,128]{2,1,0:T(8,128)S(1)} all-to-all(f32[8,32,128]{2,1,0:T(8,128)S(1)} %get-tuple-element.9), channel_id=1, replica_groups=mesh['freq'=8,'lat'=16] {'freq'}, dimensions={0} | all-to-all | bytes 262144 | tf_op jit(solution)/shard_map/all_to_all | solution.py:561
  102.8 0.7 shard_map.217
  (20 shorter events, 0.0 us)
Async XLA Ops:
  0.6 0.8 copy-start.14
  1.5 0.7 copy-start.16
  2.2 0.7 copy-start.17
  2.9 0.7 copy-start.18
  3.5 0.7 copy-start.19
  35.4 14.2 %all-to-all-start.1 = ((f32[128,2,128]{2,1,0:T(2,128)}), f32[128,2,128]{2,1,0:T(2,128)S(1)}, u32[]{:S(2)}, u32[]{:S(2)}) async-start(f32[128,2,128]{2,1,0:T(2,128)} %bitcast.7), calls=%async_computation.1 | async-start | bytes 262144 | tf_op jit(solution)/shard_map/all_to_all | solution.py:515
  49.6 1.6 %copy-start = (bf16[16,128,512]{2,1,0:T(8,128)(2,1)S(1)}, bf16[16,128,512]{2,1,0:T(8,128)(2,1)}, u32[]{:S(2)}) copy-start(bf16[16,128,512]{2,1,0:T(8,128)(2,1)} %constant.30.clone.own_hbm) | copy-start | bytes 6291460
  51.2 1.0 %copy-start.1 = (bf16[2,256,512]{2,1,0:T(8,128)(2,1)S(1)}, bf16[2,256,512]{2,1,0:T(8,128)(2,1)}, u32[]{:S(2)}) copy-start(bf16[2,256,512]{2,1,0:T(8,128)(2,1)} %constant.36.clone.by_l) | copy-start | bytes 1572868
  52.2 1.0 %copy-start.2 = (bf16[2,256,512]{2,1,0:T(8,128)(2,1)S(1)}, bf16[2,256,512]{2,1,0:T(8,128)(2,1)}, u32[]{:S(2)}) copy-start(bf16[2,256,512]{2,1,0:T(8,128)(2,1)} %constant.35.clone.by_h) | copy-start | bytes 1572868
  53.3 0.9 copy-start.3
  54.2 1.0 %copy-start.8 = (bf16[2,256,512]{2,1,0:T(8,128)(2,1)S(1)}, bf16[2,256,512]{2,1,0:T(8,128)(2,1)}, u32[]{:S(2)}) copy-start(bf16[2,256,512]{2,1,0:T(8,128)(2,1)} %constant.38.clone.fy_l) | copy-start | bytes 1572868
  55.2 1.0 %copy-start.9 = (bf16[2,256,512]{2,1,0:T(8,128)(2,1)S(1)}, bf16[2,256,512]{2,1,0:T(8,128)(2,1)}, u32[]{:S(2)}) copy-start(bf16[2,256,512]{2,1,0:T(8,128)(2,1)} %constant.37.clone.fy_h) | copy-start | bytes 1572868
  56.3 1.0 %copy-start.10 = (bf16[1024,256]{1,0:T(8,128)(2,1)S(1)}, bf16[1024,256]{1,0:T(8,128)(2,1)}, u32[]{:S(2)}) copy-start(bf16[1024,256]{1,0:T(8,128)(2,1)} %constant.34.clone.ex_l) | copy-start | bytes 1572868
  57.3 1.0 %copy-start.11 = (bf16[1024,256]{1,0:T(8,128)(2,1)S(1)}, bf16[1024,256]{1,0:T(8,128)(2,1)}, u32[]{:S(2)}) copy-start(bf16[1024,256]{1,0:T(8,128)(2,1)} %constant.33.clone.ex_h) | copy-start | bytes 1572868
  58.4 0.9 copy-start.12
  59.3 0.9 copy-start.13
  60.3 0.7 copy-start.15
  60.9 16.4 %copy-start.4 = (bf16[2,512,256]{2,1,0:T(8,128)(2,1)S(1)}, bf16[2,512,256]{2,1,0:T(8,128)(2,1)}, u32[]{:S(2)}) copy-start(bf16[2,512,256]{2,1,0:T(8,128)(2,1)} %constant.42.clone.bx_l) | copy-start | bytes 1572868
  60.9 16.4 %copy-start.5 = (bf16[2,512,256]{2,1,0:T(8,128)(2,1)S(1)}, bf16[2,512,256]{2,1,0:T(8,128)(2,1)}, u32[]{:S(2)}) copy-start(bf16[2,512,256]{2,1,0:T(8,128)(2,1)} %constant.41.clone.bx_h) | copy-start | bytes 1572868
  60.9 16.4 %copy-start.6 = (bf16[2,512,256]{2,1,0:T(8,128)(2,1)S(1)}, bf16[2,512,256]{2,1,0:T(8,128)(2,1)}, u32[]{:S(2)}) copy-start(bf16[2,512,256]{2,1,0:T(8,128)(2,1)} %constant.40.clone.fx_l) | copy-start | bytes 1572868
  60.9 16.4 %copy-start.7 = (bf16[2,512,256]{2,1,0:T(8,128)(2,1)S(1)}, bf16[2,512,256]{2,1,0:T(8,128)(2,1)}, u32[]{:S(2)}) copy-start(bf16[2,512,256]{2,1,0:T(8,128)(2,1)} %constant.39.clone.fx_h) | copy-start | bytes 1572868

commit v2 on v1

--- a/solution.py
+++ b/solution.py
@@ -21,7 +21,7 @@
 bf16 = jnp.bfloat16
 VM = pl.BlockSpec(memory_space=pltpu.VMEM)
 SM = pl.BlockSpec(memory_space=pltpu.SMEM)
-ANY = pl.BlockSpec(memory_space=pl.ANY)
+HBM = pl.BlockSpec(memory_space=pltpu.HBM)
 
 
 def pair(table):
@@ -191,8 +191,26 @@
     )
 
 
-def route_kernel(tile_ref, bin_ref, offset_ref, weight_ref, spectra_ref, out_ref):
-    tile = tile_ref[...]
+class Fetch:
+    def __init__(self, sources, targets, sems):
+        self.targets = targets
+        self.copies = [
+            pltpu.make_async_copy(s, t, sems.at[i]) for i, (s, t) in enumerate(zip(sources, targets))
+        ]
+        for copy in self.copies:
+            copy.start()
+
+    def take(self, *which):
+        for i in which:
+            self.copies[i].wait()
+        out = [self.targets[i] for i in which]
+        return out[0] if len(out) == 1 else out
+
+
+def route_kernel(*refs):
+    sources, out_ref, targets, sems = refs[:5], refs[5], refs[6:11], refs[11]
+    fetch = Fetch(sources, targets, sems)
+    tile = fetch.take(0)[...]
     tile_f = tile.astype(f32)
     below = lax.broadcasted_iota(jnp.int32, (128, 128), 0) < lanes((128, 128))
     columns = []
@@ -208,6 +226,7 @@
     rank = jnp.concatenate(ranks, 1).astype(jnp.int32)
     row_at = (tile >> 1) * 4 + (rank & 3)
     group_at = (tile & 1) * 2 + (rank >> 2)
+    bin_ref, offset_ref, weight_ref, spectra_ref = fetch.take(1, 2, 3, 4)
     place = bin_ref[...]
     cell_x = (place >> 5).astype(f32) + offset_ref[0:1, :]
     cell_y = (place & 31).astype(f32) + offset_ref[1:2, :]
@@ -284,24 +303,12 @@
     freq_ref,
     slow_ref,
     got_ref,
-    vel_ref,
-    own_hbm,
-    ey_h,
-    ey_l,
-    ex_h,
-    ex_l,
-    by_h,
-    by_l,
-    fy_h,
-    fy_l,
-    out_ref,
-    image_ref,
-    own_ref,
-    vel_tmp,
-    sem,
+    *refs,
 ):
-    fetch = pltpu.make_async_copy(own_hbm.at[lat_ref[0]], own_ref, sem)
-    fetch.start()
+    sources, out_ref, image_ref = refs[:10], refs[10], refs[11]
+    targets, vel_tmp, sems = refs[12:22], refs[22], refs[23]
+    sources = (*sources[:4], sources[4].at[lat_ref[0]], *sources[5:])
+    fetch = Fetch(sources, targets, sems)
     rows = lax.broadcasted_iota(jnp.int32, (128, 128), 0)
     groups = lanes((128, 128)) >> 4
     stacked = []
@@ -315,12 +322,13 @@
                 s_bit & ~g_bit, down, jnp.where(~s_bit & g_bit, up, value)
             )
         stacked.append(value)
+    ey_h, ey_l = fetch.take(0, 1)
     both = dot3(split(jnp.concatenate(stacked, 0)), (ey_h[...], ey_l[...]))
     along_y = jnp.concatenate(
         [both[:128, :512] - both[128:, 512:], both[:128, 512:] + both[128:, :512]], 0
     )
     along_y = split(along_y)
-    fetch.wait()
+    ex_h, ex_l, own_ref = fetch.take(2, 3, 4)
     own_high, own_both = own_ref[:64], own_ref[...]
     values, refs = references_of(slow_ref, 0)
     row_at = lax.broadcasted_iota(jnp.int32, (HALF, 128), 0)
@@ -366,9 +374,11 @@
         parts.append(
             jnp.concatenate([per_ref[g][p] for p in range(2) for g in range(2)], 0)
         )
+    vel_ref, by_h, by_l = fetch.take(5, 6, 7)
     field = rows_to_field(0, parts, by_h, by_l, vel_ref, vel_tmp, slow_ref, freq_ref)
     image_ref[...] = field[0]
     stacked = jnp.concatenate(field, 0)
+    fy_h, fy_l = fetch.take(8, 9)
     group = lanes((16, 128)) >> 5
     for q in range(2):
         lower, upper = stacked[:, :HALF], stacked[:, HALF:]
@@ -503,7 +513,20 @@
     const = tables()
     lat_at = lax.axis_index("lat").astype(jnp.int32).reshape(1)
     everyone = ("freq", "lat")
-    sent = call(route_kernel, (512, 128), [VM] * 5, 24)(
+    sent = call(
+        route_kernel,
+        (512, 128),
+        [HBM] * 5,
+        60,
+        [
+            pltpu.VMEM((1, 1024), jnp.int32),
+            pltpu.VMEM((1, 1024), jnp.int32),
+            pltpu.VMEM((2, 1024), f32),
+            pltpu.VMEM((1, 1024), f32),
+            pltpu.VMEM((16, 1024), f32),
+            pltpu.SemaphoreType.DMA((5,)),
+        ],
+    )(
         tile_route.reshape(1, 1024),
         bin_in_tile.reshape(1, 1024),
         trace_offset,
@@ -516,22 +539,28 @@
     sent, image = call(
         first_kernel,
         [(256, 128), (32, 512)],
-        [SM, SM, SM, VM, VM, ANY] + [VM] * 8,
-        40,
+        [SM, SM, SM, VM] + [HBM] * 10,
+        59,
         [
+            pltpu.VMEM((128, 1024), bf16),
+            pltpu.VMEM((128, 1024), bf16),
+            pltpu.VMEM((1024, 256), bf16),
+            pltpu.VMEM((1024, 256), bf16),
             pltpu.VMEM((128, 512), bf16),
+            pltpu.VMEM((2, 32, 512), jnp.int32),
+            *[pltpu.VMEM((2, 256, 512), bf16)] * 4,
             pltpu.VMEM((4, 32, 128), jnp.int32),
-            pltpu.SemaphoreType.DMA,
+            pltpu.SemaphoreType.DMA((10,)),
         ],
     )(
         lat_at,
         frequency,
         slowness,
         got.reshape(256, 128),
-        vel_index,
-        const["own"],
         *const["ey"],
         *const["ex"],
+        const["own"],
+        vel_index,
         *const["back_y"],
         *const["forth_y"],
     )

time: 104 us -> 93.7 us (0.901)
  local copies, waits for them, and re-layouts: 14.9 us -> 0.7 us
  Pallas kernels: 19.9 us -> 23.1 us
    unnamed x40 -> x20, local copies, waits for them, and re-layouts: 14.9 us -> 0.7 us
    pallas_call x2, Pallas kernels: 7.9 us -> 11.2 us  [the longest x1 8.67 us: local(): call(first_kernel, [(256, 128), (32, 512)], [SM, SM, SM, VM] + [HBM] * 10...]
where the time goes in v2:
time: 93.7 us; the launch traced here: 93.2 us
  blocking collectives  54.4 us (58%)
  Pallas kernels  23.1 us (25%)
  waiting for transfers between devices  9.59 us (10%)
  starting transfers between devices  3.99 us (4%)
  between operations  1.39 us (1%)
    all_to_all x1, blocking collectives, local(): got = lax.all_to_all(sent.reshape(128, 4, 128), everyone, 0, 0, tiled=True)  23 us
    all_to_all x1, blocking collectives, local(): got = lax.all_to_all(sent.reshape(16, 32, 128), 'lat', 0, 0, tiled=True)  10.6 us
    all_to_all x1, blocking collectives, local(): got = lax.all_to_all(sent.reshape(16, 16, 128), 'lat', 0, 0, tiled=True)  10.5 us
    all_to_all x1, blocking collectives, local(): got = lax.all_to_all(sent, 'freq', 0, 0, tiled=True)  10.4 us
    all_to_all x1, waiting for transfers between devices, local(): got = lax.all_to_all(sent.reshape(128, 2, 128), everyone, 0, 0, tiled=True)  9.59 us
    pallas_call x1, Pallas kernels, local(): call(first_kernel, [(256, 128), (32, 512)], [SM, SM, SM, VM] + [HBM] * 10...  8.67 us
    pallas_call x1, Pallas kernels, local(): sent = call(solve_kernel, (256, 128), [VM], 24)(got.reshape(512, 128))  7.28 us
    all_to_all x1, starting transfers between devices, local(): got = lax.all_to_all(sent.reshape(128, 2, 128), everyone, 0, 0, tiled=True)  3.99 us
  transfers between devices with their start and end apart: 1, of which 1 were waited for; matrix products, arithmetic and copies ran while one was open for 0% of the time, Pallas kernels for 0%

profile of v2, /device:TPU:1, one launch (start us, length us, event | category | flops | bytes accessed | tf_op | source)
XLA Modules:
  0.0 93.2 jit_solution(506883671057384454)
XLA Ops:
  0.6 2.5 %shard_map.212 = f32[512,128]{1,0:T(8,128)} custom-call(s32[1,1024]{1,0:T(1,128)} %bitcast.24, s32[1,1024]{1,0:T(1,128)} %bitcast.25, f32[2,1024]{1,0:T(2,128)} %refs_2_.2, f32[1,1024]{1,0:T(1,128)} %bitcast.26, f32[16,1024]{1,0:T(8,128)} %bitcast.23), custom_call_target="tpu_custom_call" | custom-call | tf_op jit(solution)/shard_map/pallas_call | solution.py:516
  3.1 23.0 %all_to_all.25 = f32[128,4,128]{2,1,0:T(4,128)S(1)} all-to-all(f32[128,4,128]{2,1,0:T(4,128)} %bitcast.20), channel_id=1, replica_groups=mesh['freq'=8,'lat'=16] {'freq','lat'}, dimensions={0} | all-to-all | bytes 524288 | tf_op jit(solution)/shard_map/all_to_all | solution.py:536
  26.1 7.3 %shard_map.213 = f32[256,128]{1,0:T(8,128)} custom-call(f32[512,128]{1,0:T(8,128)S(1)} %bitcast.17), custom_call_target="tpu_custom_call" | custom-call | tf_op jit(solution)/shard_map/pallas_call | solution.py:537
  33.4 4.0 %all-to-all-start.1 = ((f32[128,2,128]{2,1,0:T(2,128)}), f32[128,2,128]{2,1,0:T(2,128)S(1)}, u32[]{:S(2)}, u32[]{:S(2)}) async-start(f32[128,2,128]{2,1,0:T(2,128)} %bitcast.7), calls=%async_computation.1 | async-start | bytes 262144 | tf_op jit(solution)/shard_map/all_to_all | solution.py:538
  38.1 9.6 %all-to-all-done.1 = f32[128,2,128]{2,1,0:T(2,128)S(1)} async-done(((f32[128,2,128]{2,1,0:T(2,128)}), f32[128,2,128]{2,1,0:T(2,128)S(1)}, u32[]{:S(2)}, u32[]{:S(2)}) %all-to-all-start.1) | async-done | bytes 131104 | tf_op jit(solution)/shard_map/all_to_all | solution.py:538
  47.7 0.0 copy-start.9
  47.7 0.7 copy-done.9
  48.3 0.0 copy-start.3
  48.3 0.0 copy-start.4
  48.3 0.0 copy-start.5
  48.3 0.0 copy-start.6
  48.3 0.0 copy-start.8
  48.3 8.7 %shard_map.214 = (f32[256,128]{1,0:T(8,128)}, f32[32,512]{1,0:T(8,128)}) custom-call(s32[1]{0:T(128)} %bitcast.lat_ref, f32[1]{0:T(128)S(6)} %copy.24.freq_ref, f32[2,8]{1,0:T(2,128)} %slow_ref.5, f32[256,128]{1,0:T(8,128)} %bitcast.21, bf16[128,1024]{1,0:T(8,128)(2,1)} %constant.30.clone.refs_0_, bf16[128,1024]{1,0:T(8,128)(2,1)} %constant.31.clone.refs_1_, ...), custom_call_target="tpu_custom_call" | custom-call | tf_op jit(solution)/shard_map/pallas_call | solution.py:539
  57.0 0.0 copy-start
  57.0 0.0 copy-start.1
  57.0 0.0 copy-start.2
  57.0 0.0 copy-start.7
  57.1 10.5 %all_to_all.26 = f32[16,16,128]{2,1,0:T(8,128)S(1)} all-to-all(f32[16,16,128]{2,1,0:T(8,128)} %bitcast.22), channel_id=1, replica_groups=mesh['freq'=8,'lat'=16] {'lat'}, dimensions={0} | all-to-all | bytes 262144 | tf_op jit(solution)/shard_map/all_to_all | solution.py:567
  67.5 0.0 copy-done.3
  67.5 0.0 copy-done.4
  67.5 0.0 copy-done.5
  67.5 0.0 copy-done.6
  67.5 0.0 copy-done.8
  67.5 2.1 %shard_map.215 = f32[16,2,16,128]{3,2,1,0:T(8,128)S(1)} custom-call(s32[1]{0:T(128)} %bitcast.lat_ref, f32[1]{0:T(128)S(6)} %copy.24.freq_ref, f32[2,8]{1,0:T(2,128)S(1)} %copy-done.8, f32[256,128]{1,0:T(8,128)S(1)} %bitcast.19, bf16[2,512,256]{2,1,0:T(8,128)(2,1)S(1)} %copy-done.6, bf16[2,512,256]{2,1,0:T(8,128)(2,1)S(1)} %copy-done.5, ...), custom_call_target="tpu_custom_call" | custom-call | tf_op jit(solution)/shard_map/pallas_call | solution.py:568
  69.7 10.6 %all_to_all.27 = f32[16,32,128]{2,1,0:T(8,128)S(1)} all-to-all(f32[16,32,128]{2,1,0:T(8,128)S(1)} %bitcast.18), channel_id=1, replica_groups=mesh['freq'=8,'lat'=16] {'lat'}, dimensions={0} | all-to-all | bytes 524288 | tf_op jit(solution)/shard_map/all_to_all | solution.py:576
  80.3 0.0 copy-done
  80.3 0.0 copy-done.1
  80.3 0.0 copy-done.2
  80.3 0.0 copy-done.7
  80.3 1.9 %shard_map.216 = (f32[2,32,512]{2,1,0:T(8,128)}, f32[8,32,128]{2,1,0:T(8,128)S(1)}) custom-call(f32[1]{0:T(128)S(6)} %copy.24.freq_ref, f32[2,8]{1,0:T(2,128)S(1)} %copy-done.8, f32[16,2,16,128]{3,2,1,0:T(8,128)S(1)} %bitcast.16, s32[2,32,512]{2,1,0:T(8,128)S(1)} %copy-done.2, f32[32,512]{1,0:T(8,128)S(1)} %copy-done.7, bf16[2,256,512]{2,1,0:T(8,128)(2,1)S(1)} %copy-done.1, ...), custom_call_target="tpu_custom_call" | custom-call | tf_op jit(solution)/shard_map/pallas_call | solution.py:577
  82.2 10.4 %all_to_all.28.got_ref = f32[8,32,128]{2,1,0:T(8,128)S(1)} all-to-all(f32[8,32,128]{2,1,0:T(8,128)S(1)} %get-tuple-element.9), channel_id=1, replica_groups=mesh['freq'=8,'lat'=16] {'freq'}, dimensions={0} | all-to-all | bytes 262144 | tf_op jit(solution)/shard_map/all_to_all | solution.py:590
  92.5 0.7 shard_map.217
Async XLA Ops:
  33.4 14.2 %all-to-all-start.1 = ((f32[128,2,128]{2,1,0:T(2,128)}), f32[128,2,128]{2,1,0:T(2,128)S(1)}, u32[]{:S(2)}, u32[]{:S(2)}) async-start(f32[128,2,128]{2,1,0:T(2,128)} %bitcast.7), calls=%async_computation.1 | async-start | bytes 262144 | tf_op jit(solution)/shard_map/all_to_all | solution.py:538
  47.7 0.7 copy-start.9
  48.3 19.2 %copy-start.3 = (bf16[2,512,256]{2,1,0:T(8,128)(2,1)S(1)}, bf16[2,512,256]{2,1,0:T(8,128)(2,1)}, u32[]{:S(2)}) copy-start(bf16[2,512,256]{2,1,0:T(8,128)(2,1)} %constant.42.clone.bx_l) | copy-start | bytes 1572868
  48.3 19.2 %copy-start.4 = (bf16[2,512,256]{2,1,0:T(8,128)(2,1)S(1)}, bf16[2,512,256]{2,1,0:T(8,128)(2,1)}, u32[]{:S(2)}) copy-start(bf16[2,512,256]{2,1,0:T(8,128)(2,1)} %constant.41.clone.bx_h) | copy-start | bytes 1572868
  48.3 19.2 %copy-start.5 = (bf16[2,512,256]{2,1,0:T(8,128)(2,1)S(1)}, bf16[2,512,256]{2,1,0:T(8,128)(2,1)}, u32[]{:S(2)}) copy-start(bf16[2,512,256]{2,1,0:T(8,128)(2,1)} %constant.40.clone.fx_l) | copy-start | bytes 1572868
  48.3 19.2 %copy-start.6 = (bf16[2,512,256]{2,1,0:T(8,128)(2,1)S(1)}, bf16[2,512,256]{2,1,0:T(8,128)(2,1)}, u32[]{:S(2)}) copy-start(bf16[2,512,256]{2,1,0:T(8,128)(2,1)} %constant.39.clone.fx_h) | copy-start | bytes 1572868
  48.3 19.2 %copy-start.8 = (f32[2,8]{1,0:T(2,128)S(1)}, f32[2,8]{1,0:T(2,128)}, u32[]{:S(2)}) copy-start(f32[2,8]{1,0:T(2,128)} %slow_ref.5) | copy-start | bytes 196
  57.0 23.3 %copy-start = (bf16[2,256,512]{2,1,0:T(8,128)(2,1)S(1)}, bf16[2,256,512]{2,1,0:T(8,128)(2,1)}, u32[]{:S(2)}) copy-start(bf16[2,256,512]{2,1,0:T(8,128)(2,1)} %constant.36.clone.refs_7_.by_l) | copy-start | bytes 1572868
  57.0 23.3 %copy-start.1 = (bf16[2,256,512]{2,1,0:T(8,128)(2,1)S(1)}, bf16[2,256,512]{2,1,0:T(8,128)(2,1)}, u32[]{:S(2)}) copy-start(bf16[2,256,512]{2,1,0:T(8,128)(2,1)} %constant.35.clone.refs_6_.by_h) | copy-start | bytes 1572868
  57.0 23.3 %copy-start.2 = (s32[2,32,512]{2,1,0:T(8,128)S(1)}, s32[2,32,512]{2,1,0:T(8,128)}, u32[]{:S(2)}) copy-start(s32[2,32,512]{2,1,0:T(8,128)} %vel_ref.1) | copy-start | bytes 393220
  57.0 23.3 %copy-start.7 = (f32[32,512]{1,0:T(8,128)S(1)}, f32[32,512]{1,0:T(8,128)}, u32[]{:S(2)}) copy-start(f32[32,512]{1,0:T(8,128)} %get-tuple-element.7.image_ref) | copy-start | bytes 196612

commit v3 on v2

v3 whole, which is shorter than its diff:
```python
import math

import jax
import jax.numpy as jnp
import ml_dtypes
import numpy as np
from jax import lax
from jax.experimental import pallas as pl
from jax.experimental.pallas import tpu as pltpu
from jax.sharding import PartitionSpec as P

NX = 512
NY = 512
TB = 32
MODES = 8
HALF = 256
SCALE = 1.0 / (NX * NY)
STEP = 2.0 * math.pi / 512

f32 = jnp.float32
bf16 = jnp.bfloat16
VM = pl.BlockSpec(memory_space=pltpu.VMEM)
SM = pl.BlockSpec(memory_space=pltpu.SMEM)
HBM = pl.BlockSpec(memory_space=pltpu.HBM)


def pair(table):
    table = np.asarray(table, np.float32)
    high = table.astype(ml_dtypes.bfloat16)
    low = (table - high.astype(np.float32)).astype(ml_dtypes.bfloat16)
    return np.stack([high, low])


def waves(bins):
    twice = 2 * np.asarray(bins)[None, :] + 1
    index = np.arange(HALF)[:, None]
    sine_index = np.where(index == 0, HALF, index)
    return (
        np.cos(np.pi / 512 * (index * twice % 1024)),
        np.sin(np.pi / 512 * (sine_index * twice % 1024)),
    )


def tables():
    cell = np.arange(TB)
    modes = np.cos(np.pi * np.arange(MODES)[:, None] * (cell[None, :] + 0.5) / TB)
    cosine, sine = waves(np.arange(512))
    along = [
        np.einsum("aj,iyj->yai", modes, t.reshape(HALF, 16, TB)).reshape(16 * MODES, HALF)
        for t in (cosine, sine)
    ]
    along = np.concatenate(along, 1)
    own = np.concatenate(
        [pair(t.reshape(HALF, 16, 32).transpose(1, 2, 0)) for t in (cosine, sine)], 0
    )
    own = own.transpose(1, 0, 2, 3).reshape(16, 128, HALF)
    first = [cosine[:, :HALF], sine[:, :HALF]]
    late = [cosine[:, HALF:], sine[:, HALF:]]
    waves_all = pair(np.stack([*first, *[t.T for t in first], *late]))
    return dict(along_y=pair(along), along_x=pair(along.T), own=own, waves=waves_all)


def split(value):
    high = value.astype(bf16)
    low = (value - high.astype(f32)).astype(bf16)
    return high, low


def mm(left, right):
    return jnp.dot(left, right, preferred_element_type=f32)


def dot3(left, right):
    return mm(left[0], right[0]) + (mm(left[0], right[1]) + mm(left[1], right[0]))


def lanes(shape):
    return lax.broadcasted_iota(jnp.int32, shape, len(shape) - 1)


def turned(value, shift, axis=1):
    size = value.shape[axis]
    shift = shift % size
    return value if shift == 0 else pltpu.roll(value, shift, axis)


def cos_sin(turn):
    half = 0.5 * turn
    sq = half * half
    cosine = 1.0 / 479001600
    for c in (-1.0 / 3628800, 1.0 / 40320, -1.0 / 720, 1.0 / 24, -0.5, 1.0):
        cosine = cosine * sq + c
    sine = 1.0 / 6227020800
    for c in (-1.0 / 39916800, 1.0 / 362880, -1.0 / 5040, 1.0 / 120, -1.0 / 6, 1.0):
        sine = sine * sq + c
    sine = sine * half
    return 1.0 - 2.0 * sine * sine, 2.0 * sine * cosine


def shift_factor(wave_sq, kx, ky):
    vertical = wave_sq - kx * kx - ky * ky
    root = jnp.sqrt(jnp.abs(vertical))
    cosine, sine = cos_sin(root)
    moving = vertical > 0.0
    return jnp.where(moving, cosine, jnp.exp(-root)), jnp.where(moving, sine, 0.0)


def references_of(slow_ref, step):
    values = [slow_ref[step, i] for i in range(8)]
    refs = [
        (values[4 * g] + values[4 * g + 1] + values[4 * g + 2] + values[4 * g + 3]) * 0.25
        for g in range(2)
    ]
    return values, refs


def split_turns(velocity, step, slow_ref, freq_ref):
    values, refs = references_of(slow_ref, step)
    pairs = [cos_sin(freq_ref[0] * (values[i] - refs[i // 4])) for i in range(8)]
    low, mid, top = (velocity & 1) == 1, (velocity & 2) == 2, velocity >= 4
    out = []
    for p in range(2):
        level = [pairs[i][p] * SCALE for i in range(8)]
        level = [jnp.where(low, level[2 * i + 1], level[2 * i]) for i in range(4)]
        level = [jnp.where(mid, level[2 * i + 1], level[2 * i]) for i in range(2)]
        out.append(jnp.where(top, level[1], level[0]))
    return out[0], out[1], top


def no_first(value, axis):
    at = lax.broadcasted_iota(jnp.int32, value.shape, axis)
    return jnp.where(at > 0, value, 0.0)


def plus_i(u, v):
    return u[0] - v[1], u[1] + v[0]


def minus_i(u, v):
    return u[0] + v[1], u[1] - v[0]


def halves_of(value, axis, count):
    if axis == 0:
        return value[:count], value[count:]
    return value[:, :count], value[:, count:]


class Fetch:
    def __init__(self, sources, targets, sems):
        self.targets = targets
        self.copies = [
            pltpu.make_async_copy(s, t, sems.at[i]) for i, (s, t) in enumerate(zip(sources, targets))
        ]
        for copy in self.copies:
            copy.start()

    def take(self, *which):
        for i in which:
            self.copies[i].wait()
        out = [self.targets[i] for i in which]
        return out[0] if len(out) == 1 else out


def route_kernel(lat_ref, *refs):
    sources, out_ref, vel_ref = refs[:6], refs[6], refs[7]
    targets, sems = refs[8:14], refs[14]
    fetch = Fetch([*sources[:5], sources[5].at[0]], targets, sems)
    tile = fetch.take(0)[...]
    tile_f = tile.astype(f32)
    below = lax.broadcasted_iota(jnp.int32, (128, 128), 0) < lanes((128, 128))
    columns = []
    ranks = []
    for j in range(8):
        here = tile_f[:, 128 * j : 128 * (j + 1)]
        here_all = jnp.broadcast_to(here, (128, 128))
        columns.append(here_all.T)
        found = jnp.where((columns[j] == here_all) & below, 1.0, 0.0)
        for i in range(j):
            found = found + jnp.where(columns[i] == here_all, 1.0, 0.0)
        ranks.append(jnp.sum(found, axis=0, keepdims=True))
    rank = jnp.concatenate(ranks, 1).astype(jnp.int32)
    row_at = (tile >> 1) * 4 + (rank & 3)
    group_at = (tile & 1) * 2 + (rank >> 2)
    bin_ref, offset_ref, weight_ref, spectra_ref = fetch.take(1, 2, 3, 4)
    place = bin_ref[...]
    cell_x = (place >> 5).astype(f32) + offset_ref[0:1, :]
    cell_y = (place & 31).astype(f32) + offset_ref[1:2, :]
    values = jnp.concatenate(
        [
            spectra_ref[...],
            jnp.concatenate([weight_ref[...], cell_x, cell_y, jnp.zeros((5, 1024), f32)], 0),
            jnp.zeros((8, 1024), f32),
        ],
        0,
    )
    spread = jnp.concatenate([jnp.where(group_at == s, values, 0.0) for s in range(4)], 0)
    high = spread.astype(bf16)
    rest = spread - high.astype(f32)
    mid = rest.astype(bf16)
    low = (rest - mid.astype(f32)).astype(bf16)
    wide = jnp.concatenate([high, mid, low], 0)
    rows = lax.broadcasted_iota(jnp.int32, (512, 1024), 0)
    chosen = jnp.where(rows == row_at, 1.0, 0.0).astype(bf16)
    moved = lax.dot_general(
        chosen, wide, (((1,), (1,)), ((), ())), preferred_element_type=f32
    )
    out_ref[...] = (moved[:, :128] + moved[:, 128:256]) + moved[:, 256:]
    velocity = fetch.take(5)[...].astype(f32).astype(bf16)
    at = lax.broadcasted_iota(jnp.int32, (HALF, HALF), 0)
    flip = jnp.where(at + lanes((HALF, HALF)) == HALF - 1, 1.0, 0.0).astype(bf16)
    right = mm(velocity[:, HALF:], flip).astype(bf16)
    velocity = jnp.concatenate([velocity[:, :HALF], right], 1)
    at, along = lax.broadcasted_iota(jnp.int32, (32, 32), 0), lanes((32, 32))
    target = jnp.where(lat_ref[0] >= 8, 31 - at, at)
    vel_ref[...] = mm(jnp.where(along == target, 1.0, 0.0).astype(bf16), velocity)


def solve_kernel(lat_ref, got_ref, *refs):
    slabs, out_ref, four_ref, sems = refs[:4], refs[4], refs[5], refs[6]
    fetch = Fetch(slabs, [four_ref.at[(lat_ref[0] & 3) ^ d] for d in range(4)], sems)
    turned_in = got_ref[...].T
    blocks = []
    mode = lax.broadcasted_iota(jnp.int32, (8, 1024), 0).astype(f32)
    eye_rows = lax.broadcasted_iota(jnp.int32, (64, 128), 0)
    eye = jnp.where(eye_rows == lanes((64, 128)), 1.0, 0.0)
    for t in range(2):
        both = jnp.concatenate(
            [turned_in[64 * t : 64 * t + 24], turned_in[64 * t + 32 : 64 * t + 56]], 1
        )
        along_x = jnp.cos(math.pi * mode * (both[17:18] + 0.5) / TB)
        along_y = jnp.cos(math.pi * mode * (both[18:19] + 0.5) / TB)
        basis = jnp.concatenate([along_x[a : a + 1] * along_y for a in range(8)], 0)
        wide = jnp.concatenate([basis, both[0:16], jnp.zeros((48, 1024), f32)], 0)
        system = lax.dot_general(
            basis * both[16:17],
            wide,
            (((1,), (1,)), ((), ())),
            preferred_element_type=f32,
            precision=lax.Precision.HIGHEST,
        )
        system = system + eye
        blocks.append([system[8 * a : 8 * a + 8] for a in range(8)])
    sub = lax.broadcasted_iota(jnp.int32, (8, 128), 0)
    for j in range(64):
        at, inner = j // 8, j % 8
        for t in range(2):
            mine = blocks[t]
            row = mine[at][inner : inner + 1]
            row = row / row[:, j : j + 1]
            fresh = []
            for a in range(8):
                new = mine[a] - mine[a][:, j : j + 1] * row
                if a == at:
                    new = jnp.where(sub == inner, row, new)
                fresh.append(new)
            blocks[t] = fresh
    stacked = jnp.concatenate([blocks[t][a] for a in range(8) for t in range(2)], 0)
    final = stacked.T
    odd = (lax.broadcasted_iota(jnp.int32, (32, 128), 0) & 1) == 1
    for f in range(8):
        out_ref[32 * f : 32 * f + 32] = jnp.where(
            odd, final[72 + f : 73 + f], final[64 + f : 65 + f]
        )
    fetch.take(0, 1, 2, 3)


def factor_kernel(freq_ref, slow_ref, factor_ref, edge_ref):
    at = lanes((1, HALF))
    ky = at.astype(f32) * STEP
    ky_mirror = jnp.where(at[:, :128] == 0, 256, at[:, :128]).astype(f32) * STEP
    for step in range(2):
        values, refs = references_of(slow_ref, step)
        for g in range(2):
            wave = freq_ref[0] * refs[g]
            wave_sq = wave * wave

            def rows_of(kx):
                first = shift_factor(wave_sq, kx, ky)
                mirror = shift_factor(wave_sq, kx[:, :128], ky_mirror)
                return [
                    jnp.concatenate([first[p], mirror[p], first[p][:, 128:]], 1) for p in range(2)
                ]

            def some_rows(k, carry):
                start = pl.multiple_of(k * 32, 32)
                kx = (lax.broadcasted_iota(jnp.int32, (32, HALF), 0) + start).astype(f32) * STEP
                found = rows_of(kx)
                for p in range(2):
                    factor_ref[step, g, p, pl.ds(start, 32), :] = found[p]
                return carry

            lax.fori_loop(0, 8, some_rows, 0)
            at_row = lax.broadcasted_iota(jnp.int32, (8, HALF), 0)
            found = rows_of(jnp.where(at_row == 0, 256, at_row).astype(f32) * STEP)
            for p in range(2):
                edge_ref[step, g, p] = found[p]


def store_spectrum(spec_ref, u, v, cols):
    first = minus_i(u, [no_first(t, 0) for t in v])
    second = plus_i([no_first(t, 0) for t in u], v)
    for k, value in enumerate((*first, *second)):
        spec_ref[k, :, cols] = value


def wave_pair(waves_ref, which):
    return waves_ref[0, which], waves_ref[1, which]


def own_dot(own_ref, rows_at, value):
    with_high = mm(own_ref[rows_at : rows_at + 64], value[0])
    return with_high[:32] + (with_high[32:] + mm(own_ref[rows_at : rows_at + 32], value[1]))


def invert_x(spec_ref, factor_ref, edge_ref, own_ref, own_back, g, cols):
    fac = [factor_ref[g, p, :, cols] for p in range(2)]
    fac_edge = [jnp.concatenate([edge_ref[g, p, :, cols], fac[p][8:]], 0) for p in range(2)]
    s = [spec_ref[i, :, cols] for i in range(4)]
    up = (s[0] * fac[0] - s[1] * fac[1], s[0] * fac[1] + s[1] * fac[0])
    down = (s[2] * fac_edge[0] - s[3] * fac_edge[1], s[2] * fac_edge[1] + s[3] * fac_edge[0])
    even = split(jnp.concatenate([up[p] + no_first(down[p], 0) for p in range(2)], 1))
    odd = split(jnp.concatenate([no_first(up[p], 0) - down[p] for p in range(2)], 1))
    mine = plus_i(
        halves_of(own_dot(own_ref, 0, even), 1, HALF),
        halves_of(own_dot(own_ref, 64, odd), 1, HALF),
    )
    for p in range(2):
        own_back[g, 32 * p : 32 * p + 32, cols] = mine[p]
    return even, odd


def fold_columns(value):
    left, right = value[:, :HALF], value[:, HALF:]
    return split(left + no_first(right, 1)), split(no_first(left, 1) - right)


def own_field(step, own_back, waves_ref, velocity, slow_ref, freq_ref):
    even, odd = fold_columns(jnp.concatenate([own_back[0], own_back[1]], 0))
    sides = []
    for at in (0, 4):
        u, v = dot3(even, wave_pair(waves_ref, at)), dot3(odd, wave_pair(waves_ref, at + 1))
        sides.append(
            [
                plus_i(
                    halves_of(u[64 * g : 64 * g + 64], 0, 32),
                    halves_of(v[64 * g : 64 * g + 64], 0, 32),
                )
                for g in range(2)
            ]
        )
    back = [
        [jnp.concatenate([sides[0][g][p], sides[1][g][p]], 1) for p in range(2)] for g in range(2)
    ]
    cosine, sine, top = split_turns(velocity, step, slow_ref, freq_ref)
    picked = [jnp.where(top, back[1][p], back[0][p]) for p in range(2)]
    return (
        picked[0] * cosine - picked[1] * sine,
        picked[0] * sine + picked[1] * cosine,
    )


def first_kernel(lat_ref, freq_ref, slow_ref, got_ref, *refs):
    sources, image_ref, back_hbm = refs[:7], refs[7], refs[8]
    targets, sems, out_sems = refs[9:16], refs[16], refs[17]
    spec_ref, own_back, back_ref = refs[18:]
    fetch = Fetch(
        [
            *sources[:2],
            sources[2].at[lat_ref[0]],
            sources[3].at[0],
            sources[4].at[0],
            sources[5],
            sources[6].at[0],
        ],
        targets,
        sems,
    )
    rows = lax.broadcasted_iota(jnp.int32, (128, 128), 0)
    groups = lanes((128, 128)) >> 4
    stacked = []
    for p in range(2):
        value = got_ref[pl.ds(p, 128, stride=2), :]
        for k in (1, 2, 4):
            s_bit, g_bit = (rows & k) != 0, (groups & k) != 0
            down = turned(turned(value, k, 0), -16 * k, 1)
            up = turned(turned(value, -k, 0), 16 * k, 1)
            value = jnp.where(
                s_bit & ~g_bit, down, jnp.where(~s_bit & g_bit, up, value)
            )
        stacked.append(value)
    table = fetch.take(0)
    both = dot3(split(jnp.concatenate(stacked, 0)), (table[0], table[1]))
    u, v = (halves_of(t, 0, 128) for t in (both[:, :HALF], both[:, HALF:]))
    first = minus_i(u, [no_first(t, 1) for t in v])
    second = plus_i([no_first(t, 1) for t in u], v)
    table = fetch.take(1)
    for c, here in enumerate((first, second)):
        both = dot3((table[0], table[1]), split(jnp.concatenate(here, 1)))
        store_spectrum(
            spec_ref,
            halves_of(both[:HALF], 1, HALF),
            halves_of(both[HALF:], 1, HALF),
            pl.ds(HALF * c, HALF),
        )
    own_ref, factor_ref, edge_ref, waves_ref = fetch.take(2, 3, 4, 5)
    leaving = []
    for g in range(2):
        for c in range(2):
            cols = pl.ds(HALF * c, HALF)
            even, odd = invert_x(spec_ref, factor_ref, edge_ref, own_ref, own_back, g, cols)
            u = halves_of(dot3(wave_pair(waves_ref, 2), even), 1, HALF)
            v = halves_of(dot3(wave_pair(waves_ref, 3), odd), 1, HALF)
            first, second = plus_i(u, v), minus_i(u, v)
            for p in range(2):
                back_ref[g, p, :HALF, cols] = first[p]
                back_ref[g, p, HALF:, cols] = second[p]
            copy = pltpu.make_async_copy(
                back_ref.at[g, :, :, cols], back_hbm.at[g, :, :, cols], out_sems.at[2 * g + c]
            )
            copy.start()
            leaving.append(copy)
    vel_ref = fetch.take(6)
    image_ref[...] = own_field(0, own_back, waves_ref, vel_ref[...], slow_ref, freq_ref)[0]
    for copy in leaving:
        copy.wait()


def second_kernel(lat_ref, freq_ref, slow_ref, image_ref, *refs):
    slabs, refs = refs[:4], refs[4:]
    sources, wave_ref, out_ref = refs[:6], refs[6], refs[7]
    targets, slabs_ref, sems, back_sems = refs[8:13], refs[13], refs[14], refs[15]
    back_ref, spec_ref, own_back, half_ref = refs[16:]

    def arriving(k):
        at = pl.ds(pl.multiple_of(k * 128, 128), 128)
        return pltpu.make_async_copy(
            sources[0].at[:, :, at, :], back_ref.at[:, :, at, :], back_sems.at[k]
        )

    arriving(0).start()
    fetch = Fetch(
        [
            sources[1],
            *slabs,
            sources[2].at[1],
            sources[3].at[1],
            sources[4].at[lat_ref[0]],
            sources[5].at[1],
        ],
        [targets[0], *[slabs_ref.at[(lat_ref[0] >> 2) ^ d] for d in range(4)], *targets[1:]],
        sems,
    )
    for k in range(1, 4):
        arriving(k).start()
    waves_ref = fetch.take(*range(5))[0]

    def some_rows(k, carry):
        arriving(k).wait()
        at = pl.ds(pl.multiple_of(k * 128, 128), 128)
        back = []
        for g in range(2):
            even, odd = fold_columns(
                jnp.concatenate([back_ref[g, p, at, :] for p in range(2)], 0)
            )
            u = halves_of(dot3(even, wave_pair(waves_ref, 0)), 0, 128)
            v = halves_of(dot3(odd, wave_pair(waves_ref, 1)), 0, 128)
            back.append((plus_i(u, v), minus_i(u, v)))
        slabs = [
            slabs_ref[jnp.where(k < 2, k, 5 - k), jnp.where(k < 2, i, 3 - i)] for i in range(4)
        ]
        velocity = jnp.concatenate(slabs, 0).astype(jnp.int32)
        fields = []
        for side in range(2):
            cosine, sine, top = split_turns(
                velocity[:, HALF * side : HALF * side + HALF], 0, slow_ref, freq_ref
            )
            picked = [jnp.where(top, back[1][side][p], back[0][side][p]) for p in range(2)]
            fields.append(
                jnp.concatenate(
                    [
                        picked[0] * cosine - picked[1] * sine,
                        picked[0] * sine + picked[1] * cosine,
                    ],
                    0,
                )
            )
        u = halves_of(dot3(split(fields[0] + fields[1]), wave_pair(waves_ref, 2)), 0, 128)
        v = halves_of(dot3(split(fields[0] - fields[1]), wave_pair(waves_ref, 3)), 0, 128)
        first = minus_i(u, [no_first(t, 1) for t in v])
        second = plus_i([no_first(t, 1) for t in u], v)
        for p in range(2):
            half_ref[p, at, :HALF] = first[p]
            half_ref[p, at, HALF:] = second[p]
        return carry

    lax.fori_loop(0, 4, some_rows, 0)

    def some_columns(c, carry):
        cols = pl.ds(pl.multiple_of(c * HALF, HALF), HALF)
        top = jnp.concatenate([half_ref[p, :HALF, cols] for p in range(2)], 1)
        low = jnp.concatenate([half_ref[p, HALF:, cols] for p in range(2)], 1)
        u = halves_of(dot3(wave_pair(waves_ref, 0), split(top + low)), 1, HALF)
        v = halves_of(dot3(wave_pair(waves_ref, 1), split(top - low)), 1, HALF)
        store_spectrum(spec_ref, u, v, cols)
        return carry

    lax.fori_loop(0, 2, some_columns, 0)
    factor_ref, edge_ref, own_ref, vel_ref = fetch.take(5, 6, 7, 8)

    def invert(k, carry):
        cols = pl.ds(pl.multiple_of((k & 1) * HALF, HALF), HALF)
        invert_x(spec_ref, factor_ref, edge_ref, own_ref, own_back, k >> 1, cols)
        return carry

    lax.fori_loop(0, 4, invert, 0)
    field = own_field(1, own_back, waves_ref, vel_ref[...], slow_ref, freq_ref)
    for p in range(2):
        wave_ref[p] = field[p]
    upper = lanes((32, 128)) >= 64
    image = image_ref[...]
    for d in range(8):
        col, pos = d // 2, d % 2
        first = turned(image[:, 128 * col : 128 * col + 128], -64 * pos)
        second = turned(field[0][:, 128 * col : 128 * col + 128], 64 - 64 * pos)
        out_ref[d] = jnp.where(upper, second, first)


def sum_kernel(got_ref, out_ref):
    total = got_ref[0]
    for d in range(1, 8):
        total = total + got_ref[d]
    out_ref[0] = total[:, :64]
    out_ref[1] = total[:, 64:]


def call(kernel, outs, in_specs, mega, scratch=(), out_specs=None):
    many = isinstance(outs, list)
    shapes = [jax.ShapeDtypeStruct(s, f32) for s in (outs if many else [outs])]
    return pl.pallas_call(
        kernel,
        out_shape=shapes if many else shapes[0],
        in_specs=in_specs,
        out_specs=out_specs or ([VM] * len(shapes) if many else VM),
        scratch_shapes=list(scratch),
        compiler_params=pltpu.CompilerParams(vmem_limit_bytes=mega * 1024 * 1024),
    )


def local(spectra, tile_route, bin_in_tile, trace_offset, weights, frequency, slowness, vel_index):
    const = tables()
    lat_at = lax.axis_index("lat").astype(jnp.int32).reshape(1)
    everyone = ("freq", "lat")
    sent, velocity = call(
        route_kernel,
        [(512, 128), (32, 512)],
        [SM] + [HBM] * 6,
        60,
        [
            pltpu.VMEM((1, 1024), jnp.int32),
            pltpu.VMEM((1, 1024), jnp.int32),
            pltpu.VMEM((2, 1024), f32),
            pltpu.VMEM((1, 1024), f32),
            pltpu.VMEM((16, 1024), f32),
            pltpu.VMEM((32, 512), jnp.int32),
            pltpu.SemaphoreType.DMA((6,)),
        ],
    )(
        lat_at,
        tile_route.reshape(1, 1024),
        bin_in_tile.reshape(1, 1024),
        trace_offset,
        weights.reshape(1, 1024),
        spectra.reshape(16, 1024),
        vel_index,
    )
    got = lax.all_to_all(sent.reshape(128, 4, 128), everyone, 0, 0, tiled=True)
    slabs = [velocity] + [
        lax.ppermute(velocity, "lat", [(i, i ^ d) for i in range(16)]) for d in (1, 2, 3)
    ]
    sent, slabs = call(
        solve_kernel,
        [(256, 128), (4, 32, 512)],
        [SM, VM] + [HBM] * 4,
        24,
        [pltpu.SemaphoreType.DMA((4,))],
        [VM, HBM],
    )(lat_at, got.reshape(512, 128), *slabs)
    got = lax.all_to_all(sent.reshape(128, 2, 128), everyone, 0, 0, tiled=True)
    slabs = [slabs] + [
        lax.ppermute(slabs, "lat", [(i, i ^ d) for i in range(16)]) for d in (4, 8, 12)
    ]
    factor, edge = call(
        factor_kernel, [(2, 2, 2, 256, 512), (2, 2, 2, 8, 512)], [SM, SM], 59
    )(frequency, slowness)
    image, back = call(
        first_kernel,
        [(32, 512), (2, 2, 512, 512)],
        [SM, SM, SM, VM] + [HBM] * 7,
        59,
        [
            pltpu.VMEM((2, 128, 512), bf16),
            pltpu.VMEM((2, 512, 128), bf16),
            pltpu.VMEM((128, 256), bf16),
            pltpu.VMEM((2, 2, 256, 512), f32),
            pltpu.VMEM((2, 2, 8, 512), f32),
            pltpu.VMEM((2, 6, 256, 256), bf16),
            pltpu.VMEM((32, 512), jnp.int32),
            pltpu.SemaphoreType.DMA((7,)),
            pltpu.SemaphoreType.DMA((4,)),
            pltpu.VMEM((4, 256, 512), f32),
            pltpu.VMEM((2, 64, 512), f32),
            pltpu.VMEM((2, 2, 512, 512), f32),
        ],
        [VM, HBM],
    )(
        lat_at,
        frequency,
        slowness,
        got.reshape(256, 128),
        const["along_y"],
        const["along_x"],
        const["own"],
        factor,
        edge,
        const["waves"],
        vel_index,
    )
    wave, sent = call(
        second_kernel,
        [(2, 32, 512), (8, 32, 128)],
        [SM, SM, SM, VM] + [HBM] * 10,
        59,
        [
            pltpu.VMEM((2, 6, 256, 256), bf16),
            pltpu.VMEM((2, 2, 256, 512), f32),
            pltpu.VMEM((2, 2, 8, 512), f32),
            pltpu.VMEM((128, 256), bf16),
            pltpu.VMEM((32, 512), jnp.int32),
            pltpu.VMEM((4, 4, 32, 512), f32),
            pltpu.SemaphoreType.DMA((9,)),
            pltpu.SemaphoreType.DMA((4,)),
            pltpu.VMEM((2, 2, 512, 512), f32),
            pltpu.VMEM((4, 256, 512), f32),
            pltpu.VMEM((2, 64, 512), f32),
            pltpu.VMEM((2, 512, 512), f32),
        ],
    )(
        lat_at,
        frequency,
        slowness,
        image,
        *slabs,
        back,
        const["waves"],
        factor,
        edge,
        const["own"],
        vel_index,
    )
    got = lax.all_to_all(sent, "freq", 0, 0, tiled=True)
    depth_image = call(sum_kernel, (2, 32, 64), [VM], 16)(got)
    return (wave.reshape(2, 1, 32, 512), depth_image)


def solution(mesh):
    return jax.shard_map(
        local,
        mesh=mesh,
        in_specs=(
            P(None, None, ("freq", "lat")),
            P(("freq", "lat"), None),
            P(("freq", "lat")),
            P(None, ("freq", "lat")),
            P(("freq", "lat")),
            P("freq"),
            P(),
            P(None, "lat", None),
        ),
        out_specs=(P(None, "freq", "lat", None), P(None, "lat", "freq")),
        check_vma=False,
    )
```

time: 93.7 us -> 87.2 us (0.931)
  blocking collectives: 54.4 us -> 9 us
  starting transfers between devices: 3.99 us -> 25.2 us
  Pallas kernels: 23.1 us -> 36.8 us
  waiting for transfers between devices: 9.59 us -> 12 us
  local copies, waits for them, and re-layouts: 0.7 us -> 2.38 us
    all_to_all x3 -> x0, blocking collectives: 44.1 us -> none  [the longest x1 23 us: local(): got = lax.all_to_all(sent.reshape(128, 4, 128), everyone, 0, 0, tiled=True)]
    pallas_call x6, Pallas kernels: 23.1 us -> 36.8 us  [the longest x1 11.9 us: local(): call(second_kernel, [(2, 32, 512), (8, 32, 128)], [SM, SM, SM, VM] + [HBM...]
    all_to_all x0 -> x1, starting transfers between devices: none -> 11.5 us  [local(): got = lax.all_to_all(sent.reshape(128, 4, 128), everyone, 0, 0, tiled=True)]
    ppermute x0 -> x6, starting transfers between devices: none -> 6.68 us  [the longest x3 3.35 us: local(): lax.ppermute(velocity, 'lat', [(i, i ^ d) for i in range(16)])]
    all_to_all x1, waiting for transfers between devices: 9.59 us -> 3.91 us  [local(): got = lax.all_to_all(sent.reshape(128, 2, 128), everyone, 0, 0, tiled=True)]
    ppermute x0 -> x6, waiting for transfers between devices: none -> 4.47 us  [the longest x3 4.46 us: local(): lax.ppermute(velocity, 'lat', [(i, i ^ d) for i in range(16)])]
    all_to_all x0 -> x1, waiting for transfers between devices: none -> 3.66 us  [local(): got = lax.all_to_all(sent.reshape(128, 4, 128), everyone, 0, 0, tiled=True)]
    all_to_all x1, starting transfers between devices: 3.99 us -> 6.98 us  [local(): got = lax.all_to_all(sent.reshape(128, 2, 128), everyone, 0, 0, tiled=True)]
  transfers between devices with their start and end apart: 1 -> 8, of which waited for: 1 -> 4; matrix products, arithmetic and copies ran while one was open for 0% -> 0% of each run, Pallas kernels for 0% -> 16%
where the time goes in v3:
time: 87.2 us; the launch traced here: 86.7 us
  Pallas kernels  36.8 us (42%)
  starting transfers between devices  25.2 us (29%)
  waiting for transfers between devices  12 us (14%)
  blocking collectives  9 us (10%)
  local copies, waits for them, and re-layouts  2.38 us (3%)
  between operations  1.4 us (2%)
    pallas_call x1, Pallas kernels, local(): call(second_kernel, [(2, 32, 512), (8, 32, 128)], [SM, SM, SM, VM] + [HBM...  11.9 us
    all_to_all x1, starting transfers between devices, local(): got = lax.all_to_all(sent.reshape(128, 4, 128), everyone, 0, 0, tiled=True)  11.5 us
    all_to_all x1, blocking collectives, local(): got = lax.all_to_all(sent, 'freq', 0, 0, tiled=True)  9 us
    pallas_call x1, Pallas kernels, local(): call(first_kernel, [(32, 512), (2, 2, 512, 512)], [SM, SM, SM, VM] + [HBM...  8.12 us
    pallas_call x1, Pallas kernels, local(): call(solve_kernel, [(256, 128), (4, 32, 512)], [SM, VM] + [HBM] * 4, 24,...  7.63 us
    all_to_all x1, starting transfers between devices, local(): got = lax.all_to_all(sent.reshape(128, 2, 128), everyone, 0, 0, tiled=True)  6.98 us
    pallas_call x1, Pallas kernels, local(): call(factor_kernel, [(2, 2, 2, 256, 512), (2, 2, 2, 8, 512)], [SM, SM], 59)  5.65 us
    ppermute x3, waiting for transfers between devices, local(): lax.ppermute(velocity, 'lat', [(i, i ^ d) for i in range(16)])  4.46 us
  transfers between devices with their start and end apart: 8, of which 4 were waited for; matrix products, arithmetic and copies ran while one was open for 0% of the time, Pallas kernels for 16%

profile of v3, /device:TPU:1, one launch (start us, length us, event | category | flops | bytes accessed | tf_op | source)
XLA Modules:
  0.0 86.7 jit_solution(1702123385473717301)
XLA Ops:
  0.6 2.7 %shard_map.131 = (f32[512,128]{1,0:T(8,128)}, f32[32,512]{1,0:T(8,128)}) custom-call(s32[1]{0:T(128)} %bitcast.lat_ref, s32[1,1024]{1,0:T(1,128)} %bitcast.16, s32[1,1024]{1,0:T(1,128)} %bitcast.17, f32[2,1024]{1,0:T(2,128)} %refs_2_.2, f32[1,1024]{1,0:T(1,128)} %bitcast.18, f32[16,1024]{1,0:T(8,128)} %bitcast.15, s32[2,32,512]{2,1,0:T(8,128)} %refs_9_.1), custom_call_target="tpu_custom_call" | custom-call | tf_op jit(solution)/shard_map/pallas_call | solution.py:554
  3.4 11.5 %all-to-all-start = ((f32[128,4,128]{2,1,0:T(4,128)}), f32[128,4,128]{2,1,0:T(4,128)S(1)}, u32[]{:S(2)}, u32[]{:S(2)}) async-start(f32[128,4,128]{2,1,0:T(4,128)} %bitcast.14), calls=%async_computation | async-start | bytes 524288 | tf_op jit(solution)/shard_map/all_to_all | solution.py:577
  14.9 2.7 %collective-permute-start.2 = (f32[32,512]{1,0:T(8,128)}, f32[32,512]{1,0:T(8,128)S(1)}, u32[]{:S(2)}, u32[]{:S(2)}) collective-permute-start(f32[32,512]{1,0:T(8,128)} %get-tuple-element.13.refs_0_), channel_id=1, source_target_pairs={{0,3},{1,2},{2,1},{3,0},{4,7},{5,6},{6,5},{7,4},{8,11},{9,10},{10,... | collective-permute-start | bytes 196616 | tf_op jit(solution)/shard_map/ppermute | solution.py:579
  17.6 0.6 collective-permute-start.1
  18.1 0.1 collective-permute-start
  18.2 3.6 %collective-permute-done.2.refs_3_ = f32[32,512]{1,0:T(8,128)S(1)} collective-permute-done((f32[32,512]{1,0:T(8,128)}, f32[32,512]{1,0:T(8,128)S(1)}, u32[]{:S(2)}, u32[]{:S(2)}) %collective-permute-start.2) | collective-permute-done | bytes 65568 | tf_op jit(solution)/shard_map/ppermute | solution.py:579
  21.9 0.8 collective-permute-done.1.refs_2_
  22.7 0.0 collective-permute-done.refs_1_
  22.7 3.7 %all-to-all-done = f32[128,4,128]{2,1,0:T(4,128)S(1)} async-done(((f32[128,4,128]{2,1,0:T(4,128)}), f32[128,4,128]{2,1,0:T(4,128)S(1)}, u32[]{:S(2)}, u32[]{:S(2)}) %all-to-all-start) | async-done | bytes 262176 | tf_op jit(solution)/shard_map/all_to_all | solution.py:577
  26.4 0.8 copy-done.1
  27.2 7.6 %shard_map.132 = (f32[256,128]{1,0:T(8,128)}, f32[4,32,512]{2,1,0:T(8,128)S(1)}) custom-call(s32[1]{0:T(128)} %bitcast.lat_ref, f32[512,128]{1,0:T(8,128)S(1)} %bitcast.12, f32[32,512]{1,0:T(8,128)S(1)} %copy-done.1, f32[32,512]{1,0:T(8,128)S(1)} %collective-permute-done.refs_1_, f32[32,512]{1,0:T(8,128)S(1)} %collective-permute-done.1.refs_2_, ...), custom_call_target="tpu_custom_call" | custom-call | tf_op jit(solution)/shard_map/pallas_call | solution.py:581
  34.8 0.0 copy-start
  34.8 0.4 collective-permute-start.5
  35.2 1.3 %collective-permute-start.4 = (f32[4,32,512]{2,1,0:T(8,128)S(1)}, f32[4,32,512]{2,1,0:T(8,128)S(1)}, u32[]{:S(2)}, u32[]{:S(2)}) collective-permute-start(f32[4,32,512]{2,1,0:T(8,128)S(1)} %get-tuple-element.18.refs_0_), channel_id=1, source_target_pairs={{0,8},{1,9},{2,10},{3,11},{4,12},{5,13},{6,14},{7,15},{8,0},{9,1},... | collective-permute-start | bytes 786440 | tf_op jit(solution)/shard_map/ppermute | solution.py:591
  36.5 1.7 %collective-permute-start.3 = (f32[4,32,512]{2,1,0:T(8,128)S(1)}, f32[4,32,512]{2,1,0:T(8,128)S(1)}, u32[]{:S(2)}, u32[]{:S(2)}) collective-permute-start(f32[4,32,512]{2,1,0:T(8,128)S(1)} %get-tuple-element.18.refs_0_), channel_id=1, source_target_pairs={{0,4},{1,5},{2,6},{3,7},{4,0},{5,1},{6,2},{7,3},{8,12},{9,13},{10,... | collective-permute-start | bytes 786440 | tf_op jit(solution)/shard_map/ppermute | solution.py:591
  38.2 7.0 %all-to-all-start.1 = ((f32[128,2,128]{2,1,0:T(2,128)}), f32[128,2,128]{2,1,0:T(2,128)S(1)}, u32[]{:S(2)}, u32[]{:S(2)}) async-start(f32[128,2,128]{2,1,0:T(2,128)} %bitcast.7), calls=%async_computation.1 | async-start | bytes 262144 | tf_op jit(solution)/shard_map/all_to_all | solution.py:589
  45.8 5.6 %shard_map.133 = (f32[2,2,2,256,512]{4,3,2,1,0:T(8,128)}, f32[2,2,2,8,512]{4,3,2,1,0:T(8,128)}) custom-call(f32[1]{0:T(128)S(6)} %copy.15.freq_ref, f32[2,8]{1,0:T(2,128)} %slow_ref.5), custom_call_target="tpu_custom_call" | custom-call | tf_op jit(solution)/shard_map/pallas_call | solution.py:593
  51.5 3.9 %all-to-all-done.1 = f32[128,2,128]{2,1,0:T(2,128)S(1)} async-done(((f32[128,2,128]{2,1,0:T(2,128)}), f32[128,2,128]{2,1,0:T(2,128)S(1)}, u32[]{:S(2)}, u32[]{:S(2)}) %all-to-all-start.1) | async-done | bytes 131104 | tf_op jit(solution)/shard_map/all_to_all | solution.py:589
  55.4 0.7 copy-done.2
  56.0 8.1 %shard_map.134 = (f32[32,512]{1,0:T(8,128)}, f32[2,2,512,512]{3,2,1,0:T(8,128)}) custom-call(s32[1]{0:T(128)} %bitcast.lat_ref, f32[1]{0:T(128)S(6)} %copy.15.freq_ref, f32[2,8]{1,0:T(2,128)} %slow_ref.5, f32[256,128]{1,0:T(8,128)} %bitcast.13, bf16[2,128,512]{2,1,0:T(8,128)(2,1)} %constant.12.clone.refs_0_, bf16[2,512,128]{2,1,0:T(8,128)(2,1)} %constant.13.clone.refs_1_, ...), custom_call_target="tpu_custom_call" | custom-call | tf_op jit(solution)/shard_map/pallas_call | solution.py:596
  64.1 0.0 collective-permute-done.5.refs_3_
  64.2 0.0 copy-start.3
  64.2 0.0 collective-permute-done.4.refs_2_
  64.2 0.0 copy-start.4
  64.2 0.0 collective-permute-done.3.refs_1_
  64.2 0.0 copy-start.5
  64.2 0.6 copy-done.3
  64.9 0.1 copy-done.4
  65.0 0.1 copy-done.5
  65.1 11.9 %shard_map.135 = (f32[2,32,512]{2,1,0:T(8,128)}, f32[8,32,128]{2,1,0:T(8,128)}) custom-call(s32[1]{0:T(128)} %bitcast.lat_ref, f32[1]{0:T(128)S(6)} %copy.15.freq_ref, f32[2,8]{1,0:T(2,128)} %slow_ref.5, f32[32,512]{1,0:T(8,128)} %get-tuple-element.17.image_ref, f32[4,32,512]{2,1,0:T(8,128)} %copy-done, f32[4,32,512]{2,1,0:T(8,128)} %copy-done.5, ...), custom_call_target="tpu_custom_call" | custom-call | tf_op jit(solution)/shard_map/pallas_call | solution.py:629
  77.0 9.0 %all_to_all.15.got_ref = f32[8,32,128]{2,1,0:T(8,128)S(1)} all-to-all(f32[8,32,128]{2,1,0:T(8,128)} %get-tuple-element.21), channel_id=1, replica_groups=mesh['freq'=8,'lat'=16] {'freq'}, dimensions={0} | all-to-all | bytes 262144 | tf_op jit(solution)/shard_map/all_to_all | solution.py:661
  86.0 0.7 shard_map.136
  (3 shorter events, 0.0 us)
Async XLA Ops:
  3.4 23.0 %all-to-all-start = ((f32[128,4,128]{2,1,0:T(4,128)}), f32[128,4,128]{2,1,0:T(4,128)S(1)}, u32[]{:S(2)}, u32[]{:S(2)}) async-start(f32[128,4,128]{2,1,0:T(4,128)} %bitcast.14), calls=%async_computation | async-start | bytes 524288 | tf_op jit(solution)/shard_map/all_to_all | solution.py:577
  14.9 7.0 %collective-permute-start.2 = (f32[32,512]{1,0:T(8,128)}, f32[32,512]{1,0:T(8,128)S(1)}, u32[]{:S(2)}, u32[]{:S(2)}) collective-permute-start(f32[32,512]{1,0:T(8,128)} %get-tuple-element.13.refs_0_), channel_id=1, source_target_pairs={{0,3},{1,2},{2,1},{3,0},{4,7},{5,6},{6,5},{7,4},{8,11},{9,10},{10,... | collective-permute-start | bytes 196616 | tf_op jit(solution)/shard_map/ppermute | solution.py:579
  17.6 5.1 %collective-permute-start.1 = (f32[32,512]{1,0:T(8,128)}, f32[32,512]{1,0:T(8,128)S(1)}, u32[]{:S(2)}, u32[]{:S(2)}) collective-permute-start(f32[32,512]{1,0:T(8,128)} %get-tuple-element.13.refs_0_), channel_id=1, source_target_pairs={{0,2},{1,3},{2,0},{3,1},{4,6},{5,7},{6,4},{7,5},{8,10},{9,11},{10,... | collective-permute-start | bytes 196616 | tf_op jit(solution)/shard_map/ppermute | solution.py:579
  18.1 4.6 %collective-permute-start = (f32[32,512]{1,0:T(8,128)}, f32[32,512]{1,0:T(8,128)S(1)}, u32[]{:S(2)}, u32[]{:S(2)}) collective-permute-start(f32[32,512]{1,0:T(8,128)} %get-tuple-element.13.refs_0_), channel_id=1, source_target_pairs={{0,1},{1,0},{2,3},{3,2},{4,5},{5,4},{6,7},{7,6},{8,9},{9,8},{10,11... | collective-permute-start | bytes 196616 | tf_op jit(solution)/shard_map/ppermute | solution.py:579
  26.4 0.8 copy-start.1
  34.8 29.4 %copy-start = (f32[4,32,512]{2,1,0:T(8,128)}, f32[4,32,512]{2,1,0:T(8,128)S(1)}, u32[]{:S(2)}) copy-start(f32[4,32,512]{2,1,0:T(8,128)S(1)} %get-tuple-element.18.refs_0_) | copy-start | bytes 786436
  34.8 29.3 %collective-permute-start.5 = (f32[4,32,512]{2,1,0:T(8,128)S(1)}, f32[4,32,512]{2,1,0:T(8,128)S(1)}, u32[]{:S(2)}, u32[]{:S(2)}) collective-permute-start(f32[4,32,512]{2,1,0:T(8,128)S(1)} %get-tuple-element.18.refs_0_), channel_id=1, source_target_pairs={{0,12},{1,13},{2,14},{3,15},{4,8},{5,9},{6,10},{7,11},{8,4},{9,5},... | collective-permute-start | bytes 786440 | tf_op jit(solution)/shard_map/ppermute | solution.py:591
  35.2 28.9 %collective-permute-start.4 = (f32[4,32,512]{2,1,0:T(8,128)S(1)}, f32[4,32,512]{2,1,0:T(8,128)S(1)}, u32[]{:S(2)}, u32[]{:S(2)}) collective-permute-start(f32[4,32,512]{2,1,0:T(8,128)S(1)} %get-tuple-element.18.refs_0_), channel_id=1, source_target_pairs={{0,8},{1,9},{2,10},{3,11},{4,12},{5,13},{6,14},{7,15},{8,0},{9,1},... | collective-permute-start | bytes 786440 | tf_op jit(solution)/shard_map/ppermute | solution.py:591
  36.5 27.7 %collective-permute-start.3 = (f32[4,32,512]{2,1,0:T(8,128)S(1)}, f32[4,32,512]{2,1,0:T(8,128)S(1)}, u32[]{:S(2)}, u32[]{:S(2)}) collective-permute-start(f32[4,32,512]{2,1,0:T(8,128)S(1)} %get-tuple-element.18.refs_0_), channel_id=1, source_target_pairs={{0,4},{1,5},{2,6},{3,7},{4,0},{5,1},{6,2},{7,3},{8,12},{9,13},{10,... | collective-permute-start | bytes 786440 | tf_op jit(solution)/shard_map/ppermute | solution.py:591
  38.2 17.2 %all-to-all-start.1 = ((f32[128,2,128]{2,1,0:T(2,128)}), f32[128,2,128]{2,1,0:T(2,128)S(1)}, u32[]{:S(2)}, u32[]{:S(2)}) async-start(f32[128,2,128]{2,1,0:T(2,128)} %bitcast.7), calls=%async_computation.1 | async-start | bytes 262144 | tf_op jit(solution)/shard_map/all_to_all | solution.py:589
  55.4 0.7 copy-start.2
  64.2 0.7 copy-start.3
  64.2 0.8 copy-start.4
  64.2 0.9 %copy-start.5 = (f32[4,32,512]{2,1,0:T(8,128)}, f32[4,32,512]{2,1,0:T(8,128)S(1)}, u32[]{:S(2)}) copy-start(f32[4,32,512]{2,1,0:T(8,128)S(1)} %collective-permute-done.3.refs_1_) | copy-start | bytes 786436

commit v4 on v3

--- a/solution.py
+++ b/solution.py
@@ -71,7 +71,10 @@
 
 
 def dot3(left, right):
-    return mm(left[0], right[0]) + (mm(left[0], right[1]) + mm(left[1], right[0]))
+    return mm(
+        jnp.concatenate([left[0], left[1], left[0]], 1),
+        jnp.concatenate([right[0], right[0], right[1]], 0),
+    )
 
 
 def lanes(shape):
@@ -216,6 +219,49 @@
     vel_ref[...] = mm(jnp.where(along == target, 1.0, 0.0).astype(bf16), velocity)
 
 
+def mode_cosines(mode, place):
+    turns = mode * place * (1.0 / 64)
+    half = (turns - jnp.round(turns)) * math.pi
+    sq = half * half
+    sine = 1.0 / 6227020800
+    for c in (-1.0 / 39916800, 1.0 / 362880, -1.0 / 5040, 1.0 / 120, -1.0 / 6, 1.0):
+        sine = sine * sq + c
+    sine = sine * half
+    return 1.0 - 2.0 * sine * sine
+
+
+def factor_rows(wave_sq, kx, ky, ky_mirror):
+    first = shift_factor(wave_sq, kx, ky)
+    mirror = shift_factor(wave_sq, kx[:, :128], ky_mirror)
+    return [jnp.concatenate([first[p], mirror[p], first[p][:, 128:]], 1) for p in range(2)]
+
+
+def factor_kernel(freq_ref, slow_ref, factor_ref, edge_ref):
+    at = lanes((1, HALF))
+    ky = at.astype(f32) * STEP
+    ky_mirror = jnp.where(at[:, :128] == 0, 256, at[:, :128]).astype(f32) * STEP
+    for step in range(2):
+        values, refs = references_of(slow_ref, step)
+        for g in range(2):
+            wave = freq_ref[0] * refs[g]
+            wave_sq = wave * wave
+
+            def some_rows(k, carry):
+                start = pl.multiple_of(k * 32, 32)
+                row = lax.broadcasted_iota(jnp.int32, (32, HALF), 0) + start
+                found = factor_rows(wave_sq, row.astype(f32) * STEP, ky, ky_mirror)
+                for p in range(2):
+                    factor_ref[step, g, p, pl.ds(start, 32), :] = found[p]
+                return carry
+
+            lax.fori_loop(0, 8, some_rows, 0)
+            row = lax.broadcasted_iota(jnp.int32, (8, HALF), 0)
+            row = jnp.where(row == 0, 256, row)
+            found = factor_rows(wave_sq, row.astype(f32) * STEP, ky, ky_mirror)
+            for p in range(2):
+                edge_ref[step, g, p] = found[p]
+
+
 def solve_kernel(lat_ref, got_ref, *refs):
     slabs, out_ref, four_ref, sems = refs[:4], refs[4], refs[5], refs[6]
     fetch = Fetch(slabs, [four_ref.at[(lat_ref[0] & 3) ^ d] for d in range(4)], sems)
@@ -228,8 +274,8 @@
         both = jnp.concatenate(
             [turned_in[64 * t : 64 * t + 24], turned_in[64 * t + 32 : 64 * t + 56]], 1
         )
-        along_x = jnp.cos(math.pi * mode * (both[17:18] + 0.5) / TB)
-        along_y = jnp.cos(math.pi * mode * (both[18:19] + 0.5) / TB)
+        along_x = mode_cosines(mode, both[17:18] + 0.5)
+        along_y = mode_cosines(mode, both[18:19] + 0.5)
         basis = jnp.concatenate([along_x[a : a + 1] * along_y for a in range(8)], 0)
         wide = jnp.concatenate([basis, both[0:16], jnp.zeros((48, 1024), f32)], 0)
         system = lax.dot_general(
@@ -242,19 +288,39 @@
         system = system + eye
         blocks.append([system[8 * a : 8 * a + 8] for a in range(8)])
     sub = lax.broadcasted_iota(jnp.int32, (8, 128), 0)
-    for j in range(64):
-        at, inner = j // 8, j % 8
-        for t in range(2):
-            mine = blocks[t]
-            row = mine[at][inner : inner + 1]
-            row = row / row[:, j : j + 1]
-            fresh = []
-            for a in range(8):
-                new = mine[a] - mine[a][:, j : j + 1] * row
-                if a == at:
-                    new = jnp.where(sub == inner, row, new)
-                fresh.append(new)
-            blocks[t] = fresh
+    for at in range(8):
+        for inner in range(0, 8, 4):
+            picked = [(8 * at + inner + i, inner + i) for i in range(4)]
+            for t in range(2):
+                mine = blocks[t]
+                rows = [
+                    jnp.broadcast_to(mine[at][s : s + 1], (8, 128)) for _, s in picked
+                ]
+                small = [
+                    [jnp.broadcast_to(row[:, j : j + 1], (8, 128)) for j, _ in picked]
+                    for row in rows
+                ]
+                count = len(picked)
+                for p in range(count):
+                    scale = 1.0 / small[p][p]
+                    rows[p] = rows[p] * scale
+                    small[p] = [v * scale for v in small[p]]
+                    for i in range(count):
+                        if i != p:
+                            by = small[i][p]
+                            rows[i] = rows[i] - by * rows[p]
+                            small[i] = [
+                                v - by * w if k > p else v
+                                for k, (v, w) in enumerate(zip(small[i], small[p]))
+                            ]
+                for k in range(0, 8):
+                    new = mine[k]
+                    for row, (j, s) in zip(rows, picked):
+                        new = new - mine[k][:, j : j + 1] * row
+                    if k == at:
+                        for row, (j, s) in zip(rows, picked):
+                            new = jnp.where(sub == s, row, new)
+                    mine[k] = new
     stacked = jnp.concatenate([blocks[t][a] for a in range(8) for t in range(2)], 0)
     final = stacked.T
     odd = (lax.broadcasted_iota(jnp.int32, (32, 128), 0) & 1) == 1
@@ -263,38 +329,6 @@
             odd, final[72 + f : 73 + f], final[64 + f : 65 + f]
         )
     fetch.take(0, 1, 2, 3)
-
-
-def factor_kernel(freq_ref, slow_ref, factor_ref, edge_ref):
-    at = lanes((1, HALF))
-    ky = at.astype(f32) * STEP
-    ky_mirror = jnp.where(at[:, :128] == 0, 256, at[:, :128]).astype(f32) * STEP
-    for step in range(2):
-        values, refs = references_of(slow_ref, step)
-        for g in range(2):
-            wave = freq_ref[0] * refs[g]
-            wave_sq = wave * wave
-
-            def rows_of(kx):
-                first = shift_factor(wave_sq, kx, ky)
-                mirror = shift_factor(wave_sq, kx[:, :128], ky_mirror)
-                return [
-                    jnp.concatenate([first[p], mirror[p], first[p][:, 128:]], 1) for p in range(2)
-                ]
-
-            def some_rows(k, carry):
-                start = pl.multiple_of(k * 32, 32)
-                kx = (lax.broadcasted_iota(jnp.int32, (32, HALF), 0) + start).astype(f32) * STEP
-                found = rows_of(kx)
-                for p in range(2):
-                    factor_ref[step, g, p, pl.ds(start, 32), :] = found[p]
-                return carry
-
-            lax.fori_loop(0, 8, some_rows, 0)
-            at_row = lax.broadcasted_iota(jnp.int32, (8, HALF), 0)
-            found = rows_of(jnp.where(at_row == 0, 256, at_row).astype(f32) * STEP)
-            for p in range(2):
-                edge_ref[step, g, p] = found[p]
 
 
 def store_spectrum(spec_ref, u, v, cols):

time: 87.2 us -> 84.7 us (0.971)
  Pallas kernels: 36.8 us -> 34.2 us
    pallas_call x1, Pallas kernels: 7.63 us -> 5.17 us  [local(): call(solve_kernel, [(256, 128), (4, 32, 512)], [SM, VM] + [HBM] * 4, 24,...]
where the time goes in v4:
time: 84.7 us; the launch traced here: 84.2 us
  Pallas kernels  34.2 us (40%)
  starting transfers between devices  25.2 us (30%)
  waiting for transfers between devices  12 us (14%)
  blocking collectives  9 us (11%)
  local copies, waits for them, and re-layouts  2.38 us (3%)
  between operations  1.4 us (2%)
    pallas_call x1, Pallas kernels, local(): call(second_kernel, [(2, 32, 512), (8, 32, 128)], [SM, SM, SM, VM] + [HBM...  11.8 us
    all_to_all x1, starting transfers between devices, local(): got = lax.all_to_all(sent.reshape(128, 4, 128), everyone, 0, 0, tiled=True)  11.5 us
    all_to_all x1, blocking collectives, local(): got = lax.all_to_all(sent, 'freq', 0, 0, tiled=True)  9 us
    pallas_call x1, Pallas kernels, local(): call(first_kernel, [(32, 512), (2, 2, 512, 512)], [SM, SM, SM, VM] + [HBM...  8.14 us
    all_to_all x1, starting transfers between devices, local(): got = lax.all_to_all(sent.reshape(128, 2, 128), everyone, 0, 0, tiled=True)  6.98 us
    pallas_call x1, Pallas kernels, local(): call(factor_kernel, [(2, 2, 2, 256, 512), (2, 2, 2, 8, 512)], [SM, SM], 59)  5.65 us
    pallas_call x1, Pallas kernels, local(): call(solve_kernel, [(256, 128), (4, 32, 512)], [SM, VM] + [HBM] * 4, 24,...  5.17 us
    ppermute x3, waiting for transfers between devices, local(): lax.ppermute(velocity, 'lat', [(i, i ^ d) for i in range(16)])  4.46 us
  transfers between devices with their start and end apart: 8, of which 4 were waited for; matrix products, arithmetic and copies ran while one was open for 0% of the time, Pallas kernels for 16%

profile of v4, /device:TPU:1, one launch (start us, length us, event | category | flops | bytes accessed | tf_op | source)
XLA Modules:
  0.0 84.2 jit_solution(13502959778080669296)
XLA Ops:
  0.6 2.7 %shard_map.131 = (f32[512,128]{1,0:T(8,128)}, f32[32,512]{1,0:T(8,128)}) custom-call(s32[1]{0:T(128)} %bitcast.lat_ref, s32[1,1024]{1,0:T(1,128)} %bitcast.16, s32[1,1024]{1,0:T(1,128)} %bitcast.17, f32[2,1024]{1,0:T(2,128)} %refs_2_.2, f32[1,1024]{1,0:T(1,128)} %bitcast.18, f32[16,1024]{1,0:T(8,128)} %bitcast.15, s32[2,32,512]{2,1,0:T(8,128)} %refs_9_.1), custom_call_target="tpu_custom_call" | custom-call | tf_op jit(solution)/shard_map/pallas_call | solution.py:588
  3.4 11.5 %all-to-all-start = ((f32[128,4,128]{2,1,0:T(4,128)}), f32[128,4,128]{2,1,0:T(4,128)S(1)}, u32[]{:S(2)}, u32[]{:S(2)}) async-start(f32[128,4,128]{2,1,0:T(4,128)} %bitcast.14), calls=%async_computation | async-start | bytes 524288 | tf_op jit(solution)/shard_map/all_to_all | solution.py:611
  14.9 2.7 %collective-permute-start.2 = (f32[32,512]{1,0:T(8,128)}, f32[32,512]{1,0:T(8,128)S(1)}, u32[]{:S(2)}, u32[]{:S(2)}) collective-permute-start(f32[32,512]{1,0:T(8,128)} %get-tuple-element.13.refs_0_), channel_id=1, source_target_pairs={{0,3},{1,2},{2,1},{3,0},{4,7},{5,6},{6,5},{7,4},{8,11},{9,10},{10,... | collective-permute-start | bytes 196616 | tf_op jit(solution)/shard_map/ppermute | solution.py:613
  17.6 0.6 collective-permute-start.1
  18.1 0.1 collective-permute-start
  18.2 3.6 %collective-permute-done.2.refs_3_ = f32[32,512]{1,0:T(8,128)S(1)} collective-permute-done((f32[32,512]{1,0:T(8,128)}, f32[32,512]{1,0:T(8,128)S(1)}, u32[]{:S(2)}, u32[]{:S(2)}) %collective-permute-start.2) | collective-permute-done | bytes 65568 | tf_op jit(solution)/shard_map/ppermute | solution.py:613
  21.9 0.8 collective-permute-done.1.refs_2_
  22.7 0.0 collective-permute-done.refs_1_
  22.7 3.7 %all-to-all-done = f32[128,4,128]{2,1,0:T(4,128)S(1)} async-done(((f32[128,4,128]{2,1,0:T(4,128)}), f32[128,4,128]{2,1,0:T(4,128)S(1)}, u32[]{:S(2)}, u32[]{:S(2)}) %all-to-all-start) | async-done | bytes 262176 | tf_op jit(solution)/shard_map/all_to_all | solution.py:611
  26.4 0.8 copy-done.1
  27.2 5.2 %shard_map.132 = (f32[256,128]{1,0:T(8,128)}, f32[4,32,512]{2,1,0:T(8,128)S(1)}) custom-call(s32[1]{0:T(128)} %bitcast.lat_ref, f32[512,128]{1,0:T(8,128)S(1)} %bitcast.12, f32[32,512]{1,0:T(8,128)S(1)} %copy-done.1, f32[32,512]{1,0:T(8,128)S(1)} %collective-permute-done.refs_1_, f32[32,512]{1,0:T(8,128)S(1)} %collective-permute-done.1.refs_2_, ...), custom_call_target="tpu_custom_call" | custom-call | tf_op jit(solution)/shard_map/pallas_call | solution.py:615
  32.4 0.0 copy-start
  32.4 0.4 collective-permute-start.5
  32.8 1.3 %collective-permute-start.4 = (f32[4,32,512]{2,1,0:T(8,128)S(1)}, f32[4,32,512]{2,1,0:T(8,128)S(1)}, u32[]{:S(2)}, u32[]{:S(2)}) collective-permute-start(f32[4,32,512]{2,1,0:T(8,128)S(1)} %get-tuple-element.18.refs_0_), channel_id=1, source_target_pairs={{0,8},{1,9},{2,10},{3,11},{4,12},{5,13},{6,14},{7,15},{8,0},{9,1},... | collective-permute-start | bytes 786440 | tf_op jit(solution)/shard_map/ppermute | solution.py:625
  34.0 1.7 %collective-permute-start.3 = (f32[4,32,512]{2,1,0:T(8,128)S(1)}, f32[4,32,512]{2,1,0:T(8,128)S(1)}, u32[]{:S(2)}, u32[]{:S(2)}) collective-permute-start(f32[4,32,512]{2,1,0:T(8,128)S(1)} %get-tuple-element.18.refs_0_), channel_id=1, source_target_pairs={{0,4},{1,5},{2,6},{3,7},{4,0},{5,1},{6,2},{7,3},{8,12},{9,13},{10,... | collective-permute-start | bytes 786440 | tf_op jit(solution)/shard_map/ppermute | solution.py:625
  35.7 7.0 %all-to-all-start.1 = ((f32[128,2,128]{2,1,0:T(2,128)}), f32[128,2,128]{2,1,0:T(2,128)S(1)}, u32[]{:S(2)}, u32[]{:S(2)}) async-start(f32[128,2,128]{2,1,0:T(2,128)} %bitcast.7), calls=%async_computation.1 | async-start | bytes 262144 | tf_op jit(solution)/shard_map/all_to_all | solution.py:623
  43.4 5.6 %shard_map.133 = (f32[2,2,2,256,512]{4,3,2,1,0:T(8,128)}, f32[2,2,2,8,512]{4,3,2,1,0:T(8,128)}) custom-call(f32[1]{0:T(128)S(6)} %copy.15.freq_ref, f32[2,8]{1,0:T(2,128)} %slow_ref.5), custom_call_target="tpu_custom_call" | custom-call | tf_op jit(solution)/shard_map/pallas_call | solution.py:627
  49.0 3.9 %all-to-all-done.1 = f32[128,2,128]{2,1,0:T(2,128)S(1)} async-done(((f32[128,2,128]{2,1,0:T(2,128)}), f32[128,2,128]{2,1,0:T(2,128)S(1)}, u32[]{:S(2)}, u32[]{:S(2)}) %all-to-all-start.1) | async-done | bytes 131104 | tf_op jit(solution)/shard_map/all_to_all | solution.py:623
  52.9 0.7 copy-done.2
  53.6 8.1 %shard_map.134 = (f32[32,512]{1,0:T(8,128)}, f32[2,2,512,512]{3,2,1,0:T(8,128)}) custom-call(s32[1]{0:T(128)} %bitcast.lat_ref, f32[1]{0:T(128)S(6)} %copy.15.freq_ref, f32[2,8]{1,0:T(2,128)} %slow_ref.5, f32[256,128]{1,0:T(8,128)} %bitcast.13, bf16[2,128,512]{2,1,0:T(8,128)(2,1)} %constant.12.clone.refs_0_, bf16[2,512,128]{2,1,0:T(8,128)(2,1)} %constant.13.clone.refs_1_, ...), custom_call_target="tpu_custom_call" | custom-call | tf_op jit(solution)/shard_map/pallas_call | solution.py:630
  61.7 0.0 collective-permute-done.5.refs_3_
  61.7 0.0 copy-start.3
  61.7 0.0 collective-permute-done.4.refs_2_
  61.7 0.0 copy-start.4
  61.8 0.0 collective-permute-done.3.refs_1_
  61.8 0.0 copy-start.5
  61.8 0.6 copy-done.3
  62.4 0.1 copy-done.4
  62.5 0.1 copy-done.5
  62.7 11.8 %shard_map.135 = (f32[2,32,512]{2,1,0:T(8,128)}, f32[8,32,128]{2,1,0:T(8,128)}) custom-call(s32[1]{0:T(128)} %bitcast.lat_ref, f32[1]{0:T(128)S(6)} %copy.15.freq_ref, f32[2,8]{1,0:T(2,128)} %slow_ref.5, f32[32,512]{1,0:T(8,128)} %get-tuple-element.17.image_ref, f32[4,32,512]{2,1,0:T(8,128)} %copy-done, f32[4,32,512]{2,1,0:T(8,128)} %copy-done.5, ...), custom_call_target="tpu_custom_call" | custom-call | tf_op jit(solution)/shard_map/pallas_call | solution.py:663
  74.5 9.0 %all_to_all.15.got_ref = f32[8,32,128]{2,1,0:T(8,128)S(1)} all-to-all(f32[8,32,128]{2,1,0:T(8,128)} %get-tuple-element.21), channel_id=1, replica_groups=mesh['freq'=8,'lat'=16] {'freq'}, dimensions={0} | all-to-all | bytes 262144 | tf_op jit(solution)/shard_map/all_to_all | solution.py:695
  83.5 0.7 shard_map.136
  (3 shorter events, 0.0 us)
Async XLA Ops:
  3.4 23.0 %all-to-all-start = ((f32[128,4,128]{2,1,0:T(4,128)}), f32[128,4,128]{2,1,0:T(4,128)S(1)}, u32[]{:S(2)}, u32[]{:S(2)}) async-start(f32[128,4,128]{2,1,0:T(4,128)} %bitcast.14), calls=%async_computation | async-start | bytes 524288 | tf_op jit(solution)/shard_map/all_to_all | solution.py:611
  14.9 7.0 %collective-permute-start.2 = (f32[32,512]{1,0:T(8,128)}, f32[32,512]{1,0:T(8,128)S(1)}, u32[]{:S(2)}, u32[]{:S(2)}) collective-permute-start(f32[32,512]{1,0:T(8,128)} %get-tuple-element.13.refs_0_), channel_id=1, source_target_pairs={{0,3},{1,2},{2,1},{3,0},{4,7},{5,6},{6,5},{7,4},{8,11},{9,10},{10,... | collective-permute-start | bytes 196616 | tf_op jit(solution)/shard_map/ppermute | solution.py:613
  17.6 5.1 %collective-permute-start.1 = (f32[32,512]{1,0:T(8,128)}, f32[32,512]{1,0:T(8,128)S(1)}, u32[]{:S(2)}, u32[]{:S(2)}) collective-permute-start(f32[32,512]{1,0:T(8,128)} %get-tuple-element.13.refs_0_), channel_id=1, source_target_pairs={{0,2},{1,3},{2,0},{3,1},{4,6},{5,7},{6,4},{7,5},{8,10},{9,11},{10,... | collective-permute-start | bytes 196616 | tf_op jit(solution)/shard_map/ppermute | solution.py:613
  18.1 4.6 %collective-permute-start = (f32[32,512]{1,0:T(8,128)}, f32[32,512]{1,0:T(8,128)S(1)}, u32[]{:S(2)}, u32[]{:S(2)}) collective-permute-start(f32[32,512]{1,0:T(8,128)} %get-tuple-element.13.refs_0_), channel_id=1, source_target_pairs={{0,1},{1,0},{2,3},{3,2},{4,5},{5,4},{6,7},{7,6},{8,9},{9,8},{10,11... | collective-permute-start | bytes 196616 | tf_op jit(solution)/shard_map/ppermute | solution.py:613
  26.4 0.8 copy-start.1
  32.4 29.4 %copy-start = (f32[4,32,512]{2,1,0:T(8,128)}, f32[4,32,512]{2,1,0:T(8,128)S(1)}, u32[]{:S(2)}) copy-start(f32[4,32,512]{2,1,0:T(8,128)S(1)} %get-tuple-element.18.refs_0_) | copy-start | bytes 786436
  32.4 29.3 %collective-permute-start.5 = (f32[4,32,512]{2,1,0:T(8,128)S(1)}, f32[4,32,512]{2,1,0:T(8,128)S(1)}, u32[]{:S(2)}, u32[]{:S(2)}) collective-permute-start(f32[4,32,512]{2,1,0:T(8,128)S(1)} %get-tuple-element.18.refs_0_), channel_id=1, source_target_pairs={{0,12},{1,13},{2,14},{3,15},{4,8},{5,9},{6,10},{7,11},{8,4},{9,5},... | collective-permute-start | bytes 786440 | tf_op jit(solution)/shard_map/ppermute | solution.py:625
  32.8 29.0 %collective-permute-start.4 = (f32[4,32,512]{2,1,0:T(8,128)S(1)}, f32[4,32,512]{2,1,0:T(8,128)S(1)}, u32[]{:S(2)}, u32[]{:S(2)}) collective-permute-start(f32[4,32,512]{2,1,0:T(8,128)S(1)} %get-tuple-element.18.refs_0_), channel_id=1, source_target_pairs={{0,8},{1,9},{2,10},{3,11},{4,12},{5,13},{6,14},{7,15},{8,0},{9,1},... | collective-permute-start | bytes 786440 | tf_op jit(solution)/shard_map/ppermute | solution.py:625
  34.0 27.7 %collective-permute-start.3 = (f32[4,32,512]{2,1,0:T(8,128)S(1)}, f32[4,32,512]{2,1,0:T(8,128)S(1)}, u32[]{:S(2)}, u32[]{:S(2)}) collective-permute-start(f32[4,32,512]{2,1,0:T(8,128)S(1)} %get-tuple-element.18.refs_0_), channel_id=1, source_target_pairs={{0,4},{1,5},{2,6},{3,7},{4,0},{5,1},{6,2},{7,3},{8,12},{9,13},{10,... | collective-permute-start | bytes 786440 | tf_op jit(solution)/shard_map/ppermute | solution.py:625
  35.7 17.2 %all-to-all-start.1 = ((f32[128,2,128]{2,1,0:T(2,128)}), f32[128,2,128]{2,1,0:T(2,128)S(1)}, u32[]{:S(2)}, u32[]{:S(2)}) async-start(f32[128,2,128]{2,1,0:T(2,128)} %bitcast.7), calls=%async_computation.1 | async-start | bytes 262144 | tf_op jit(solution)/shard_map/all_to_all | solution.py:623
  52.9 0.7 copy-start.2
  61.7 0.7 copy-start.3
  61.7 0.8 copy-start.4
  61.8 0.9 %copy-start.5 = (f32[4,32,512]{2,1,0:T(8,128)}, f32[4,32,512]{2,1,0:T(8,128)S(1)}, u32[]{:S(2)}) copy-start(f32[4,32,512]{2,1,0:T(8,128)S(1)} %collective-permute-done.3.refs_1_) | copy-start | bytes 786436

commit v5 on v4

--- a/solution.py
+++ b/solution.py
@@ -236,7 +236,8 @@
     return [jnp.concatenate([first[p], mirror[p], first[p][:, 128:]], 1) for p in range(2)]
 
 
-def factor_kernel(freq_ref, slow_ref, factor_ref, edge_ref):
+def factor_kernel(freq_ref, slow_ref, factor_hbm, edge_ref, factor_ref, sems):
+    leaving = []
     at = lanes((1, HALF))
     ky = at.astype(f32) * STEP
     ky_mirror = jnp.where(at[:, :128] == 0, 256, at[:, :128]).astype(f32) * STEP
@@ -260,6 +261,13 @@
             found = factor_rows(wave_sq, row.astype(f32) * STEP, ky, ky_mirror)
             for p in range(2):
                 edge_ref[step, g, p] = found[p]
+            copy = pltpu.make_async_copy(
+                factor_ref.at[step, g], factor_hbm.at[step, g], sems.at[2 * step + g]
+            )
+            copy.start()
+            leaving.append(copy)
+    for copy in leaving:
+        copy.wait()
 
 
 def solve_kernel(lat_ref, got_ref, *refs):
@@ -394,20 +402,21 @@
     )
 
 
-def first_kernel(lat_ref, freq_ref, slow_ref, got_ref, *refs):
-    sources, image_ref, back_hbm = refs[:7], refs[7], refs[8]
-    targets, sems, out_sems = refs[9:16], refs[16], refs[17]
-    spec_ref, own_back, back_ref = refs[18:]
+def grid_kernel(lat_ref, freq_ref, slow_ref, got_ref, *refs):
+    slabs, refs = refs[:4], refs[4:]
+    sources, wave_ref, out_ref = refs[:7], refs[7], refs[8]
+    targets, slabs_ref, later_ref, sems = refs[9:16], *refs[16:19]
+    spec_ref, own_back, back_ref, half_ref = refs[19:]
     fetch = Fetch(
         [
             *sources[:2],
             sources[2].at[lat_ref[0]],
             sources[3].at[0],
-            sources[4].at[0],
-            sources[5],
-            sources[6].at[0],
+            *sources[4:],
+            *slabs,
+            sources[3].at[1],
         ],
-        targets,
+        [*targets, *[slabs_ref.at[(lat_ref[0] >> 2) ^ d] for d in range(4)], later_ref],
         sems,
     )
     rows = lax.broadcasted_iota(jnp.int32, (128, 128), 0)
@@ -438,59 +447,21 @@
             pl.ds(HALF * c, HALF),
         )
     own_ref, factor_ref, edge_ref, waves_ref = fetch.take(2, 3, 4, 5)
-    leaving = []
     for g in range(2):
         for c in range(2):
             cols = pl.ds(HALF * c, HALF)
-            even, odd = invert_x(spec_ref, factor_ref, edge_ref, own_ref, own_back, g, cols)
+            even, odd = invert_x(spec_ref, factor_ref, edge_ref.at[0], own_ref, own_back, g, cols)
             u = halves_of(dot3(wave_pair(waves_ref, 2), even), 1, HALF)
             v = halves_of(dot3(wave_pair(waves_ref, 3), odd), 1, HALF)
             first, second = plus_i(u, v), minus_i(u, v)
             for p in range(2):
                 back_ref[g, p, :HALF, cols] = first[p]
                 back_ref[g, p, HALF:, cols] = second[p]
-            copy = pltpu.make_async_copy(
-                back_ref.at[g, :, :, cols], back_hbm.at[g, :, :, cols], out_sems.at[2 * g + c]
-            )
-            copy.start()
-            leaving.append(copy)
     vel_ref = fetch.take(6)
-    image_ref[...] = own_field(0, own_back, waves_ref, vel_ref[...], slow_ref, freq_ref)[0]
-    for copy in leaving:
-        copy.wait()
-
-
-def second_kernel(lat_ref, freq_ref, slow_ref, image_ref, *refs):
-    slabs, refs = refs[:4], refs[4:]
-    sources, wave_ref, out_ref = refs[:6], refs[6], refs[7]
-    targets, slabs_ref, sems, back_sems = refs[8:13], refs[13], refs[14], refs[15]
-    back_ref, spec_ref, own_back, half_ref = refs[16:]
-
-    def arriving(k):
-        at = pl.ds(pl.multiple_of(k * 128, 128), 128)
-        return pltpu.make_async_copy(
-            sources[0].at[:, :, at, :], back_ref.at[:, :, at, :], back_sems.at[k]
-        )
-
-    arriving(0).start()
-    fetch = Fetch(
-        [
-            sources[1],
-            *slabs,
-            sources[2].at[1],
-            sources[3].at[1],
-            sources[4].at[lat_ref[0]],
-            sources[5].at[1],
-        ],
-        [targets[0], *[slabs_ref.at[(lat_ref[0] >> 2) ^ d] for d in range(4)], *targets[1:]],
-        sems,
-    )
-    for k in range(1, 4):
-        arriving(k).start()
-    waves_ref = fetch.take(*range(5))[0]
+    image = own_field(0, own_back, waves_ref, vel_ref[0], slow_ref, freq_ref)[0]
+    fetch.take(7, 8, 9, 10)
 
     def some_rows(k, carry):
-        arriving(k).wait()
         at = pl.ds(pl.multiple_of(k * 128, 128), 128)
         back = []
         for g in range(2):
@@ -540,19 +511,18 @@
         return carry
 
     lax.fori_loop(0, 2, some_columns, 0)
-    factor_ref, edge_ref, own_ref, vel_ref = fetch.take(5, 6, 7, 8)
+    later_factor = fetch.take(11)
 
     def invert(k, carry):
         cols = pl.ds(pl.multiple_of((k & 1) * HALF, HALF), HALF)
-        invert_x(spec_ref, factor_ref, edge_ref, own_ref, own_back, k >> 1, cols)
+        invert_x(spec_ref, later_factor, edge_ref.at[1], own_ref, own_back, k >> 1, cols)
         return carry
 
     lax.fori_loop(0, 4, invert, 0)
-    field = own_field(1, own_back, waves_ref, vel_ref[...], slow_ref, freq_ref)
+    field = own_field(1, own_back, waves_ref, vel_ref[1], slow_ref, freq_ref)
     for p in range(2):
         wave_ref[p] = field[p]
     upper = lanes((32, 128)) >= 64
-    image = image_ref[...]
     for d in range(8):
         col, pos = d // 2, d % 2
         first = turned(image[:, 128 * col : 128 * col + 128], -64 * pos)
@@ -625,71 +595,46 @@
         lax.ppermute(slabs, "lat", [(i, i ^ d) for i in range(16)]) for d in (4, 8, 12)
     ]
     factor, edge = call(
-        factor_kernel, [(2, 2, 2, 256, 512), (2, 2, 2, 8, 512)], [SM, SM], 59
+        factor_kernel,
+        [(2, 2, 2, 256, 512), (2, 2, 2, 8, 512)],
+        [SM, SM],
+        59,
+        [pltpu.VMEM((2, 2, 2, 256, 512), f32), pltpu.SemaphoreType.DMA((4,))],
+        [HBM, VM],
     )(frequency, slowness)
-    image, back = call(
-        first_kernel,
-        [(32, 512), (2, 2, 512, 512)],
-        [SM, SM, SM, VM] + [HBM] * 7,
+    wave, sent = call(
+        grid_kernel,
+        [(2, 32, 512), (8, 32, 128)],
+        [SM, SM, SM, VM] + [HBM] * 11,
         59,
         [
             pltpu.VMEM((2, 128, 512), bf16),
             pltpu.VMEM((2, 512, 128), bf16),
             pltpu.VMEM((128, 256), bf16),
             pltpu.VMEM((2, 2, 256, 512), f32),
-            pltpu.VMEM((2, 2, 8, 512), f32),
+            pltpu.VMEM((2, 2, 2, 8, 512), f32),
             pltpu.VMEM((2, 6, 256, 256), bf16),
-            pltpu.VMEM((32, 512), jnp.int32),
-            pltpu.SemaphoreType.DMA((7,)),
-            pltpu.SemaphoreType.DMA((4,)),
+            pltpu.VMEM((2, 32, 512), jnp.int32),
+            pltpu.VMEM((4, 4, 32, 512), f32),
+            pltpu.VMEM((2, 2, 256, 512), f32),
+            pltpu.SemaphoreType.DMA((12,)),
             pltpu.VMEM((4, 256, 512), f32),
             pltpu.VMEM((2, 64, 512), f32),
             pltpu.VMEM((2, 2, 512, 512), f32),
+            pltpu.VMEM((2, 512, 512), f32),
         ],
-        [VM, HBM],
     )(
         lat_at,
         frequency,
         slowness,
         got.reshape(256, 128),
+        *slabs,
         const["along_y"],
         const["along_x"],
         const["own"],
         factor,
         edge,
         const["waves"],
-        vel_index,
-    )
-    wave, sent = call(
-        second_kernel,
-        [(2, 32, 512), (8, 32, 128)],
-        [SM, SM, SM, VM] + [HBM] * 10,
-        59,
-        [
-            pltpu.VMEM((2, 6, 256, 256), bf16),
-            pltpu.VMEM((2, 2, 256, 512), f32),
-            pltpu.VMEM((2, 2, 8, 512), f32),
-            pltpu.VMEM((128, 256), bf16),
-            pltpu.VMEM((32, 512), jnp.int32),
-            pltpu.VMEM((4, 4, 32, 512), f32),
-            pltpu.SemaphoreType.DMA((9,)),
-            pltpu.SemaphoreType.DMA((4,)),
-            pltpu.VMEM((2, 2, 512, 512), f32),
-            pltpu.VMEM((4, 256, 512), f32),
-            pltpu.VMEM((2, 64, 512), f32),
-            pltpu.VMEM((2, 512, 512), f32),
-        ],
-    )(
-        lat_at,
-        frequency,
-        slowness,
-        image,
-        *slabs,
-        back,
-        const["waves"],
-        factor,
-        edge,
-        const["own"],
         vel_index,
     )
     got = lax.all_to_all(sent, "freq", 0, 0, tiled=True)

time: 84.7 us -> 79.8 us (0.942)
  Pallas kernels: 34.2 us -> 29.8 us
    pallas_call x3 -> x2, Pallas kernels: 25.6 us -> 21.2 us  [the longest x1 15.9 us: local(): call(grid_kernel, [(2, 32, 512), (8, 32, 128)], [SM, SM, SM, VM] + [HBM]...]
  transfers between devices with their start and end apart: 8 -> 8, of which waited for: 4 -> 4; matrix products, arithmetic and copies ran while one was open for 0% -> 0% of each run, Pallas kernels for 16% -> 7%
where the time goes in v5:
time: 79.8 us; the launch traced here: 79.4 us
  Pallas kernels  29.8 us (37%)
  starting transfers between devices  25.2 us (32%)
  waiting for transfers between devices  12.3 us (15%)
  blocking collectives  9.01 us (11%)
  local copies, waits for them, and re-layouts  1.76 us (2%)
  between operations  1.38 us (2%)
    pallas_call x1, Pallas kernels, local(): call(grid_kernel, [(2, 32, 512), (8, 32, 128)], [SM, SM, SM, VM] + [HBM]...  15.9 us
    all_to_all x1, starting transfers between devices, local(): got = lax.all_to_all(sent.reshape(128, 4, 128), everyone, 0, 0, tiled=True)  11.5 us
    all_to_all x1, blocking collectives, local(): got = lax.all_to_all(sent, 'freq', 0, 0, tiled=True)  9.01 us
    all_to_all x1, starting transfers between devices, local(): got = lax.all_to_all(sent.reshape(128, 2, 128), everyone, 0, 0, tiled=True)  6.98 us
    pallas_call x1, Pallas kernels, local(): call(factor_kernel, [(2, 2, 2, 256, 512), (2, 2, 2, 8, 512)], [SM, SM], 5...  5.34 us
    pallas_call x1, Pallas kernels, local(): call(solve_kernel, [(256, 128), (4, 32, 512)], [SM, VM] + [HBM] * 4, 24,...  5.17 us
    ppermute x3, waiting for transfers between devices, local(): lax.ppermute(velocity, 'lat', [(i, i ^ d) for i in range(16)])  4.46 us
    all_to_all x1, waiting for transfers between devices, local(): got = lax.all_to_all(sent.reshape(128, 2, 128), everyone, 0, 0, tiled=True)  4.21 us
  transfers between devices with their start and end apart: 8, of which 4 were waited for; matrix products, arithmetic and copies ran while one was open for 0% of the time, Pallas kernels for 7%

profile of v5, /device:TPU:1, one launch (start us, length us, event | category | flops | bytes accessed | tf_op | source)
XLA Modules:
  0.0 79.4 jit_solution(14598591569215929283)
XLA Ops:
  0.6 2.7 %shard_map.131 = (f32[512,128]{1,0:T(8,128)}, f32[32,512]{1,0:T(8,128)}) custom-call(s32[1]{0:T(128)} %bitcast.lat_ref, s32[1,1024]{1,0:T(1,128)} %bitcast.16, s32[1,1024]{1,0:T(1,128)} %bitcast.17, f32[2,1024]{1,0:T(2,128)} %refs_2_.1, f32[1,1024]{1,0:T(1,128)} %bitcast.18, f32[16,1024]{1,0:T(8,128)} %bitcast.15, s32[2,32,512]{2,1,0:T(8,128)} %refs_10_.1), custom_call_target="tpu_custom_call" | custom-call | tf_op jit(solution)/shard_map/pallas_call | solution.py:558
  3.4 11.5 %all-to-all-start = ((f32[128,4,128]{2,1,0:T(4,128)}), f32[128,4,128]{2,1,0:T(4,128)S(1)}, u32[]{:S(2)}, u32[]{:S(2)}) async-start(f32[128,4,128]{2,1,0:T(4,128)} %bitcast.14), calls=%async_computation | async-start | bytes 524288 | tf_op jit(solution)/shard_map/all_to_all | solution.py:581
  14.9 2.7 %collective-permute-start.2 = (f32[32,512]{1,0:T(8,128)}, f32[32,512]{1,0:T(8,128)S(1)}, u32[]{:S(2)}, u32[]{:S(2)}) collective-permute-start(f32[32,512]{1,0:T(8,128)} %get-tuple-element.11.refs_0_), channel_id=1, source_target_pairs={{0,3},{1,2},{2,1},{3,0},{4,7},{5,6},{6,5},{7,4},{8,11},{9,10},{10,... | collective-permute-start | bytes 196616 | tf_op jit(solution)/shard_map/ppermute | solution.py:583
  17.6 0.6 collective-permute-start.1
  18.1 0.1 collective-permute-start
  18.2 3.6 %collective-permute-done.2.refs_3_ = f32[32,512]{1,0:T(8,128)S(1)} collective-permute-done((f32[32,512]{1,0:T(8,128)}, f32[32,512]{1,0:T(8,128)S(1)}, u32[]{:S(2)}, u32[]{:S(2)}) %collective-permute-start.2) | collective-permute-done | bytes 65568 | tf_op jit(solution)/shard_map/ppermute | solution.py:583
  21.9 0.8 %collective-permute-done.1.refs_2_ = f32[32,512]{1,0:T(8,128)S(1)} collective-permute-done((f32[32,512]{1,0:T(8,128)}, f32[32,512]{1,0:T(8,128)S(1)}, u32[]{:S(2)}, u32[]{:S(2)}) %collective-permute-start.1) | collective-permute-done | bytes 65568 | tf_op jit(solution)/shard_map/ppermute | solution.py:583
  22.7 0.0 collective-permute-done.refs_1_
  22.7 3.7 %all-to-all-done = f32[128,4,128]{2,1,0:T(4,128)S(1)} async-done(((f32[128,4,128]{2,1,0:T(4,128)}), f32[128,4,128]{2,1,0:T(4,128)S(1)}, u32[]{:S(2)}, u32[]{:S(2)}) %all-to-all-start) | async-done | bytes 262176 | tf_op jit(solution)/shard_map/all_to_all | solution.py:581
  26.4 0.0 copy-start.1
  26.4 0.8 %copy-done.1 = f32[32,512]{1,0:T(8,128)S(1)} copy-done((f32[32,512]{1,0:T(8,128)S(1)}, f32[32,512]{1,0:T(8,128)}, u32[]{:S(2)}) %copy-start.1) | copy-done | bytes 65560
  27.2 5.2 %shard_map.132 = (f32[256,128]{1,0:T(8,128)}, f32[4,32,512]{2,1,0:T(8,128)S(1)}) custom-call(s32[1]{0:T(128)} %bitcast.lat_ref, f32[512,128]{1,0:T(8,128)S(1)} %bitcast.12, f32[32,512]{1,0:T(8,128)S(1)} %copy-done.1, f32[32,512]{1,0:T(8,128)S(1)} %collective-permute-done.refs_1_, f32[32,512]{1,0:T(8,128)S(1)} %collective-permute-done.1.refs_2_, ...), custom_call_target="tpu_custom_call" | custom-call | tf_op jit(solution)/shard_map/pallas_call | solution.py:585
  32.4 0.0 copy-start
  32.4 0.4 collective-permute-start.5
  32.8 1.3 %collective-permute-start.4 = (f32[4,32,512]{2,1,0:T(8,128)S(1)}, f32[4,32,512]{2,1,0:T(8,128)S(1)}, u32[]{:S(2)}, u32[]{:S(2)}) collective-permute-start(f32[4,32,512]{2,1,0:T(8,128)S(1)} %get-tuple-element.13.refs_0_), channel_id=1, source_target_pairs={{0,8},{1,9},{2,10},{3,11},{4,12},{5,13},{6,14},{7,15},{8,0},{9,1},... | collective-permute-start | bytes 786440 | tf_op jit(solution)/shard_map/ppermute | solution.py:595
  34.0 1.7 %collective-permute-start.3 = (f32[4,32,512]{2,1,0:T(8,128)S(1)}, f32[4,32,512]{2,1,0:T(8,128)S(1)}, u32[]{:S(2)}, u32[]{:S(2)}) collective-permute-start(f32[4,32,512]{2,1,0:T(8,128)S(1)} %get-tuple-element.13.refs_0_), channel_id=1, source_target_pairs={{0,4},{1,5},{2,6},{3,7},{4,0},{5,1},{6,2},{7,3},{8,12},{9,13},{10,... | collective-permute-start | bytes 786440 | tf_op jit(solution)/shard_map/ppermute | solution.py:595
  35.7 7.0 %all-to-all-start.1 = ((f32[128,2,128]{2,1,0:T(2,128)}), f32[128,2,128]{2,1,0:T(2,128)S(1)}, u32[]{:S(2)}, u32[]{:S(2)}) async-start(f32[128,2,128]{2,1,0:T(2,128)} %bitcast.7), calls=%async_computation.1 | async-start | bytes 262144 | tf_op jit(solution)/shard_map/all_to_all | solution.py:593
  43.4 5.3 %shard_map.133 = (f32[2,2,2,256,512]{4,3,2,1,0:T(8,128)}, f32[2,2,2,8,512]{4,3,2,1,0:T(8,128)}) custom-call(f32[1]{0:T(128)S(6)} %copy.15.freq_ref, f32[2,8]{1,0:T(2,128)} %slow_ref.3), custom_call_target="tpu_custom_call" | custom-call | tf_op jit(solution)/shard_map/pallas_call | solution.py:597
  48.7 4.2 %all-to-all-done.1 = f32[128,2,128]{2,1,0:T(2,128)S(1)} async-done(((f32[128,2,128]{2,1,0:T(2,128)}), f32[128,2,128]{2,1,0:T(2,128)S(1)}, u32[]{:S(2)}, u32[]{:S(2)}) %all-to-all-start.1) | async-done | bytes 131104 | tf_op jit(solution)/shard_map/all_to_all | solution.py:593
  52.9 0.0 collective-permute-done.5.refs_3_
  52.9 0.0 collective-permute-done.4.refs_2_
  52.9 0.0 copy-start.4
  52.9 0.0 collective-permute-done.3.refs_1_
  52.9 0.0 copy-start.5
  53.0 0.0 copy-done
  53.0 0.6 copy-done.2
  53.6 0.1 copy-done.3
  53.7 0.1 copy-done.4
  53.8 0.1 copy-done.5
  53.9 15.9 %shard_map.134 = (f32[2,32,512]{2,1,0:T(8,128)}, f32[8,32,128]{2,1,0:T(8,128)}) custom-call(s32[1]{0:T(128)} %bitcast.lat_ref, f32[1]{0:T(128)S(6)} %copy.15.freq_ref, f32[2,8]{1,0:T(2,128)} %slow_ref.3, f32[256,128]{1,0:T(8,128)} %bitcast.13, f32[4,32,512]{2,1,0:T(8,128)} %copy-done, f32[4,32,512]{2,1,0:T(8,128)} %copy-done.5, f32[4,32,512]{2,1,0:T(8,128)} %copy-done.4, ...), custom_call_target="tpu_custom_call" | custom-call | tf_op jit(solution)/shard_map/pallas_call | solution.py:605
  69.7 9.0 %all_to_all.15.got_ref = f32[8,32,128]{2,1,0:T(8,128)S(1)} all-to-all(f32[8,32,128]{2,1,0:T(8,128)} %get-tuple-element.17), channel_id=1, replica_groups=mesh['freq'=8,'lat'=16] {'freq'}, dimensions={0} | all-to-all | bytes 262144 | tf_op jit(solution)/shard_map/all_to_all | solution.py:640
  78.7 0.7 shard_map.135
  (2 shorter events, 0.0 us)
Async XLA Ops:
  3.4 23.0 %all-to-all-start = ((f32[128,4,128]{2,1,0:T(4,128)}), f32[128,4,128]{2,1,0:T(4,128)S(1)}, u32[]{:S(2)}, u32[]{:S(2)}) async-start(f32[128,4,128]{2,1,0:T(4,128)} %bitcast.14), calls=%async_computation | async-start | bytes 524288 | tf_op jit(solution)/shard_map/all_to_all | solution.py:581
  14.9 7.0 %collective-permute-start.2 = (f32[32,512]{1,0:T(8,128)}, f32[32,512]{1,0:T(8,128)S(1)}, u32[]{:S(2)}, u32[]{:S(2)}) collective-permute-start(f32[32,512]{1,0:T(8,128)} %get-tuple-element.11.refs_0_), channel_id=1, source_target_pairs={{0,3},{1,2},{2,1},{3,0},{4,7},{5,6},{6,5},{7,4},{8,11},{9,10},{10,... | collective-permute-start | bytes 196616 | tf_op jit(solution)/shard_map/ppermute | solution.py:583
  17.6 5.1 %collective-permute-start.1 = (f32[32,512]{1,0:T(8,128)}, f32[32,512]{1,0:T(8,128)S(1)}, u32[]{:S(2)}, u32[]{:S(2)}) collective-permute-start(f32[32,512]{1,0:T(8,128)} %get-tuple-element.11.refs_0_), channel_id=1, source_target_pairs={{0,2},{1,3},{2,0},{3,1},{4,6},{5,7},{6,4},{7,5},{8,10},{9,11},{10,... | collective-permute-start | bytes 196616 | tf_op jit(solution)/shard_map/ppermute | solution.py:583
  18.1 4.6 %collective-permute-start = (f32[32,512]{1,0:T(8,128)}, f32[32,512]{1,0:T(8,128)S(1)}, u32[]{:S(2)}, u32[]{:S(2)}) collective-permute-start(f32[32,512]{1,0:T(8,128)} %get-tuple-element.11.refs_0_), channel_id=1, source_target_pairs={{0,1},{1,0},{2,3},{3,2},{4,5},{5,4},{6,7},{7,6},{8,9},{9,8},{10,11... | collective-permute-start | bytes 196616 | tf_op jit(solution)/shard_map/ppermute | solution.py:583
  26.4 0.8 %copy-start.1 = (f32[32,512]{1,0:T(8,128)S(1)}, f32[32,512]{1,0:T(8,128)}, u32[]{:S(2)}) copy-start(f32[32,512]{1,0:T(8,128)} %get-tuple-element.11.refs_0_) | copy-start | bytes 196612
  32.4 20.6 %copy-start = (f32[4,32,512]{2,1,0:T(8,128)}, f32[4,32,512]{2,1,0:T(8,128)S(1)}, u32[]{:S(2)}) copy-start(f32[4,32,512]{2,1,0:T(8,128)S(1)} %get-tuple-element.13.refs_0_) | copy-start | bytes 786436
  32.4 20.5 %collective-permute-start.5 = (f32[4,32,512]{2,1,0:T(8,128)S(1)}, f32[4,32,512]{2,1,0:T(8,128)S(1)}, u32[]{:S(2)}, u32[]{:S(2)}) collective-permute-start(f32[4,32,512]{2,1,0:T(8,128)S(1)} %get-tuple-element.13.refs_0_), channel_id=1, source_target_pairs={{0,12},{1,13},{2,14},{3,15},{4,8},{5,9},{6,10},{7,11},{8,4},{9,5},... | collective-permute-start | bytes 786440 | tf_op jit(solution)/shard_map/ppermute | solution.py:595
  32.8 20.2 %collective-permute-start.4 = (f32[4,32,512]{2,1,0:T(8,128)S(1)}, f32[4,32,512]{2,1,0:T(8,128)S(1)}, u32[]{:S(2)}, u32[]{:S(2)}) collective-permute-start(f32[4,32,512]{2,1,0:T(8,128)S(1)} %get-tuple-element.13.refs_0_), channel_id=1, source_target_pairs={{0,8},{1,9},{2,10},{3,11},{4,12},{5,13},{6,14},{7,15},{8,0},{9,1},... | collective-permute-start | bytes 786440 | tf_op jit(solution)/shard_map/ppermute | solution.py:595
  34.0 18.9 %collective-permute-start.3 = (f32[4,32,512]{2,1,0:T(8,128)S(1)}, f32[4,32,512]{2,1,0:T(8,128)S(1)}, u32[]{:S(2)}, u32[]{:S(2)}) collective-permute-start(f32[4,32,512]{2,1,0:T(8,128)S(1)} %get-tuple-element.13.refs_0_), channel_id=1, source_target_pairs={{0,4},{1,5},{2,6},{3,7},{4,0},{5,1},{6,2},{7,3},{8,12},{9,13},{10,... | collective-permute-start | bytes 786440 | tf_op jit(solution)/shard_map/ppermute | solution.py:595
  35.7 17.2 %all-to-all-start.1 = ((f32[128,2,128]{2,1,0:T(2,128)}), f32[128,2,128]{2,1,0:T(2,128)S(1)}, u32[]{:S(2)}, u32[]{:S(2)}) async-start(f32[128,2,128]{2,1,0:T(2,128)} %bitcast.7), calls=%async_computation.1 | async-start | bytes 262144 | tf_op jit(solution)/shard_map/all_to_all | solution.py:593
  52.9 0.7 copy-start.2
  52.9 0.7 copy-start.3
  52.9 0.8 %copy-start.4 = (f32[4,32,512]{2,1,0:T(8,128)}, f32[4,32,512]{2,1,0:T(8,128)S(1)}, u32[]{:S(2)}) copy-start(f32[4,32,512]{2,1,0:T(8,128)S(1)} %collective-permute-done.4.refs_2_) | copy-start | bytes 786436
  52.9 0.9 %copy-start.5 = (f32[4,32,512]{2,1,0:T(8,128)}, f32[4,32,512]{2,1,0:T(8,128)S(1)}, u32[]{:S(2)}) copy-start(f32[4,32,512]{2,1,0:T(8,128)S(1)} %collective-permute-done.3.refs_1_) | copy-start | bytes 786436

commit v6 on v5

--- a/solution.py
+++ b/solution.py
@@ -355,7 +355,7 @@
     return with_high[:32] + (with_high[32:] + mm(own_ref[rows_at : rows_at + 32], value[1]))
 
 
-def invert_x(spec_ref, factor_ref, edge_ref, own_ref, own_back, g, cols):
+def shifted(spec_ref, factor_ref, edge_ref, g, cols):
     fac = [factor_ref[g, p, :, cols] for p in range(2)]
     fac_edge = [jnp.concatenate([edge_ref[g, p, :, cols], fac[p][8:]], 0) for p in range(2)]
     s = [spec_ref[i, :, cols] for i in range(4)]
@@ -363,18 +363,34 @@
     down = (s[2] * fac_edge[0] - s[3] * fac_edge[1], s[2] * fac_edge[1] + s[3] * fac_edge[0])
     even = split(jnp.concatenate([up[p] + no_first(down[p], 0) for p in range(2)], 1))
     odd = split(jnp.concatenate([no_first(up[p], 0) - down[p] for p in range(2)], 1))
-    mine = plus_i(
-        halves_of(own_dot(own_ref, 0, even), 1, HALF),
-        halves_of(own_dot(own_ref, 64, odd), 1, HALF),
-    )
-    for p in range(2):
-        own_back[g, 32 * p : 32 * p + 32, cols] = mine[p]
     return even, odd
 
 
 def fold_columns(value):
     left, right = value[:, :HALF], value[:, HALF:]
     return split(left + no_first(right, 1)), split(no_first(left, 1) - right)
+
+
+def in_three(value):
+    high = value.astype(bf16)
+    rest = value - high.astype(f32)
+    mid = rest.astype(bf16)
+    return high, mid, (rest - mid.astype(f32)).astype(bf16)
+
+
+def own_image(slab, real_ref):
+    start = pl.multiple_of(32 * jnp.where(slab < 8, slab, 23 - slab), 32)
+    value = real_ref[pl.ds(start, 32), :]
+    at = lax.broadcasted_iota(jnp.int32, (32, 32), 0)
+    target = jnp.where(slab >= 8, 31 - at, at)
+    order = jnp.where(lanes((32, 32)) == target, 1.0, 0.0).astype(bf16)
+    pieces = in_three(value)
+    value = mm(order, pieces[0]) + mm(order, pieces[1]) + mm(order, pieces[2])
+    at = lax.broadcasted_iota(jnp.int32, (HALF, HALF), 0)
+    flip = jnp.where(at + lanes((HALF, HALF)) == HALF - 1, 1.0, 0.0).astype(bf16)
+    right = mm(jnp.concatenate(in_three(value[:, HALF:]), 0), flip)
+    right = right[:32] + right[32:64] + right[64:]
+    return jnp.concatenate([value[:, :HALF], right], 1)
 
 
 def own_field(step, own_back, waves_ref, velocity, slow_ref, freq_ref):
@@ -406,7 +422,7 @@
     slabs, refs = refs[:4], refs[4:]
     sources, wave_ref, out_ref = refs[:7], refs[7], refs[8]
     targets, slabs_ref, later_ref, sems = refs[9:16], *refs[16:19]
-    spec_ref, own_back, back_ref, half_ref = refs[19:]
+    spec_ref, own_back, back_ref, half_ref, real_ref = refs[19:]
     fetch = Fetch(
         [
             *sources[:2],
@@ -450,7 +466,7 @@
     for g in range(2):
         for c in range(2):
             cols = pl.ds(HALF * c, HALF)
-            even, odd = invert_x(spec_ref, factor_ref, edge_ref.at[0], own_ref, own_back, g, cols)
+            even, odd = shifted(spec_ref, factor_ref, edge_ref.at[0], g, cols)
             u = halves_of(dot3(wave_pair(waves_ref, 2), even), 1, HALF)
             v = halves_of(dot3(wave_pair(waves_ref, 3), odd), 1, HALF)
             first, second = plus_i(u, v), minus_i(u, v)
@@ -458,7 +474,6 @@
                 back_ref[g, p, :HALF, cols] = first[p]
                 back_ref[g, p, HALF:, cols] = second[p]
     vel_ref = fetch.take(6)
-    image = own_field(0, own_back, waves_ref, vel_ref[0], slow_ref, freq_ref)[0]
     fetch.take(7, 8, 9, 10)
 
     def some_rows(k, carry):
@@ -490,6 +505,8 @@
                     0,
                 )
             )
+        for side in range(2):
+            real_ref[at, HALF * side : HALF * side + HALF] = fields[side][:128]
         u = halves_of(dot3(split(fields[0] + fields[1]), wave_pair(waves_ref, 2)), 0, 128)
         v = halves_of(dot3(split(fields[0] - fields[1]), wave_pair(waves_ref, 3)), 0, 128)
         first = minus_i(u, [no_first(t, 1) for t in v])
@@ -515,13 +532,20 @@
 
     def invert(k, carry):
         cols = pl.ds(pl.multiple_of((k & 1) * HALF, HALF), HALF)
-        invert_x(spec_ref, later_factor, edge_ref.at[1], own_ref, own_back, k >> 1, cols)
+        even, odd = shifted(spec_ref, later_factor, edge_ref.at[1], k >> 1, cols)
+        mine = plus_i(
+            halves_of(own_dot(own_ref, 0, even), 1, HALF),
+            halves_of(own_dot(own_ref, 64, odd), 1, HALF),
+        )
+        for p in range(2):
+            own_back[k >> 1, 32 * p : 32 * p + 32, cols] = mine[p]
         return carry
 
     lax.fori_loop(0, 4, invert, 0)
     field = own_field(1, own_back, waves_ref, vel_ref[1], slow_ref, freq_ref)
     for p in range(2):
         wave_ref[p] = field[p]
+    image = own_image(lat_ref[0], real_ref)
     upper = lanes((32, 128)) >= 64
     for d in range(8):
         col, pos = d // 2, d % 2
@@ -622,6 +646,7 @@
             pltpu.VMEM((2, 64, 512), f32),
             pltpu.VMEM((2, 2, 512, 512), f32),
             pltpu.VMEM((2, 512, 512), f32),
+            pltpu.VMEM((512, 512), f32),
         ],
     )(
         lat_at,

time: 79.8 us -> 78.7 us (0.986)
  Pallas kernels: 29.8 us -> 28.7 us
    pallas_call x1, Pallas kernels: 15.9 us -> 14.7 us  [local(): call(grid_kernel, [(2, 32, 512), (8, 32, 128)], [SM, SM, SM, VM] + [HBM]...]
where the time goes in v6:
time: 78.7 us; the launch traced here: 78.3 us
  Pallas kernels  28.7 us (36%)
  starting transfers between devices  25.2 us (32%)
  waiting for transfers between devices  12.3 us (16%)
  blocking collectives  9 us (11%)
  local copies, waits for them, and re-layouts  1.76 us (2%)
  between operations  1.38 us (2%)
    pallas_call x1, Pallas kernels, local(): call(grid_kernel, [(2, 32, 512), (8, 32, 128)], [SM, SM, SM, VM] + [HBM]...  14.7 us
    all_to_all x1, starting transfers between devices, local(): got = lax.all_to_all(sent.reshape(128, 4, 128), everyone, 0, 0, tiled=True)  11.5 us
    all_to_all x1, blocking collectives, local(): got = lax.all_to_all(sent, 'freq', 0, 0, tiled=True)  9 us
    all_to_all x1, starting transfers between devices, local(): got = lax.all_to_all(sent.reshape(128, 2, 128), everyone, 0, 0, tiled=True)  6.98 us
    pallas_call x1, Pallas kernels, local(): call(factor_kernel, [(2, 2, 2, 256, 512), (2, 2, 2, 8, 512)], [SM, SM], 5...  5.34 us
    pallas_call x1, Pallas kernels, local(): call(solve_kernel, [(256, 128), (4, 32, 512)], [SM, VM] + [HBM] * 4, 24,...  5.17 us
    ppermute x3, waiting for transfers between devices, local(): lax.ppermute(velocity, 'lat', [(i, i ^ d) for i in range(16)])  4.46 us
    all_to_all x1, waiting for transfers between devices, local(): got = lax.all_to_all(sent.reshape(128, 2, 128), everyone, 0, 0, tiled=True)  4.21 us
  transfers between devices with their start and end apart: 8, of which 4 were waited for; matrix products, arithmetic and copies ran while one was open for 0% of the time, Pallas kernels for 7%

profile of v6, /device:TPU:1, one launch (start us, length us, event | category | flops | bytes accessed | tf_op | source)
XLA Modules:
  0.0 78.3 jit_solution(1501728828735604501)
XLA Ops:
  0.6 2.7 %shard_map.131 = (f32[512,128]{1,0:T(8,128)}, f32[32,512]{1,0:T(8,128)}) custom-call(s32[1]{0:T(128)} %bitcast.lat_ref, s32[1,1024]{1,0:T(1,128)} %bitcast.16, s32[1,1024]{1,0:T(1,128)} %bitcast.17, f32[2,1024]{1,0:T(2,128)} %refs_2_.1, f32[1,1024]{1,0:T(1,128)} %bitcast.18, f32[16,1024]{1,0:T(8,128)} %bitcast.15, s32[2,32,512]{2,1,0:T(8,128)} %refs_10_.1), custom_call_target="tpu_custom_call" | custom-call | tf_op jit(solution)/shard_map/pallas_call | solution.py:582
  3.4 11.5 %all-to-all-start = ((f32[128,4,128]{2,1,0:T(4,128)}), f32[128,4,128]{2,1,0:T(4,128)S(1)}, u32[]{:S(2)}, u32[]{:S(2)}) async-start(f32[128,4,128]{2,1,0:T(4,128)} %bitcast.14), calls=%async_computation | async-start | bytes 524288 | tf_op jit(solution)/shard_map/all_to_all | solution.py:605
  14.9 2.7 %collective-permute-start.2 = (f32[32,512]{1,0:T(8,128)}, f32[32,512]{1,0:T(8,128)S(1)}, u32[]{:S(2)}, u32[]{:S(2)}) collective-permute-start(f32[32,512]{1,0:T(8,128)} %get-tuple-element.11.refs_0_), channel_id=1, source_target_pairs={{0,3},{1,2},{2,1},{3,0},{4,7},{5,6},{6,5},{7,4},{8,11},{9,10},{10,... | collective-permute-start | bytes 196616 | tf_op jit(solution)/shard_map/ppermute | solution.py:607
  17.6 0.6 collective-permute-start.1
  18.1 0.1 collective-permute-start
  18.2 3.6 %collective-permute-done.2.refs_3_ = f32[32,512]{1,0:T(8,128)S(1)} collective-permute-done((f32[32,512]{1,0:T(8,128)}, f32[32,512]{1,0:T(8,128)S(1)}, u32[]{:S(2)}, u32[]{:S(2)}) %collective-permute-start.2) | collective-permute-done | bytes 65568 | tf_op jit(solution)/shard_map/ppermute | solution.py:607
  21.9 0.8 %collective-permute-done.1.refs_2_ = f32[32,512]{1,0:T(8,128)S(1)} collective-permute-done((f32[32,512]{1,0:T(8,128)}, f32[32,512]{1,0:T(8,128)S(1)}, u32[]{:S(2)}, u32[]{:S(2)}) %collective-permute-start.1) | collective-permute-done | bytes 65568 | tf_op jit(solution)/shard_map/ppermute | solution.py:607
  22.7 0.0 collective-permute-done.refs_1_
  22.7 3.7 %all-to-all-done = f32[128,4,128]{2,1,0:T(4,128)S(1)} async-done(((f32[128,4,128]{2,1,0:T(4,128)}), f32[128,4,128]{2,1,0:T(4,128)S(1)}, u32[]{:S(2)}, u32[]{:S(2)}) %all-to-all-start) | async-done | bytes 262176 | tf_op jit(solution)/shard_map/all_to_all | solution.py:605
  26.4 0.0 copy-start.1
  26.4 0.8 %copy-done.1 = f32[32,512]{1,0:T(8,128)S(1)} copy-done((f32[32,512]{1,0:T(8,128)S(1)}, f32[32,512]{1,0:T(8,128)}, u32[]{:S(2)}) %copy-start.1) | copy-done | bytes 65560
  27.2 5.2 %shard_map.132 = (f32[256,128]{1,0:T(8,128)}, f32[4,32,512]{2,1,0:T(8,128)S(1)}) custom-call(s32[1]{0:T(128)} %bitcast.lat_ref, f32[512,128]{1,0:T(8,128)S(1)} %bitcast.12, f32[32,512]{1,0:T(8,128)S(1)} %copy-done.1, f32[32,512]{1,0:T(8,128)S(1)} %collective-permute-done.refs_1_, f32[32,512]{1,0:T(8,128)S(1)} %collective-permute-done.1.refs_2_, ...), custom_call_target="tpu_custom_call" | custom-call | tf_op jit(solution)/shard_map/pallas_call | solution.py:609
  32.4 0.0 copy-start
  32.4 0.4 collective-permute-start.5
  32.8 1.3 %collective-permute-start.4 = (f32[4,32,512]{2,1,0:T(8,128)S(1)}, f32[4,32,512]{2,1,0:T(8,128)S(1)}, u32[]{:S(2)}, u32[]{:S(2)}) collective-permute-start(f32[4,32,512]{2,1,0:T(8,128)S(1)} %get-tuple-element.13.refs_0_), channel_id=1, source_target_pairs={{0,8},{1,9},{2,10},{3,11},{4,12},{5,13},{6,14},{7,15},{8,0},{9,1},... | collective-permute-start | bytes 786440 | tf_op jit(solution)/shard_map/ppermute | solution.py:619
  34.0 1.7 %collective-permute-start.3 = (f32[4,32,512]{2,1,0:T(8,128)S(1)}, f32[4,32,512]{2,1,0:T(8,128)S(1)}, u32[]{:S(2)}, u32[]{:S(2)}) collective-permute-start(f32[4,32,512]{2,1,0:T(8,128)S(1)} %get-tuple-element.13.refs_0_), channel_id=1, source_target_pairs={{0,4},{1,5},{2,6},{3,7},{4,0},{5,1},{6,2},{7,3},{8,12},{9,13},{10,... | collective-permute-start | bytes 786440 | tf_op jit(solution)/shard_map/ppermute | solution.py:619
  35.7 7.0 %all-to-all-start.1 = ((f32[128,2,128]{2,1,0:T(2,128)}), f32[128,2,128]{2,1,0:T(2,128)S(1)}, u32[]{:S(2)}, u32[]{:S(2)}) async-start(f32[128,2,128]{2,1,0:T(2,128)} %bitcast.7), calls=%async_computation.1 | async-start | bytes 262144 | tf_op jit(solution)/shard_map/all_to_all | solution.py:617
  43.4 5.3 %shard_map.133 = (f32[2,2,2,256,512]{4,3,2,1,0:T(8,128)}, f32[2,2,2,8,512]{4,3,2,1,0:T(8,128)}) custom-call(f32[1]{0:T(128)S(6)} %copy.15.freq_ref, f32[2,8]{1,0:T(2,128)} %slow_ref.3), custom_call_target="tpu_custom_call" | custom-call | tf_op jit(solution)/shard_map/pallas_call | solution.py:621
  48.7 4.2 %all-to-all-done.1 = f32[128,2,128]{2,1,0:T(2,128)S(1)} async-done(((f32[128,2,128]{2,1,0:T(2,128)}), f32[128,2,128]{2,1,0:T(2,128)S(1)}, u32[]{:S(2)}, u32[]{:S(2)}) %all-to-all-start.1) | async-done | bytes 131104 | tf_op jit(solution)/shard_map/all_to_all | solution.py:617
  52.9 0.0 collective-permute-done.5.refs_3_
  52.9 0.0 collective-permute-done.4.refs_2_
  52.9 0.0 copy-start.4
  52.9 0.0 collective-permute-done.3.refs_1_
  52.9 0.0 copy-start.5
  53.0 0.0 copy-done
  53.0 0.6 copy-done.2
  53.6 0.1 copy-done.3
  53.7 0.1 copy-done.4
  53.8 0.1 copy-done.5
  53.9 14.7 %shard_map.134 = (f32[2,32,512]{2,1,0:T(8,128)}, f32[8,32,128]{2,1,0:T(8,128)}) custom-call(s32[1]{0:T(128)} %bitcast.lat_ref, f32[1]{0:T(128)S(6)} %copy.15.freq_ref, f32[2,8]{1,0:T(2,128)} %slow_ref.3, f32[256,128]{1,0:T(8,128)} %bitcast.13, f32[4,32,512]{2,1,0:T(8,128)} %copy-done, f32[4,32,512]{2,1,0:T(8,128)} %copy-done.5, f32[4,32,512]{2,1,0:T(8,128)} %copy-done.4, ...), custom_call_target="tpu_custom_call" | custom-call | tf_op jit(solution)/shard_map/pallas_call | solution.py:629
  68.6 9.0 %all_to_all.15.got_ref = f32[8,32,128]{2,1,0:T(8,128)S(1)} all-to-all(f32[8,32,128]{2,1,0:T(8,128)} %get-tuple-element.17), channel_id=1, replica_groups=mesh['freq'=8,'lat'=16] {'freq'}, dimensions={0} | all-to-all | bytes 262144 | tf_op jit(solution)/shard_map/all_to_all | solution.py:665
  77.6 0.7 shard_map.135
  (2 shorter events, 0.0 us)
Async XLA Ops:
  3.4 23.0 %all-to-all-start = ((f32[128,4,128]{2,1,0:T(4,128)}), f32[128,4,128]{2,1,0:T(4,128)S(1)}, u32[]{:S(2)}, u32[]{:S(2)}) async-start(f32[128,4,128]{2,1,0:T(4,128)} %bitcast.14), calls=%async_computation | async-start | bytes 524288 | tf_op jit(solution)/shard_map/all_to_all | solution.py:605
  14.9 7.0 %collective-permute-start.2 = (f32[32,512]{1,0:T(8,128)}, f32[32,512]{1,0:T(8,128)S(1)}, u32[]{:S(2)}, u32[]{:S(2)}) collective-permute-start(f32[32,512]{1,0:T(8,128)} %get-tuple-element.11.refs_0_), channel_id=1, source_target_pairs={{0,3},{1,2},{2,1},{3,0},{4,7},{5,6},{6,5},{7,4},{8,11},{9,10},{10,... | collective-permute-start | bytes 196616 | tf_op jit(solution)/shard_map/ppermute | solution.py:607
  17.6 5.1 %collective-permute-start.1 = (f32[32,512]{1,0:T(8,128)}, f32[32,512]{1,0:T(8,128)S(1)}, u32[]{:S(2)}, u32[]{:S(2)}) collective-permute-start(f32[32,512]{1,0:T(8,128)} %get-tuple-element.11.refs_0_), channel_id=1, source_target_pairs={{0,2},{1,3},{2,0},{3,1},{4,6},{5,7},{6,4},{7,5},{8,10},{9,11},{10,... | collective-permute-start | bytes 196616 | tf_op jit(solution)/shard_map/ppermute | solution.py:607
  18.1 4.6 %collective-permute-start = (f32[32,512]{1,0:T(8,128)}, f32[32,512]{1,0:T(8,128)S(1)}, u32[]{:S(2)}, u32[]{:S(2)}) collective-permute-start(f32[32,512]{1,0:T(8,128)} %get-tuple-element.11.refs_0_), channel_id=1, source_target_pairs={{0,1},{1,0},{2,3},{3,2},{4,5},{5,4},{6,7},{7,6},{8,9},{9,8},{10,11... | collective-permute-start | bytes 196616 | tf_op jit(solution)/shard_map/ppermute | solution.py:607
  26.4 0.8 %copy-start.1 = (f32[32,512]{1,0:T(8,128)S(1)}, f32[32,512]{1,0:T(8,128)}, u32[]{:S(2)}) copy-start(f32[32,512]{1,0:T(8,128)} %get-tuple-element.11.refs_0_) | copy-start | bytes 196612
  32.4 20.6 %copy-start = (f32[4,32,512]{2,1,0:T(8,128)}, f32[4,32,512]{2,1,0:T(8,128)S(1)}, u32[]{:S(2)}) copy-start(f32[4,32,512]{2,1,0:T(8,128)S(1)} %get-tuple-element.13.refs_0_) | copy-start | bytes 786436
  32.4 20.5 %collective-permute-start.5 = (f32[4,32,512]{2,1,0:T(8,128)S(1)}, f32[4,32,512]{2,1,0:T(8,128)S(1)}, u32[]{:S(2)}, u32[]{:S(2)}) collective-permute-start(f32[4,32,512]{2,1,0:T(8,128)S(1)} %get-tuple-element.13.refs_0_), channel_id=1, source_target_pairs={{0,12},{1,13},{2,14},{3,15},{4,8},{5,9},{6,10},{7,11},{8,4},{9,5},... | collective-permute-start | bytes 786440 | tf_op jit(solution)/shard_map/ppermute | solution.py:619
  32.8 20.2 %collective-permute-start.4 = (f32[4,32,512]{2,1,0:T(8,128)S(1)}, f32[4,32,512]{2,1,0:T(8,128)S(1)}, u32[]{:S(2)}, u32[]{:S(2)}) collective-permute-start(f32[4,32,512]{2,1,0:T(8,128)S(1)} %get-tuple-element.13.refs_0_), channel_id=1, source_target_pairs={{0,8},{1,9},{2,10},{3,11},{4,12},{5,13},{6,14},{7,15},{8,0},{9,1},... | collective-permute-start | bytes 786440 | tf_op jit(solution)/shard_map/ppermute | solution.py:619
  34.0 18.9 %collective-permute-start.3 = (f32[4,32,512]{2,1,0:T(8,128)S(1)}, f32[4,32,512]{2,1,0:T(8,128)S(1)}, u32[]{:S(2)}, u32[]{:S(2)}) collective-permute-start(f32[4,32,512]{2,1,0:T(8,128)S(1)} %get-tuple-element.13.refs_0_), channel_id=1, source_target_pairs={{0,4},{1,5},{2,6},{3,7},{4,0},{5,1},{6,2},{7,3},{8,12},{9,13},{10,... | collective-permute-start | bytes 786440 | tf_op jit(solution)/shard_map/ppermute | solution.py:619
  35.7 17.2 %all-to-all-start.1 = ((f32[128,2,128]{2,1,0:T(2,128)}), f32[128,2,128]{2,1,0:T(2,128)S(1)}, u32[]{:S(2)}, u32[]{:S(2)}) async-start(f32[128,2,128]{2,1,0:T(2,128)} %bitcast.7), calls=%async_computation.1 | async-start | bytes 262144 | tf_op jit(solution)/shard_map/all_to_all | solution.py:617
  52.9 0.7 copy-start.2
  52.9 0.7 copy-start.3
  52.9 0.8 %copy-start.4 = (f32[4,32,512]{2,1,0:T(8,128)}, f32[4,32,512]{2,1,0:T(8,128)S(1)}, u32[]{:S(2)}) copy-start(f32[4,32,512]{2,1,0:T(8,128)S(1)} %collective-permute-done.4.refs_2_) | copy-start | bytes 786436
  52.9 0.9 %copy-start.5 = (f32[4,32,512]{2,1,0:T(8,128)}, f32[4,32,512]{2,1,0:T(8,128)S(1)}, u32[]{:S(2)}) copy-start(f32[4,32,512]{2,1,0:T(8,128)S(1)} %collective-permute-done.3.refs_1_) | copy-start | bytes 786436

commit v7 on v6

--- a/solution.py
+++ b/solution.py
@@ -233,7 +233,7 @@
 def factor_rows(wave_sq, kx, ky, ky_mirror):
     first = shift_factor(wave_sq, kx, ky)
     mirror = shift_factor(wave_sq, kx[:, :128], ky_mirror)
-    return [jnp.concatenate([first[p], mirror[p], first[p][:, 128:]], 1) for p in range(2)]
+    return [jnp.concatenate([first[p], mirror[p]], 1) for p in range(2)]
 
 
 def factor_kernel(freq_ref, slow_ref, factor_hbm, edge_ref, factor_ref, sems):
@@ -355,9 +355,14 @@
     return with_high[:32] + (with_high[32:] + mm(own_ref[rows_at : rows_at + 32], value[1]))
 
 
-def shifted(spec_ref, factor_ref, edge_ref, g, cols):
-    fac = [factor_ref[g, p, :, cols] for p in range(2)]
-    fac_edge = [jnp.concatenate([edge_ref[g, p, :, cols], fac[p][8:]], 0) for p in range(2)]
+def shifted(spec_ref, factor_ref, edge_ref, g, start):
+    cols, side = pl.ds(start, HALF), pl.ds(start, 128)
+
+    def both_sides(ref, p):
+        return jnp.concatenate([ref[g, p, :, side], ref[g, p, :, 128:HALF]], 1)
+
+    fac = [both_sides(factor_ref, p) for p in range(2)]
+    fac_edge = [jnp.concatenate([both_sides(edge_ref, p), fac[p][8:]], 0) for p in range(2)]
     s = [spec_ref[i, :, cols] for i in range(4)]
     up = (s[0] * fac[0] - s[1] * fac[1], s[0] * fac[1] + s[1] * fac[0])
     down = (s[2] * fac_edge[0] - s[3] * fac_edge[1], s[2] * fac_edge[1] + s[3] * fac_edge[0])
@@ -466,7 +471,7 @@
     for g in range(2):
         for c in range(2):
             cols = pl.ds(HALF * c, HALF)
-            even, odd = shifted(spec_ref, factor_ref, edge_ref.at[0], g, cols)
+            even, odd = shifted(spec_ref, factor_ref, edge_ref.at[0], g, HALF * c)
             u = halves_of(dot3(wave_pair(waves_ref, 2), even), 1, HALF)
             v = halves_of(dot3(wave_pair(waves_ref, 3), odd), 1, HALF)
             first, second = plus_i(u, v), minus_i(u, v)
@@ -531,8 +536,9 @@
     later_factor = fetch.take(11)
 
     def invert(k, carry):
-        cols = pl.ds(pl.multiple_of((k & 1) * HALF, HALF), HALF)
-        even, odd = shifted(spec_ref, later_factor, edge_ref.at[1], k >> 1, cols)
+        start = pl.multiple_of((k & 1) * HALF, HALF)
+        cols = pl.ds(start, HALF)
+        even, odd = shifted(spec_ref, later_factor, edge_ref.at[1], k >> 1, start)
         mine = plus_i(
             halves_of(own_dot(own_ref, 0, even), 1, HALF),
             halves_of(own_dot(own_ref, 64, odd), 1, HALF),
@@ -620,10 +626,10 @@
     ]
     factor, edge = call(
         factor_kernel,
-        [(2, 2, 2, 256, 512), (2, 2, 2, 8, 512)],
+        [(2, 2, 2, 256, 384), (2, 2, 2, 8, 384)],
         [SM, SM],
         59,
-        [pltpu.VMEM((2, 2, 2, 256, 512), f32), pltpu.SemaphoreType.DMA((4,))],
+        [pltpu.VMEM((2, 2, 2, 256, 384), f32), pltpu.SemaphoreType.DMA((4,))],
         [HBM, VM],
     )(frequency, slowness)
     wave, sent = call(
@@ -635,12 +641,12 @@
             pltpu.VMEM((2, 128, 512), bf16),
             pltpu.VMEM((2, 512, 128), bf16),
             pltpu.VMEM((128, 256), bf16),
-            pltpu.VMEM((2, 2, 256, 512), f32),
-            pltpu.VMEM((2, 2, 2, 8, 512), f32),
+            pltpu.VMEM((2, 2, 256, 384), f32),
+            pltpu.VMEM((2, 2, 2, 8, 384), f32),
             pltpu.VMEM((2, 6, 256, 256), bf16),
             pltpu.VMEM((2, 32, 512), jnp.int32),
             pltpu.VMEM((4, 4, 32, 512), f32),
-            pltpu.VMEM((2, 2, 256, 512), f32),
+            pltpu.VMEM((2, 2, 256, 384), f32),
             pltpu.SemaphoreType.DMA((12,)),
             pltpu.VMEM((4, 256, 512), f32),
             pltpu.VMEM((2, 64, 512), f32),

time: 78.7 us -> 78.5 us (level)
  no operation moved by 1% of the time
where the time goes in v7:
time: 78.5 us; the launch traced here: 78.1 us
  Pallas kernels  28.3 us (36%)
  starting transfers between devices  25.2 us (32%)
  waiting for transfers between devices  12.5 us (16%)
  blocking collectives  9.02 us (11%)
  local copies, waits for them, and re-layouts  1.72 us (2%)
  between operations  1.38 us (2%)
    pallas_call x1, Pallas kernels, local(): call(grid_kernel, [(2, 32, 512), (8, 32, 128)], [SM, SM, SM, VM] + [HBM]...  14.5 us
    all_to_all x1, starting transfers between devices, local(): got = lax.all_to_all(sent.reshape(128, 4, 128), everyone, 0, 0, tiled=True)  11.5 us
    all_to_all x1, blocking collectives, local(): got = lax.all_to_all(sent, 'freq', 0, 0, tiled=True)  9.02 us
    all_to_all x1, starting transfers between devices, local(): got = lax.all_to_all(sent.reshape(128, 2, 128), everyone, 0, 0, tiled=True)  6.98 us
    pallas_call x1, Pallas kernels, local(): call(factor_kernel, [(2, 2, 2, 256, 384), (2, 2, 2, 8, 384)], [SM, SM], 5...  5.21 us
    pallas_call x1, Pallas kernels, local(): call(solve_kernel, [(256, 128), (4, 32, 512)], [SM, VM] + [HBM] * 4, 24,...  5.17 us
    ppermute x3, waiting for transfers between devices, local(): lax.ppermute(velocity, 'lat', [(i, i ^ d) for i in range(16)])  4.46 us
    all_to_all x1, waiting for transfers between devices, local(): got = lax.all_to_all(sent.reshape(128, 2, 128), everyone, 0, 0, tiled=True)  4.33 us
  transfers between devices with their start and end apart: 8, of which 4 were waited for; matrix products, arithmetic and copies ran while one was open for 0% of the time, Pallas kernels for 7%

profile of v7, /device:TPU:1, one launch (start us, length us, event | category | flops | bytes accessed | tf_op | source)
XLA Modules:
  0.0 78.1 jit_solution(16545368585749125020)
XLA Ops:
  0.6 2.7 %shard_map.131 = (f32[512,128]{1,0:T(8,128)}, f32[32,512]{1,0:T(8,128)}) custom-call(s32[1]{0:T(128)} %bitcast.lat_ref, s32[1,1024]{1,0:T(1,128)} %bitcast.16, s32[1,1024]{1,0:T(1,128)} %bitcast.17, f32[2,1024]{1,0:T(2,128)} %refs_2_.1, f32[1,1024]{1,0:T(1,128)} %bitcast.18, f32[16,1024]{1,0:T(8,128)} %bitcast.15, s32[2,32,512]{2,1,0:T(8,128)} %refs_10_.1), custom_call_target="tpu_custom_call" | custom-call | tf_op jit(solution)/shard_map/pallas_call | solution.py:588
  3.4 11.5 %all-to-all-start = ((f32[128,4,128]{2,1,0:T(4,128)}), f32[128,4,128]{2,1,0:T(4,128)S(1)}, u32[]{:S(2)}, u32[]{:S(2)}) async-start(f32[128,4,128]{2,1,0:T(4,128)} %bitcast.14), calls=%async_computation | async-start | bytes 524288 | tf_op jit(solution)/shard_map/all_to_all | solution.py:611
  14.9 2.7 %collective-permute-start.2 = (f32[32,512]{1,0:T(8,128)}, f32[32,512]{1,0:T(8,128)S(1)}, u32[]{:S(2)}, u32[]{:S(2)}) collective-permute-start(f32[32,512]{1,0:T(8,128)} %get-tuple-element.11.refs_0_), channel_id=1, source_target_pairs={{0,3},{1,2},{2,1},{3,0},{4,7},{5,6},{6,5},{7,4},{8,11},{9,10},{10,... | collective-permute-start | bytes 196616 | tf_op jit(solution)/shard_map/ppermute | solution.py:613
  17.6 0.6 collective-permute-start.1
  18.1 0.1 collective-permute-start
  18.2 3.6 %collective-permute-done.2.refs_3_ = f32[32,512]{1,0:T(8,128)S(1)} collective-permute-done((f32[32,512]{1,0:T(8,128)}, f32[32,512]{1,0:T(8,128)S(1)}, u32[]{:S(2)}, u32[]{:S(2)}) %collective-permute-start.2) | collective-permute-done | bytes 65568 | tf_op jit(solution)/shard_map/ppermute | solution.py:613
  21.9 0.8 %collective-permute-done.1.refs_2_ = f32[32,512]{1,0:T(8,128)S(1)} collective-permute-done((f32[32,512]{1,0:T(8,128)}, f32[32,512]{1,0:T(8,128)S(1)}, u32[]{:S(2)}, u32[]{:S(2)}) %collective-permute-start.1) | collective-permute-done | bytes 65568 | tf_op jit(solution)/shard_map/ppermute | solution.py:613
  22.7 0.0 collective-permute-done.refs_1_
  22.7 3.7 %all-to-all-done = f32[128,4,128]{2,1,0:T(4,128)S(1)} async-done(((f32[128,4,128]{2,1,0:T(4,128)}), f32[128,4,128]{2,1,0:T(4,128)S(1)}, u32[]{:S(2)}, u32[]{:S(2)}) %all-to-all-start) | async-done | bytes 262176 | tf_op jit(solution)/shard_map/all_to_all | solution.py:611
  26.4 0.0 copy-start.1
  26.4 0.8 %copy-done.1 = f32[32,512]{1,0:T(8,128)S(1)} copy-done((f32[32,512]{1,0:T(8,128)S(1)}, f32[32,512]{1,0:T(8,128)}, u32[]{:S(2)}) %copy-start.1) | copy-done | bytes 65560
  27.2 5.2 %shard_map.132 = (f32[256,128]{1,0:T(8,128)}, f32[4,32,512]{2,1,0:T(8,128)S(1)}) custom-call(s32[1]{0:T(128)} %bitcast.lat_ref, f32[512,128]{1,0:T(8,128)S(1)} %bitcast.12, f32[32,512]{1,0:T(8,128)S(1)} %copy-done.1, f32[32,512]{1,0:T(8,128)S(1)} %collective-permute-done.refs_1_, f32[32,512]{1,0:T(8,128)S(1)} %collective-permute-done.1.refs_2_, ...), custom_call_target="tpu_custom_call" | custom-call | tf_op jit(solution)/shard_map/pallas_call | solution.py:615
  32.4 0.0 copy-start
  32.4 0.4 collective-permute-start.5
  32.8 1.3 %collective-permute-start.4 = (f32[4,32,512]{2,1,0:T(8,128)S(1)}, f32[4,32,512]{2,1,0:T(8,128)S(1)}, u32[]{:S(2)}, u32[]{:S(2)}) collective-permute-start(f32[4,32,512]{2,1,0:T(8,128)S(1)} %get-tuple-element.13.refs_0_), channel_id=1, source_target_pairs={{0,8},{1,9},{2,10},{3,11},{4,12},{5,13},{6,14},{7,15},{8,0},{9,1},... | collective-permute-start | bytes 786440 | tf_op jit(solution)/shard_map/ppermute | solution.py:625
  34.0 1.7 %collective-permute-start.3 = (f32[4,32,512]{2,1,0:T(8,128)S(1)}, f32[4,32,512]{2,1,0:T(8,128)S(1)}, u32[]{:S(2)}, u32[]{:S(2)}) collective-permute-start(f32[4,32,512]{2,1,0:T(8,128)S(1)} %get-tuple-element.13.refs_0_), channel_id=1, source_target_pairs={{0,4},{1,5},{2,6},{3,7},{4,0},{5,1},{6,2},{7,3},{8,12},{9,13},{10,... | collective-permute-start | bytes 786440 | tf_op jit(solution)/shard_map/ppermute | solution.py:625
  35.7 7.0 %all-to-all-start.1 = ((f32[128,2,128]{2,1,0:T(2,128)}), f32[128,2,128]{2,1,0:T(2,128)S(1)}, u32[]{:S(2)}, u32[]{:S(2)}) async-start(f32[128,2,128]{2,1,0:T(2,128)} %bitcast.7), calls=%async_computation.1 | async-start | bytes 262144 | tf_op jit(solution)/shard_map/all_to_all | solution.py:623
  43.4 5.2 %shard_map.133 = (f32[2,2,2,256,384]{4,3,2,1,0:T(8,128)}, f32[2,2,2,8,384]{4,3,2,1,0:T(8,128)}) custom-call(f32[1]{0:T(128)S(6)} %copy.15.freq_ref, f32[2,8]{1,0:T(2,128)} %slow_ref.3), custom_call_target="tpu_custom_call" | custom-call | tf_op jit(solution)/shard_map/pallas_call | solution.py:627
  48.6 4.3 %all-to-all-done.1 = f32[128,2,128]{2,1,0:T(2,128)S(1)} async-done(((f32[128,2,128]{2,1,0:T(2,128)}), f32[128,2,128]{2,1,0:T(2,128)S(1)}, u32[]{:S(2)}, u32[]{:S(2)}) %all-to-all-start.1) | async-done | bytes 131104 | tf_op jit(solution)/shard_map/all_to_all | solution.py:623
  52.9 0.0 collective-permute-done.5.refs_3_
  52.9 0.0 collective-permute-done.4.refs_2_
  52.9 0.0 copy-start.4
  52.9 0.0 collective-permute-done.3.refs_1_
  52.9 0.0 copy-start.5
  53.0 0.0 copy-done
  53.0 0.6 copy-done.2
  53.6 0.1 copy-done.3
  53.7 0.1 copy-done.4
  53.8 0.1 copy-done.5
  53.8 14.5 %shard_map.134 = (f32[2,32,512]{2,1,0:T(8,128)}, f32[8,32,128]{2,1,0:T(8,128)}) custom-call(s32[1]{0:T(128)} %bitcast.lat_ref, f32[1]{0:T(128)S(6)} %copy.15.freq_ref, f32[2,8]{1,0:T(2,128)} %slow_ref.3, f32[256,128]{1,0:T(8,128)} %bitcast.13, f32[4,32,512]{2,1,0:T(8,128)} %copy-done, f32[4,32,512]{2,1,0:T(8,128)} %copy-done.5, f32[4,32,512]{2,1,0:T(8,128)} %copy-done.4, ...), custom_call_target="tpu_custom_call" | custom-call | tf_op jit(solution)/shard_map/pallas_call | solution.py:635
  68.4 9.0 %all_to_all.15.got_ref = f32[8,32,128]{2,1,0:T(8,128)S(1)} all-to-all(f32[8,32,128]{2,1,0:T(8,128)} %get-tuple-element.17), channel_id=1, replica_groups=mesh['freq'=8,'lat'=16] {'freq'}, dimensions={0} | all-to-all | bytes 262144 | tf_op jit(solution)/shard_map/all_to_all | solution.py:671
  77.4 0.7 shard_map.135
  (2 shorter events, 0.0 us)
Async XLA Ops:
  3.4 23.0 %all-to-all-start = ((f32[128,4,128]{2,1,0:T(4,128)}), f32[128,4,128]{2,1,0:T(4,128)S(1)}, u32[]{:S(2)}, u32[]{:S(2)}) async-start(f32[128,4,128]{2,1,0:T(4,128)} %bitcast.14), calls=%async_computation | async-start | bytes 524288 | tf_op jit(solution)/shard_map/all_to_all | solution.py:611
  14.9 7.0 %collective-permute-start.2 = (f32[32,512]{1,0:T(8,128)}, f32[32,512]{1,0:T(8,128)S(1)}, u32[]{:S(2)}, u32[]{:S(2)}) collective-permute-start(f32[32,512]{1,0:T(8,128)} %get-tuple-element.11.refs_0_), channel_id=1, source_target_pairs={{0,3},{1,2},{2,1},{3,0},{4,7},{5,6},{6,5},{7,4},{8,11},{9,10},{10,... | collective-permute-start | bytes 196616 | tf_op jit(solution)/shard_map/ppermute | solution.py:613
  17.6 5.1 %collective-permute-start.1 = (f32[32,512]{1,0:T(8,128)}, f32[32,512]{1,0:T(8,128)S(1)}, u32[]{:S(2)}, u32[]{:S(2)}) collective-permute-start(f32[32,512]{1,0:T(8,128)} %get-tuple-element.11.refs_0_), channel_id=1, source_target_pairs={{0,2},{1,3},{2,0},{3,1},{4,6},{5,7},{6,4},{7,5},{8,10},{9,11},{10,... | collective-permute-start | bytes 196616 | tf_op jit(solution)/shard_map/ppermute | solution.py:613
  18.1 4.6 %collective-permute-start = (f32[32,512]{1,0:T(8,128)}, f32[32,512]{1,0:T(8,128)S(1)}, u32[]{:S(2)}, u32[]{:S(2)}) collective-permute-start(f32[32,512]{1,0:T(8,128)} %get-tuple-element.11.refs_0_), channel_id=1, source_target_pairs={{0,1},{1,0},{2,3},{3,2},{4,5},{5,4},{6,7},{7,6},{8,9},{9,8},{10,11... | collective-permute-start | bytes 196616 | tf_op jit(solution)/shard_map/ppermute | solution.py:613
  26.4 0.8 %copy-start.1 = (f32[32,512]{1,0:T(8,128)S(1)}, f32[32,512]{1,0:T(8,128)}, u32[]{:S(2)}) copy-start(f32[32,512]{1,0:T(8,128)} %get-tuple-element.11.refs_0_) | copy-start | bytes 196612
  32.4 20.6 %copy-start = (f32[4,32,512]{2,1,0:T(8,128)}, f32[4,32,512]{2,1,0:T(8,128)S(1)}, u32[]{:S(2)}) copy-start(f32[4,32,512]{2,1,0:T(8,128)S(1)} %get-tuple-element.13.refs_0_) | copy-start | bytes 786436
  32.4 20.5 %collective-permute-start.5 = (f32[4,32,512]{2,1,0:T(8,128)S(1)}, f32[4,32,512]{2,1,0:T(8,128)S(1)}, u32[]{:S(2)}, u32[]{:S(2)}) collective-permute-start(f32[4,32,512]{2,1,0:T(8,128)S(1)} %get-tuple-element.13.refs_0_), channel_id=1, source_target_pairs={{0,12},{1,13},{2,14},{3,15},{4,8},{5,9},{6,10},{7,11},{8,4},{9,5},... | collective-permute-start | bytes 786440 | tf_op jit(solution)/shard_map/ppermute | solution.py:625
  32.8 20.2 %collective-permute-start.4 = (f32[4,32,512]{2,1,0:T(8,128)S(1)}, f32[4,32,512]{2,1,0:T(8,128)S(1)}, u32[]{:S(2)}, u32[]{:S(2)}) collective-permute-start(f32[4,32,512]{2,1,0:T(8,128)S(1)} %get-tuple-element.13.refs_0_), channel_id=1, source_target_pairs={{0,8},{1,9},{2,10},{3,11},{4,12},{5,13},{6,14},{7,15},{8,0},{9,1},... | collective-permute-start | bytes 786440 | tf_op jit(solution)/shard_map/ppermute | solution.py:625
  34.0 18.9 %collective-permute-start.3 = (f32[4,32,512]{2,1,0:T(8,128)S(1)}, f32[4,32,512]{2,1,0:T(8,128)S(1)}, u32[]{:S(2)}, u32[]{:S(2)}) collective-permute-start(f32[4,32,512]{2,1,0:T(8,128)S(1)} %get-tuple-element.13.refs_0_), channel_id=1, source_target_pairs={{0,4},{1,5},{2,6},{3,7},{4,0},{5,1},{6,2},{7,3},{8,12},{9,13},{10,... | collective-permute-start | bytes 786440 | tf_op jit(solution)/shard_map/ppermute | solution.py:625
  35.7 17.2 %all-to-all-start.1 = ((f32[128,2,128]{2,1,0:T(2,128)}), f32[128,2,128]{2,1,0:T(2,128)S(1)}, u32[]{:S(2)}, u32[]{:S(2)}) async-start(f32[128,2,128]{2,1,0:T(2,128)} %bitcast.7), calls=%async_computation.1 | async-start | bytes 262144 | tf_op jit(solution)/shard_map/all_to_all | solution.py:623
  52.9 0.7 copy-start.2
  52.9 0.7 copy-start.3
  52.9 0.8 %copy-start.4 = (f32[4,32,512]{2,1,0:T(8,128)}, f32[4,32,512]{2,1,0:T(8,128)S(1)}, u32[]{:S(2)}) copy-start(f32[4,32,512]{2,1,0:T(8,128)S(1)} %collective-permute-done.4.refs_2_) | copy-start | bytes 786436
  52.9 0.9 %copy-start.5 = (f32[4,32,512]{2,1,0:T(8,128)}, f32[4,32,512]{2,1,0:T(8,128)S(1)}, u32[]{:S(2)}) copy-start(f32[4,32,512]{2,1,0:T(8,128)S(1)} %collective-permute-done.3.refs_1_) | copy-start | bytes 786436

commit v8 on v7

--- a/solution.py
+++ b/solution.py
@@ -521,7 +521,7 @@
             half_ref[p, at, HALF:] = second[p]
         return carry
 
-    lax.fori_loop(0, 4, some_rows, 0)
+    lax.fori_loop(0, 4, some_rows, 0, unroll=True)
 
     def some_columns(c, carry):
         cols = pl.ds(pl.multiple_of(c * HALF, HALF), HALF)
@@ -532,7 +532,7 @@
         store_spectrum(spec_ref, u, v, cols)
         return carry
 
-    lax.fori_loop(0, 2, some_columns, 0)
+    lax.fori_loop(0, 2, some_columns, 0, unroll=True)
     later_factor = fetch.take(11)
 
     def invert(k, carry):
@@ -547,7 +547,7 @@
             own_back[k >> 1, 32 * p : 32 * p + 32, cols] = mine[p]
         return carry
 
-    lax.fori_loop(0, 4, invert, 0)
+    lax.fori_loop(0, 4, invert, 0, unroll=True)
     field = own_field(1, own_back, waves_ref, vel_ref[1], slow_ref, freq_ref)
     for p in range(2):
         wave_ref[p] = field[p]

time: 78.5 us -> 77.4 us (0.986)
  Pallas kernels: 28.3 us -> 27.3 us
    pallas_call x1, Pallas kernels: 14.5 us -> 13.5 us  [local(): call(grid_kernel, [(2, 32, 512), (8, 32, 128)], [SM, SM, SM, VM] + [HBM]...]
where the time goes in v8:
time: 77.4 us; the launch traced here: 77 us
  Pallas kernels  27.3 us (35%)
  starting transfers between devices  25.2 us (33%)
  waiting for transfers between devices  12.5 us (16%)
  blocking collectives  9 us (12%)
  local copies, waits for them, and re-layouts  1.72 us (2%)
  between operations  1.38 us (2%)
    pallas_call x1, Pallas kernels, local(): call(grid_kernel, [(2, 32, 512), (8, 32, 128)], [SM, SM, SM, VM] + [HBM]...  13.5 us
    all_to_all x1, starting transfers between devices, local(): got = lax.all_to_all(sent.reshape(128, 4, 128), everyone, 0, 0, tiled=True)  11.5 us
    all_to_all x1, blocking collectives, local(): got = lax.all_to_all(sent, 'freq', 0, 0, tiled=True)  9 us
    all_to_all x1, starting transfers between devices, local(): got = lax.all_to_all(sent.reshape(128, 2, 128), everyone, 0, 0, tiled=True)  6.98 us
    pallas_call x1, Pallas kernels, local(): call(factor_kernel, [(2, 2, 2, 256, 384), (2, 2, 2, 8, 384)], [SM, SM], 5...  5.21 us
    pallas_call x1, Pallas kernels, local(): call(solve_kernel, [(256, 128), (4, 32, 512)], [SM, VM] + [HBM] * 4, 24,...  5.17 us
    ppermute x3, waiting for transfers between devices, local(): lax.ppermute(velocity, 'lat', [(i, i ^ d) for i in range(16)])  4.46 us
    all_to_all x1, waiting for transfers between devices, local(): got = lax.all_to_all(sent.reshape(128, 2, 128), everyone, 0, 0, tiled=True)  4.33 us
  transfers between devices with their start and end apart: 8, of which 4 were waited for; matrix products, arithmetic and copies ran while one was open for 0% of the time, Pallas kernels for 7%

profile of v8, /device:TPU:1, one launch (start us, length us, event | category | flops | bytes accessed | tf_op | source)
XLA Modules:
  0.0 77.0 jit_solution(15260094874198682017)
XLA Ops:
  0.6 2.7 %shard_map.131 = (f32[512,128]{1,0:T(8,128)}, f32[32,512]{1,0:T(8,128)}) custom-call(s32[1]{0:T(128)} %bitcast.lat_ref, s32[1,1024]{1,0:T(1,128)} %bitcast.16, s32[1,1024]{1,0:T(1,128)} %bitcast.17, f32[2,1024]{1,0:T(2,128)} %refs_2_.1, f32[1,1024]{1,0:T(1,128)} %bitcast.18, f32[16,1024]{1,0:T(8,128)} %bitcast.15, s32[2,32,512]{2,1,0:T(8,128)} %refs_10_.1), custom_call_target="tpu_custom_call" | custom-call | tf_op jit(solution)/shard_map/pallas_call | solution.py:588
  3.4 11.5 %all-to-all-start = ((f32[128,4,128]{2,1,0:T(4,128)}), f32[128,4,128]{2,1,0:T(4,128)S(1)}, u32[]{:S(2)}, u32[]{:S(2)}) async-start(f32[128,4,128]{2,1,0:T(4,128)} %bitcast.14), calls=%async_computation | async-start | bytes 524288 | tf_op jit(solution)/shard_map/all_to_all | solution.py:611
  14.9 2.7 %collective-permute-start.2 = (f32[32,512]{1,0:T(8,128)}, f32[32,512]{1,0:T(8,128)S(1)}, u32[]{:S(2)}, u32[]{:S(2)}) collective-permute-start(f32[32,512]{1,0:T(8,128)} %get-tuple-element.11.refs_0_), channel_id=1, source_target_pairs={{0,3},{1,2},{2,1},{3,0},{4,7},{5,6},{6,5},{7,4},{8,11},{9,10},{10,... | collective-permute-start | bytes 196616 | tf_op jit(solution)/shard_map/ppermute | solution.py:613
  17.6 0.6 collective-permute-start.1
  18.1 0.1 collective-permute-start
  18.2 3.6 %collective-permute-done.2.refs_3_ = f32[32,512]{1,0:T(8,128)S(1)} collective-permute-done((f32[32,512]{1,0:T(8,128)}, f32[32,512]{1,0:T(8,128)S(1)}, u32[]{:S(2)}, u32[]{:S(2)}) %collective-permute-start.2) | collective-permute-done | bytes 65568 | tf_op jit(solution)/shard_map/ppermute | solution.py:613
  21.9 0.8 %collective-permute-done.1.refs_2_ = f32[32,512]{1,0:T(8,128)S(1)} collective-permute-done((f32[32,512]{1,0:T(8,128)}, f32[32,512]{1,0:T(8,128)S(1)}, u32[]{:S(2)}, u32[]{:S(2)}) %collective-permute-start.1) | collective-permute-done | bytes 65568 | tf_op jit(solution)/shard_map/ppermute | solution.py:613
  22.7 0.0 collective-permute-done.refs_1_
  22.7 3.7 %all-to-all-done = f32[128,4,128]{2,1,0:T(4,128)S(1)} async-done(((f32[128,4,128]{2,1,0:T(4,128)}), f32[128,4,128]{2,1,0:T(4,128)S(1)}, u32[]{:S(2)}, u32[]{:S(2)}) %all-to-all-start) | async-done | bytes 262176 | tf_op jit(solution)/shard_map/all_to_all | solution.py:611
  26.4 0.0 copy-start.1
  26.4 0.8 %copy-done.1 = f32[32,512]{1,0:T(8,128)S(1)} copy-done((f32[32,512]{1,0:T(8,128)S(1)}, f32[32,512]{1,0:T(8,128)}, u32[]{:S(2)}) %copy-start.1) | copy-done | bytes 65560
  27.2 5.2 %shard_map.132 = (f32[256,128]{1,0:T(8,128)}, f32[4,32,512]{2,1,0:T(8,128)S(1)}) custom-call(s32[1]{0:T(128)} %bitcast.lat_ref, f32[512,128]{1,0:T(8,128)S(1)} %bitcast.12, f32[32,512]{1,0:T(8,128)S(1)} %copy-done.1, f32[32,512]{1,0:T(8,128)S(1)} %collective-permute-done.refs_1_, f32[32,512]{1,0:T(8,128)S(1)} %collective-permute-done.1.refs_2_, ...), custom_call_target="tpu_custom_call" | custom-call | tf_op jit(solution)/shard_map/pallas_call | solution.py:615
  32.4 0.0 copy-start
  32.4 0.4 collective-permute-start.5
  32.8 1.3 %collective-permute-start.4 = (f32[4,32,512]{2,1,0:T(8,128)S(1)}, f32[4,32,512]{2,1,0:T(8,128)S(1)}, u32[]{:S(2)}, u32[]{:S(2)}) collective-permute-start(f32[4,32,512]{2,1,0:T(8,128)S(1)} %get-tuple-element.13.refs_0_), channel_id=1, source_target_pairs={{0,8},{1,9},{2,10},{3,11},{4,12},{5,13},{6,14},{7,15},{8,0},{9,1},... | collective-permute-start | bytes 786440 | tf_op jit(solution)/shard_map/ppermute | solution.py:625
  34.0 1.7 %collective-permute-start.3 = (f32[4,32,512]{2,1,0:T(8,128)S(1)}, f32[4,32,512]{2,1,0:T(8,128)S(1)}, u32[]{:S(2)}, u32[]{:S(2)}) collective-permute-start(f32[4,32,512]{2,1,0:T(8,128)S(1)} %get-tuple-element.13.refs_0_), channel_id=1, source_target_pairs={{0,4},{1,5},{2,6},{3,7},{4,0},{5,1},{6,2},{7,3},{8,12},{9,13},{10,... | collective-permute-start | bytes 786440 | tf_op jit(solution)/shard_map/ppermute | solution.py:625
  35.7 7.0 %all-to-all-start.1 = ((f32[128,2,128]{2,1,0:T(2,128)}), f32[128,2,128]{2,1,0:T(2,128)S(1)}, u32[]{:S(2)}, u32[]{:S(2)}) async-start(f32[128,2,128]{2,1,0:T(2,128)} %bitcast.7), calls=%async_computation.1 | async-start | bytes 262144 | tf_op jit(solution)/shard_map/all_to_all | solution.py:623
  43.4 5.2 %shard_map.133 = (f32[2,2,2,256,384]{4,3,2,1,0:T(8,128)}, f32[2,2,2,8,384]{4,3,2,1,0:T(8,128)}) custom-call(f32[1]{0:T(128)S(6)} %copy.15.freq_ref, f32[2,8]{1,0:T(2,128)} %slow_ref.3), custom_call_target="tpu_custom_call" | custom-call | tf_op jit(solution)/shard_map/pallas_call | solution.py:627
  48.6 4.3 %all-to-all-done.1 = f32[128,2,128]{2,1,0:T(2,128)S(1)} async-done(((f32[128,2,128]{2,1,0:T(2,128)}), f32[128,2,128]{2,1,0:T(2,128)S(1)}, u32[]{:S(2)}, u32[]{:S(2)}) %all-to-all-start.1) | async-done | bytes 131104 | tf_op jit(solution)/shard_map/all_to_all | solution.py:623
  52.9 0.0 collective-permute-done.5.refs_3_
  52.9 0.0 collective-permute-done.4.refs_2_
  52.9 0.0 copy-start.4
  52.9 0.0 collective-permute-done.3.refs_1_
  52.9 0.0 copy-start.5
  53.0 0.0 copy-done
  53.0 0.6 copy-done.2
  53.6 0.1 copy-done.3
  53.7 0.1 copy-done.4
  53.8 0.1 copy-done.5
  53.8 13.5 %shard_map.134 = (f32[2,32,512]{2,1,0:T(8,128)}, f32[8,32,128]{2,1,0:T(8,128)}) custom-call(s32[1]{0:T(128)} %bitcast.lat_ref, f32[1]{0:T(128)S(6)} %copy.15.freq_ref, f32[2,8]{1,0:T(2,128)} %slow_ref.3, f32[256,128]{1,0:T(8,128)} %bitcast.13, f32[4,32,512]{2,1,0:T(8,128)} %copy-done, f32[4,32,512]{2,1,0:T(8,128)} %copy-done.5, f32[4,32,512]{2,1,0:T(8,128)} %copy-done.4, ...), custom_call_target="tpu_custom_call" | custom-call | tf_op jit(solution)/shard_map/pallas_call | solution.py:635
  67.3 9.0 %all_to_all.15.got_ref = f32[8,32,128]{2,1,0:T(8,128)S(1)} all-to-all(f32[8,32,128]{2,1,0:T(8,128)} %get-tuple-element.17), channel_id=1, replica_groups=mesh['freq'=8,'lat'=16] {'freq'}, dimensions={0} | all-to-all | bytes 262144 | tf_op jit(solution)/shard_map/all_to_all | solution.py:671
  76.3 0.7 shard_map.135
  (2 shorter events, 0.0 us)
Async XLA Ops:
  3.4 23.0 %all-to-all-start = ((f32[128,4,128]{2,1,0:T(4,128)}), f32[128,4,128]{2,1,0:T(4,128)S(1)}, u32[]{:S(2)}, u32[]{:S(2)}) async-start(f32[128,4,128]{2,1,0:T(4,128)} %bitcast.14), calls=%async_computation | async-start | bytes 524288 | tf_op jit(solution)/shard_map/all_to_all | solution.py:611
  14.9 7.0 %collective-permute-start.2 = (f32[32,512]{1,0:T(8,128)}, f32[32,512]{1,0:T(8,128)S(1)}, u32[]{:S(2)}, u32[]{:S(2)}) collective-permute-start(f32[32,512]{1,0:T(8,128)} %get-tuple-element.11.refs_0_), channel_id=1, source_target_pairs={{0,3},{1,2},{2,1},{3,0},{4,7},{5,6},{6,5},{7,4},{8,11},{9,10},{10,... | collective-permute-start | bytes 196616 | tf_op jit(solution)/shard_map/ppermute | solution.py:613
  17.6 5.1 %collective-permute-start.1 = (f32[32,512]{1,0:T(8,128)}, f32[32,512]{1,0:T(8,128)S(1)}, u32[]{:S(2)}, u32[]{:S(2)}) collective-permute-start(f32[32,512]{1,0:T(8,128)} %get-tuple-element.11.refs_0_), channel_id=1, source_target_pairs={{0,2},{1,3},{2,0},{3,1},{4,6},{5,7},{6,4},{7,5},{8,10},{9,11},{10,... | collective-permute-start | bytes 196616 | tf_op jit(solution)/shard_map/ppermute | solution.py:613
  18.1 4.6 %collective-permute-start = (f32[32,512]{1,0:T(8,128)}, f32[32,512]{1,0:T(8,128)S(1)}, u32[]{:S(2)}, u32[]{:S(2)}) collective-permute-start(f32[32,512]{1,0:T(8,128)} %get-tuple-element.11.refs_0_), channel_id=1, source_target_pairs={{0,1},{1,0},{2,3},{3,2},{4,5},{5,4},{6,7},{7,6},{8,9},{9,8},{10,11... | collective-permute-start | bytes 196616 | tf_op jit(solution)/shard_map/ppermute | solution.py:613
  26.4 0.8 %copy-start.1 = (f32[32,512]{1,0:T(8,128)S(1)}, f32[32,512]{1,0:T(8,128)}, u32[]{:S(2)}) copy-start(f32[32,512]{1,0:T(8,128)} %get-tuple-element.11.refs_0_) | copy-start | bytes 196612
  32.4 20.6 %copy-start = (f32[4,32,512]{2,1,0:T(8,128)}, f32[4,32,512]{2,1,0:T(8,128)S(1)}, u32[]{:S(2)}) copy-start(f32[4,32,512]{2,1,0:T(8,128)S(1)} %get-tuple-element.13.refs_0_) | copy-start | bytes 786436
  32.4 20.5 %collective-permute-start.5 = (f32[4,32,512]{2,1,0:T(8,128)S(1)}, f32[4,32,512]{2,1,0:T(8,128)S(1)}, u32[]{:S(2)}, u32[]{:S(2)}) collective-permute-start(f32[4,32,512]{2,1,0:T(8,128)S(1)} %get-tuple-element.13.refs_0_), channel_id=1, source_target_pairs={{0,12},{1,13},{2,14},{3,15},{4,8},{5,9},{6,10},{7,11},{8,4},{9,5},... | collective-permute-start | bytes 786440 | tf_op jit(solution)/shard_map/ppermute | solution.py:625
  32.8 20.2 %collective-permute-start.4 = (f32[4,32,512]{2,1,0:T(8,128)S(1)}, f32[4,32,512]{2,1,0:T(8,128)S(1)}, u32[]{:S(2)}, u32[]{:S(2)}) collective-permute-start(f32[4,32,512]{2,1,0:T(8,128)S(1)} %get-tuple-element.13.refs_0_), channel_id=1, source_target_pairs={{0,8},{1,9},{2,10},{3,11},{4,12},{5,13},{6,14},{7,15},{8,0},{9,1},... | collective-permute-start | bytes 786440 | tf_op jit(solution)/shard_map/ppermute | solution.py:625
  34.0 18.9 %collective-permute-start.3 = (f32[4,32,512]{2,1,0:T(8,128)S(1)}, f32[4,32,512]{2,1,0:T(8,128)S(1)}, u32[]{:S(2)}, u32[]{:S(2)}) collective-permute-start(f32[4,32,512]{2,1,0:T(8,128)S(1)} %get-tuple-element.13.refs_0_), channel_id=1, source_target_pairs={{0,4},{1,5},{2,6},{3,7},{4,0},{5,1},{6,2},{7,3},{8,12},{9,13},{10,... | collective-permute-start | bytes 786440 | tf_op jit(solution)/shard_map/ppermute | solution.py:625
  35.7 17.2 %all-to-all-start.1 = ((f32[128,2,128]{2,1,0:T(2,128)}), f32[128,2,128]{2,1,0:T(2,128)S(1)}, u32[]{:S(2)}, u32[]{:S(2)}) async-start(f32[128,2,128]{2,1,0:T(2,128)} %bitcast.7), calls=%async_computation.1 | async-start | bytes 262144 | tf_op jit(solution)/shard_map/all_to_all | solution.py:623
  52.9 0.7 copy-start.2
  52.9 0.7 copy-start.3
  52.9 0.8 %copy-start.4 = (f32[4,32,512]{2,1,0:T(8,128)}, f32[4,32,512]{2,1,0:T(8,128)S(1)}, u32[]{:S(2)}) copy-start(f32[4,32,512]{2,1,0:T(8,128)S(1)} %collective-permute-done.4.refs_2_) | copy-start | bytes 786436
  52.9 0.9 %copy-start.5 = (f32[4,32,512]{2,1,0:T(8,128)}, f32[4,32,512]{2,1,0:T(8,128)S(1)}, u32[]{:S(2)}) copy-start(f32[4,32,512]{2,1,0:T(8,128)S(1)} %collective-permute-done.3.refs_1_) | copy-start | bytes 786436

commit v9 on v8

--- a/solution.py
+++ b/solution.py
@@ -90,11 +90,11 @@
 def cos_sin(turn):
     half = 0.5 * turn
     sq = half * half
-    cosine = 1.0 / 479001600
-    for c in (-1.0 / 3628800, 1.0 / 40320, -1.0 / 720, 1.0 / 24, -0.5, 1.0):
+    cosine = -1.0 / 3628800
+    for c in (1.0 / 40320, -1.0 / 720, 1.0 / 24, -0.5, 1.0):
         cosine = cosine * sq + c
-    sine = 1.0 / 6227020800
-    for c in (-1.0 / 39916800, 1.0 / 362880, -1.0 / 5040, 1.0 / 120, -1.0 / 6, 1.0):
+    sine = -1.0 / 39916800
+    for c in (1.0 / 362880, -1.0 / 5040, 1.0 / 120, -1.0 / 6, 1.0):
         sine = sine * sq + c
     sine = sine * half
     return 1.0 - 2.0 * sine * sine, 2.0 * sine * cosine
@@ -102,7 +102,8 @@
 
 def shift_factor(wave_sq, kx, ky):
     vertical = wave_sq - kx * kx - ky * ky
-    root = jnp.sqrt(jnp.abs(vertical))
+    size = jnp.maximum(jnp.abs(vertical), 1e-30)
+    root = size * lax.rsqrt(size)
     cosine, sine = cos_sin(root)
     moving = vertical > 0.0
     return jnp.where(moving, cosine, jnp.exp(-root)), jnp.where(moving, sine, 0.0)
@@ -255,7 +256,7 @@
                     factor_ref[step, g, p, pl.ds(start, 32), :] = found[p]
                 return carry
 
-            lax.fori_loop(0, 8, some_rows, 0)
+            lax.fori_loop(0, 8, some_rows, 0, unroll=4)
             row = lax.broadcasted_iota(jnp.int32, (8, HALF), 0)
             row = jnp.where(row == 0, 256, row)
             found = factor_rows(wave_sq, row.astype(f32) * STEP, ky, ky_mirror)

time: 77.4 us -> 77.4 us (level)
  transfers between devices with their start and end apart: 8 -> 8, of which waited for: 4 -> 4; matrix products, arithmetic and copies ran while one was open for 0% -> 0% of each run, Pallas kernels for 7% -> 6%
where the time goes in v9:
time: 77.4 us; the launch traced here: 76.9 us
  Pallas kernels  26.7 us (34%)
  starting transfers between devices  25.2 us (33%)
  waiting for transfers between devices  13 us (17%)
  blocking collectives  8.99 us (12%)
  local copies, waits for them, and re-layouts  1.72 us (2%)
  between operations  1.38 us (2%)
    pallas_call x1, Pallas kernels, local(): call(grid_kernel, [(2, 32, 512), (8, 32, 128)], [SM, SM, SM, VM] + [HBM]...  13.4 us
    all_to_all x1, starting transfers between devices, local(): got = lax.all_to_all(sent.reshape(128, 4, 128), everyone, 0, 0, tiled=True)  11.5 us
    all_to_all x1, blocking collectives, local(): got = lax.all_to_all(sent, 'freq', 0, 0, tiled=True)  8.99 us
    all_to_all x1, starting transfers between devices, local(): got = lax.all_to_all(sent.reshape(128, 2, 128), everyone, 0, 0, tiled=True)  6.98 us
    pallas_call x1, Pallas kernels, local(): call(solve_kernel, [(256, 128), (4, 32, 512)], [SM, VM] + [HBM] * 4, 24,...  5.17 us
    all_to_all x1, waiting for transfers between devices, local(): got = lax.all_to_all(sent.reshape(128, 2, 128), everyone, 0, 0, tiled=True)  4.88 us
    pallas_call x1, Pallas kernels, local(): call(factor_kernel, [(2, 2, 2, 256, 384), (2, 2, 2, 8, 384)], [SM, SM], 5...  4.66 us
    ppermute x3, waiting for transfers between devices, local(): lax.ppermute(velocity, 'lat', [(i, i ^ d) for i in range(16)])  4.46 us
  transfers between devices with their start and end apart: 8, of which 4 were waited for; matrix products, arithmetic and copies ran while one was open for 0% of the time, Pallas kernels for 6%

profile of v9, /device:TPU:1, one launch (start us, length us, event | category | flops | bytes accessed | tf_op | source)
XLA Modules:
  0.0 76.9 jit_solution(9556637240283608956)
XLA Ops:
  0.6 2.7 %shard_map.131 = (f32[512,128]{1,0:T(8,128)}, f32[32,512]{1,0:T(8,128)}) custom-call(s32[1]{0:T(128)} %bitcast.lat_ref, s32[1,1024]{1,0:T(1,128)} %bitcast.16, s32[1,1024]{1,0:T(1,128)} %bitcast.17, f32[2,1024]{1,0:T(2,128)} %refs_2_.1, f32[1,1024]{1,0:T(1,128)} %bitcast.18, f32[16,1024]{1,0:T(8,128)} %bitcast.15, s32[2,32,512]{2,1,0:T(8,128)} %refs_10_.1), custom_call_target="tpu_custom_call" | custom-call | tf_op jit(solution)/shard_map/pallas_call | solution.py:589
  3.4 11.5 %all-to-all-start = ((f32[128,4,128]{2,1,0:T(4,128)}), f32[128,4,128]{2,1,0:T(4,128)S(1)}, u32[]{:S(2)}, u32[]{:S(2)}) async-start(f32[128,4,128]{2,1,0:T(4,128)} %bitcast.14), calls=%async_computation | async-start | bytes 524288 | tf_op jit(solution)/shard_map/all_to_all | solution.py:612
  14.9 2.7 %collective-permute-start.2 = (f32[32,512]{1,0:T(8,128)}, f32[32,512]{1,0:T(8,128)S(1)}, u32[]{:S(2)}, u32[]{:S(2)}) collective-permute-start(f32[32,512]{1,0:T(8,128)} %get-tuple-element.11.refs_0_), channel_id=1, source_target_pairs={{0,3},{1,2},{2,1},{3,0},{4,7},{5,6},{6,5},{7,4},{8,11},{9,10},{10,... | collective-permute-start | bytes 196616 | tf_op jit(solution)/shard_map/ppermute | solution.py:614
  17.6 0.6 collective-permute-start.1
  18.1 0.1 collective-permute-start
  18.2 3.6 %collective-permute-done.2.refs_3_ = f32[32,512]{1,0:T(8,128)S(1)} collective-permute-done((f32[32,512]{1,0:T(8,128)}, f32[32,512]{1,0:T(8,128)S(1)}, u32[]{:S(2)}, u32[]{:S(2)}) %collective-permute-start.2) | collective-permute-done | bytes 65568 | tf_op jit(solution)/shard_map/ppermute | solution.py:614
  21.9 0.8 %collective-permute-done.1.refs_2_ = f32[32,512]{1,0:T(8,128)S(1)} collective-permute-done((f32[32,512]{1,0:T(8,128)}, f32[32,512]{1,0:T(8,128)S(1)}, u32[]{:S(2)}, u32[]{:S(2)}) %collective-permute-start.1) | collective-permute-done | bytes 65568 | tf_op jit(solution)/shard_map/ppermute | solution.py:614
  22.7 0.0 collective-permute-done.refs_1_
  22.7 3.7 %all-to-all-done = f32[128,4,128]{2,1,0:T(4,128)S(1)} async-done(((f32[128,4,128]{2,1,0:T(4,128)}), f32[128,4,128]{2,1,0:T(4,128)S(1)}, u32[]{:S(2)}, u32[]{:S(2)}) %all-to-all-start) | async-done | bytes 262176 | tf_op jit(solution)/shard_map/all_to_all | solution.py:612
  26.4 0.0 copy-start.1
  26.4 0.8 %copy-done.1 = f32[32,512]{1,0:T(8,128)S(1)} copy-done((f32[32,512]{1,0:T(8,128)S(1)}, f32[32,512]{1,0:T(8,128)}, u32[]{:S(2)}) %copy-start.1) | copy-done | bytes 65560
  27.2 5.2 %shard_map.132 = (f32[256,128]{1,0:T(8,128)}, f32[4,32,512]{2,1,0:T(8,128)S(1)}) custom-call(s32[1]{0:T(128)} %bitcast.lat_ref, f32[512,128]{1,0:T(8,128)S(1)} %bitcast.12, f32[32,512]{1,0:T(8,128)S(1)} %copy-done.1, f32[32,512]{1,0:T(8,128)S(1)} %collective-permute-done.refs_1_, f32[32,512]{1,0:T(8,128)S(1)} %collective-permute-done.1.refs_2_, ...), custom_call_target="tpu_custom_call" | custom-call | tf_op jit(solution)/shard_map/pallas_call | solution.py:616
  32.4 0.0 copy-start
  32.4 0.4 collective-permute-start.5
  32.8 1.3 %collective-permute-start.4 = (f32[4,32,512]{2,1,0:T(8,128)S(1)}, f32[4,32,512]{2,1,0:T(8,128)S(1)}, u32[]{:S(2)}, u32[]{:S(2)}) collective-permute-start(f32[4,32,512]{2,1,0:T(8,128)S(1)} %get-tuple-element.13.refs_0_), channel_id=1, source_target_pairs={{0,8},{1,9},{2,10},{3,11},{4,12},{5,13},{6,14},{7,15},{8,0},{9,1},... | collective-permute-start | bytes 786440 | tf_op jit(solution)/shard_map/ppermute | solution.py:626
  34.0 1.7 %collective-permute-start.3 = (f32[4,32,512]{2,1,0:T(8,128)S(1)}, f32[4,32,512]{2,1,0:T(8,128)S(1)}, u32[]{:S(2)}, u32[]{:S(2)}) collective-permute-start(f32[4,32,512]{2,1,0:T(8,128)S(1)} %get-tuple-element.13.refs_0_), channel_id=1, source_target_pairs={{0,4},{1,5},{2,6},{3,7},{4,0},{5,1},{6,2},{7,3},{8,12},{9,13},{10,... | collective-permute-start | bytes 786440 | tf_op jit(solution)/shard_map/ppermute | solution.py:626
  35.7 7.0 %all-to-all-start.1 = ((f32[128,2,128]{2,1,0:T(2,128)}), f32[128,2,128]{2,1,0:T(2,128)S(1)}, u32[]{:S(2)}, u32[]{:S(2)}) async-start(f32[128,2,128]{2,1,0:T(2,128)} %bitcast.7), calls=%async_computation.1 | async-start | bytes 262144 | tf_op jit(solution)/shard_map/all_to_all | solution.py:624
  43.4 4.7 %shard_map.133 = (f32[2,2,2,256,384]{4,3,2,1,0:T(8,128)}, f32[2,2,2,8,384]{4,3,2,1,0:T(8,128)}) custom-call(f32[1]{0:T(128)S(6)} %copy.15.freq_ref, f32[2,8]{1,0:T(2,128)} %slow_ref.3), custom_call_target="tpu_custom_call" | custom-call | tf_op jit(solution)/shard_map/pallas_call | solution.py:628
  48.0 4.9 %all-to-all-done.1 = f32[128,2,128]{2,1,0:T(2,128)S(1)} async-done(((f32[128,2,128]{2,1,0:T(2,128)}), f32[128,2,128]{2,1,0:T(2,128)S(1)}, u32[]{:S(2)}, u32[]{:S(2)}) %all-to-all-start.1) | async-done | bytes 131104 | tf_op jit(solution)/shard_map/all_to_all | solution.py:624
  52.9 0.0 collective-permute-done.5.refs_3_
  52.9 0.0 collective-permute-done.4.refs_2_
  52.9 0.0 copy-start.4
  52.9 0.0 collective-permute-done.3.refs_1_
  52.9 0.0 copy-start.5
  53.0 0.0 copy-done
  53.0 0.6 copy-done.2
  53.6 0.1 copy-done.3
  53.7 0.1 copy-done.4
  53.8 0.1 copy-done.5
  53.8 13.4 %shard_map.134 = (f32[2,32,512]{2,1,0:T(8,128)}, f32[8,32,128]{2,1,0:T(8,128)}) custom-call(s32[1]{0:T(128)} %bitcast.lat_ref, f32[1]{0:T(128)S(6)} %copy.15.freq_ref, f32[2,8]{1,0:T(2,128)} %slow_ref.3, f32[256,128]{1,0:T(8,128)} %bitcast.13, f32[4,32,512]{2,1,0:T(8,128)} %copy-done, f32[4,32,512]{2,1,0:T(8,128)} %copy-done.5, f32[4,32,512]{2,1,0:T(8,128)} %copy-done.4, ...), custom_call_target="tpu_custom_call" | custom-call | tf_op jit(solution)/shard_map/pallas_call | solution.py:636
  67.3 9.0 %all_to_all.15.got_ref = f32[8,32,128]{2,1,0:T(8,128)S(1)} all-to-all(f32[8,32,128]{2,1,0:T(8,128)} %get-tuple-element.17), channel_id=1, replica_groups=mesh['freq'=8,'lat'=16] {'freq'}, dimensions={0} | all-to-all | bytes 262144 | tf_op jit(solution)/shard_map/all_to_all | solution.py:672
  76.3 0.7 shard_map.135
  (2 shorter events, 0.0 us)
Async XLA Ops:
  3.4 23.0 %all-to-all-start = ((f32[128,4,128]{2,1,0:T(4,128)}), f32[128,4,128]{2,1,0:T(4,128)S(1)}, u32[]{:S(2)}, u32[]{:S(2)}) async-start(f32[128,4,128]{2,1,0:T(4,128)} %bitcast.14), calls=%async_computation | async-start | bytes 524288 | tf_op jit(solution)/shard_map/all_to_all | solution.py:612
  14.9 7.0 %collective-permute-start.2 = (f32[32,512]{1,0:T(8,128)}, f32[32,512]{1,0:T(8,128)S(1)}, u32[]{:S(2)}, u32[]{:S(2)}) collective-permute-start(f32[32,512]{1,0:T(8,128)} %get-tuple-element.11.refs_0_), channel_id=1, source_target_pairs={{0,3},{1,2},{2,1},{3,0},{4,7},{5,6},{6,5},{7,4},{8,11},{9,10},{10,... | collective-permute-start | bytes 196616 | tf_op jit(solution)/shard_map/ppermute | solution.py:614
  17.6 5.1 %collective-permute-start.1 = (f32[32,512]{1,0:T(8,128)}, f32[32,512]{1,0:T(8,128)S(1)}, u32[]{:S(2)}, u32[]{:S(2)}) collective-permute-start(f32[32,512]{1,0:T(8,128)} %get-tuple-element.11.refs_0_), channel_id=1, source_target_pairs={{0,2},{1,3},{2,0},{3,1},{4,6},{5,7},{6,4},{7,5},{8,10},{9,11},{10,... | collective-permute-start | bytes 196616 | tf_op jit(solution)/shard_map/ppermute | solution.py:614
  18.1 4.6 %collective-permute-start = (f32[32,512]{1,0:T(8,128)}, f32[32,512]{1,0:T(8,128)S(1)}, u32[]{:S(2)}, u32[]{:S(2)}) collective-permute-start(f32[32,512]{1,0:T(8,128)} %get-tuple-element.11.refs_0_), channel_id=1, source_target_pairs={{0,1},{1,0},{2,3},{3,2},{4,5},{5,4},{6,7},{7,6},{8,9},{9,8},{10,11... | collective-permute-start | bytes 196616 | tf_op jit(solution)/shard_map/ppermute | solution.py:614
  26.4 0.8 %copy-start.1 = (f32[32,512]{1,0:T(8,128)S(1)}, f32[32,512]{1,0:T(8,128)}, u32[]{:S(2)}) copy-start(f32[32,512]{1,0:T(8,128)} %get-tuple-element.11.refs_0_) | copy-start | bytes 196612
  32.4 20.6 %copy-start = (f32[4,32,512]{2,1,0:T(8,128)}, f32[4,32,512]{2,1,0:T(8,128)S(1)}, u32[]{:S(2)}) copy-start(f32[4,32,512]{2,1,0:T(8,128)S(1)} %get-tuple-element.13.refs_0_) | copy-start | bytes 786436
  32.4 20.5 %collective-permute-start.5 = (f32[4,32,512]{2,1,0:T(8,128)S(1)}, f32[4,32,512]{2,1,0:T(8,128)S(1)}, u32[]{:S(2)}, u32[]{:S(2)}) collective-permute-start(f32[4,32,512]{2,1,0:T(8,128)S(1)} %get-tuple-element.13.refs_0_), channel_id=1, source_target_pairs={{0,12},{1,13},{2,14},{3,15},{4,8},{5,9},{6,10},{7,11},{8,4},{9,5},... | collective-permute-start | bytes 786440 | tf_op jit(solution)/shard_map/ppermute | solution.py:626
  32.8 20.2 %collective-permute-start.4 = (f32[4,32,512]{2,1,0:T(8,128)S(1)}, f32[4,32,512]{2,1,0:T(8,128)S(1)}, u32[]{:S(2)}, u32[]{:S(2)}) collective-permute-start(f32[4,32,512]{2,1,0:T(8,128)S(1)} %get-tuple-element.13.refs_0_), channel_id=1, source_target_pairs={{0,8},{1,9},{2,10},{3,11},{4,12},{5,13},{6,14},{7,15},{8,0},{9,1},... | collective-permute-start | bytes 786440 | tf_op jit(solution)/shard_map/ppermute | solution.py:626
  34.0 18.9 %collective-permute-start.3 = (f32[4,32,512]{2,1,0:T(8,128)S(1)}, f32[4,32,512]{2,1,0:T(8,128)S(1)}, u32[]{:S(2)}, u32[]{:S(2)}) collective-permute-start(f32[4,32,512]{2,1,0:T(8,128)S(1)} %get-tuple-element.13.refs_0_), channel_id=1, source_target_pairs={{0,4},{1,5},{2,6},{3,7},{4,0},{5,1},{6,2},{7,3},{8,12},{9,13},{10,... | collective-permute-start | bytes 786440 | tf_op jit(solution)/shard_map/ppermute | solution.py:626
  35.7 17.2 %all-to-all-start.1 = ((f32[128,2,128]{2,1,0:T(2,128)}), f32[128,2,128]{2,1,0:T(2,128)S(1)}, u32[]{:S(2)}, u32[]{:S(2)}) async-start(f32[128,2,128]{2,1,0:T(2,128)} %bitcast.7), calls=%async_computation.1 | async-start | bytes 262144 | tf_op jit(solution)/shard_map/all_to_all | solution.py:624
  52.9 0.7 copy-start.2
  52.9 0.7 copy-start.3
  52.9 0.8 %copy-start.4 = (f32[4,32,512]{2,1,0:T(8,128)}, f32[4,32,512]{2,1,0:T(8,128)S(1)}, u32[]{:S(2)}) copy-start(f32[4,32,512]{2,1,0:T(8,128)S(1)} %collective-permute-done.4.refs_2_) | copy-start | bytes 786436
  52.9 0.9 %copy-start.5 = (f32[4,32,512]{2,1,0:T(8,128)}, f32[4,32,512]{2,1,0:T(8,128)S(1)}, u32[]{:S(2)}) copy-start(f32[4,32,512]{2,1,0:T(8,128)S(1)} %collective-permute-done.3.refs_1_) | copy-start | bytes 786436
